TPU v7x, 32 devices: a whole 2x2x4 slice. The times are simulated.
32 devices in a mesh: dp: 8 (over z, core), seq: 4 (over y, x).
Axes of the slice: x: 2, y: 2, z: 4, core: 2. Of those that a mesh axis runs over, the one named last changes fastest.
Arguments:
- tokens: bfloat16 [4, 8, 1024, 768], P(None, 'dp', 'seq'), may hold values from -6 to 6
- image_lengths: int32 [4, 8, 5], P(None, 'dp'), may hold values from 1 to 576, 1016 in all within a row
- cotangent: bfloat16 [4, 8, 1024, 768], P(None, 'dp', 'seq'), may hold values from -6 to 6
- attn_gain: float32 [768], replicated, may hold values from 0.5 to 1.5
- attn_shift: float32 [768], replicated, may hold values from -3 to 3
- qkv_weight: bfloat16 [768, 2304], replicated, may hold values from -0.21875 to 0.21875
- qv_bias: float32 [1536], replicated, may hold values from -3 to 3
- out_weight: bfloat16 [768, 768], replicated, may hold values from -2.5 to 2.5
- out_bias: float32 [768], replicated, may hold values from -2 to 2
- mlp_gain: float32 [768], replicated, may hold values from 0.5 to 1.5
- mlp_shift: float32 [768], replicated, may hold values from -3 to 3
- fc1_weight: bfloat16 [768, 3072], replicated, may hold values from -0.21875 to 0.21875
- fc1_bias: float32 [3072], replicated, may hold values from -3 to 3
- fc2_weight: bfloat16 [3072, 768], replicated, may hold values from -0.109375 to 0.109375
- fc2_bias: float32 [768], replicated, may hold values from -2 to 2
Outputs:
- block_out: bfloat16 [4, 8, 1024, 768], P(None, 'dp', 'seq')
- tokens_grad: bfloat16 [4, 8, 1024, 768], P(None, 'dp', 'seq')
- attn_gain_grad: float32 [768], replicated
- attn_shift_grad: float32 [768], replicated
- qkv_weight_grad: float32 [768, 2304], replicated
- qv_bias_grad: float32 [1536], replicated
- out_weight_grad: float32 [768, 768], replicated
- out_bias_grad: float32 [768], replicated
- mlp_gain_grad: float32 [768], replicated
- mlp_shift_grad: float32 [768], replicated
- fc1_weight_grad: float32 [768, 3072], replicated
- fc1_bias_grad: float32 [3072], replicated
- fc2_weight_grad: float32 [3072, 768], replicated
- fc2_bias_grad: float32 [768], replicated
Inputs may be any that keep to these rules, and one draw needn't show every extreme that they name: Each row of image_lengths gives the patch counts of the row's 4 images in order, then the count of padding positions at the row's end; a row's entries sum to 1016, and its largest entry is exactly 576.
All inputs are finite; a program needn't handle non-finite values.
Results may differ from a plain program's by a relative error of at most 0.013.
Values may be sent and summed in bfloat16 or wider, within the bound.
A program may use at most 256 MiB of HBM per device.

v0:
```python
import jax
import jax.numpy as jnp
from jax import lax
from jax.sharding import PartitionSpec as P

HEADS = 12


EPS = 1e-06
NEG = -1e30


def layer_norm(values, scale_row, shift_row):
    center = values - jnp.mean(values, axis=-1, keepdims=True)
    spread = jnp.mean(center * center, axis=-1, keepdims=True)
    return center * lax.rsqrt(spread + EPS) * scale_row + shift_row


def gelu_exact(values):
    return jax.nn.gelu(values, approximate=False)


def segment_ids(lengths, row_len, images):
    positions = jnp.arange(row_len, dtype=jnp.int32)
    ends = jnp.cumsum(lengths, axis=-1) + 2 * images
    patches = jnp.sum((positions[:, None] >= ends[..., None, :]).astype(jnp.int32), axis=-1)
    return jnp.where(positions < 2 * images, positions // 2, patches)


def matmul(first_op, second_op, pattern):
    return jnp.einsum(pattern, first_op, second_op, preferred_element_type=jnp.float32)


def shards(
    tokens,
    image_lengths,
    cotangent,
    attn_gain,
    attn_shift,
    qkv_weight,
    qv_bias,
    out_weight,
    out_bias,
    mlp_gain,
    mlp_shift,
    fc1_weight,
    fc1_bias,
    fc2_weight,
    fc2_bias,
):
    micro_count, row_count, shard_len, features = tokens.shape
    row_len = shard_len * lax.axis_size("seq")
    images = image_lengths.shape[2] - 1
    head_dim = features // HEADS
    score_scale = head_dim ** (-0.5)
    offset = lax.axis_index("seq") * shard_len
    tok_count = row_count * shard_len
    zero_keys = jnp.zeros((features,), jnp.float32)
    full_bias = jnp.concatenate([qv_bias[:features], zero_keys, qv_bias[features:]])
    totals = [
        jnp.zeros(weight.shape, jnp.float32)
        for weight in (
            attn_gain,
            attn_shift,
            qkv_weight,
            qv_bias,
            out_weight,
            out_bias,
            mlp_gain,
            mlp_shift,
            fc1_weight,
            fc1_bias,
            fc2_weight,
            fc2_bias,
        )
    ]
    outputs_list = []
    grads_list = []
    for micro_step in range(micro_count):
        inputs = tokens[micro_step].astype(jnp.float32)
        seg_all = segment_ids(image_lengths[micro_step], row_len, images)
        seg_here = lax.dynamic_slice_in_dim(seg_all, offset, shard_len, 1)
        allowed = seg_here[:, None, :, None] == seg_all[:, None, None, :]
        normed, first_pull = jax.vjp(layer_norm, inputs, attn_gain, attn_shift)
        normed_low = normed.astype(jnp.bfloat16).reshape(tok_count, features)
        projected = (matmul(normed_low, qkv_weight, "td,de->te") + full_bias).astype(jnp.bfloat16)
        projected = projected.reshape(row_count, shard_len, 3 * features)
        queries = projected[:, :, :features].reshape(row_count, shard_len, HEADS, head_dim)
        keys_all, values_all = (
            lax.all_gather(projected[:, :, features : 2 * features], "seq", axis=1, tiled=True),
            lax.all_gather(projected[:, :, 2 * features :], "seq", axis=1, tiled=True),
        )
        keys_all = keys_all.reshape(row_count, row_len, HEADS, head_dim)
        values_all = values_all.reshape(row_count, row_len, HEADS, head_dim)
        scores = jnp.where(allowed, matmul(queries, keys_all, "rqhd,rkhd->rhqk") * score_scale, NEG)
        largest = jnp.max(scores, axis=-1, keepdims=True)
        log_total = largest + jnp.log(jnp.sum(jnp.exp(scores - largest), axis=-1, keepdims=True))
        weights_low = jnp.exp(scores - log_total).astype(jnp.bfloat16)
        attended = (
            matmul(weights_low, values_all, "rhqk,rkhd->rqhd")
            .astype(jnp.bfloat16)
            .reshape(tok_count, features)
        )
        branch = matmul(attended, out_weight, "td,de->te") + out_bias
        middle = inputs + branch.reshape(inputs.shape)
        normed_two, second_pull = jax.vjp(layer_norm, middle, mlp_gain, mlp_shift)
        normed_two_low = normed_two.astype(jnp.bfloat16).reshape(tok_count, features)
        hidden_pre = matmul(normed_two_low, fc1_weight, "td,df->tf") + fc1_bias
        hidden, gelu_pull = jax.vjp(gelu_exact, hidden_pre)
        hidden_low = hidden.astype(jnp.bfloat16)
        result = middle + (matmul(hidden_low, fc2_weight, "tf,fd->td") + fc2_bias).reshape(
            inputs.shape
        )
        outputs_list.append(result.astype(jnp.bfloat16))
        incoming = cotangent[micro_step].reshape(tok_count, features)
        fc2_weight_part = matmul(hidden_low, incoming, "tf,td->fd")
        fc2_bias_part = jnp.sum(incoming.astype(jnp.float32), axis=0)
        hidden_grad = gelu_pull(matmul(incoming, fc2_weight, "td,fd->tf"))[0].astype(jnp.bfloat16)
        fc1_weight_part = matmul(normed_two_low, hidden_grad, "td,tf->df")
        fc1_bias_part = jnp.sum(hidden_grad.astype(jnp.float32), axis=0)
        back_two = matmul(hidden_grad, fc1_weight, "tf,df->td").reshape(inputs.shape)
        middle_norm, mlp_gain_part, mlp_shift_part = second_pull(back_two)
        middle_grad = incoming.astype(jnp.float32).reshape(inputs.shape) + middle_norm
        branch_grad = middle_grad.astype(jnp.bfloat16).reshape(tok_count, features)
        out_weight_part = matmul(attended, branch_grad, "td,te->de")
        out_bias_part = jnp.sum(branch_grad.astype(jnp.float32), axis=0)
        attended_grad = matmul(branch_grad, out_weight, "te,de->td").astype(jnp.bfloat16)
        attended_grad = attended_grad.reshape(row_count, shard_len, HEADS, head_dim)
        scores_again = jnp.where(
            allowed, matmul(queries, keys_all, "rqhd,rkhd->rhqk") * score_scale, NEG
        )
        chances = jnp.exp(scores_again - log_total)
        chances_low = chances.astype(jnp.bfloat16)
        chance_grad = matmul(attended_grad, values_all, "rqhd,rkhd->rhqk")
        row_delta = jnp.sum(chances * chance_grad, axis=-1, keepdims=True)
        score_grad = (chances * (chance_grad - row_delta)).astype(jnp.bfloat16)
        query_grad = matmul(score_grad, keys_all, "rhqk,rkhd->rqhd") * score_scale
        key_terms = matmul(score_grad, queries, "rhqk,rqhd->rkhd") * score_scale
        value_terms = matmul(chances_low, attended_grad, "rhqk,rqhd->rkhd")
        key_grad, value_grad = (
            lax.psum_scatter(
                key_terms.reshape(row_count, row_len, features).astype(jnp.bfloat16),
                "seq",
                scatter_dimension=1,
                tiled=True,
            ).astype(jnp.float32),
            lax.psum_scatter(
                value_terms.reshape(row_count, row_len, features).astype(jnp.bfloat16),
                "seq",
                scatter_dimension=1,
                tiled=True,
            ).astype(jnp.float32),
        )
        projected_grad = jnp.concatenate(
            [query_grad.reshape(row_count, shard_len, features), key_grad, value_grad], axis=-1
        )
        projected_grad = projected_grad.astype(jnp.bfloat16).reshape(tok_count, 3 * features)
        qkv_weight_part = matmul(normed_low, projected_grad, "td,te->de")
        bias_sums = jnp.sum(projected_grad.astype(jnp.float32), axis=0)
        qv_bias_part = jnp.concatenate([bias_sums[:features], bias_sums[2 * features :]])
        back_one = matmul(projected_grad, qkv_weight, "te,de->td").reshape(inputs.shape)
        inputs_norm, attn_gain_part, attn_shift_part = first_pull(back_one)
        grads_list.append((middle_grad + inputs_norm).astype(jnp.bfloat16))
        pieces = (
            attn_gain_part,
            attn_shift_part,
            qkv_weight_part,
            qv_bias_part,
            out_weight_part,
            out_bias_part,
            mlp_gain_part,
            mlp_shift_part,
            fc1_weight_part,
            fc1_bias_part,
            fc2_weight_part,
            fc2_bias_part,
        )
        totals = [running + member for running, member in zip(totals, pieces)]
    (
        attn_gain_sum,
        attn_shift_sum,
        qkv_weight_sum,
        qv_bias_sum,
        out_weight_sum,
        out_bias_sum,
        mlp_gain_sum,
        mlp_shift_sum,
        fc1_weight_sum,
        fc1_bias_sum,
        fc2_weight_sum,
        fc2_bias_sum,
    ) = totals
    summed = lax.psum(
        (
            attn_gain_sum,
            attn_shift_sum,
            qkv_weight_sum,
            qv_bias_sum,
            out_weight_sum,
            out_bias_sum,
            mlp_gain_sum,
            mlp_shift_sum,
            fc1_weight_sum,
            fc1_bias_sum,
            fc2_weight_sum,
            fc2_bias_sum,
        ),
        ("dp", "seq"),
    )
    return (jnp.stack(outputs_list), jnp.stack(grads_list)) + tuple(summed)


def solution(mesh):
    placed = (
        P(None, "dp", "seq", None),
        P(None, "dp", None),
        P(None, "dp", "seq", None),
        P(),
        P(),
        P(),
        P(),
        P(),
        P(),
        P(),
        P(),
        P(),
        P(),
        P(),
        P(),
    )
    return jax.shard_map(
        shards,
        mesh=mesh,
        in_specs=placed,
        out_specs=(
            P(None, "dp", "seq", None),
            P(None, "dp", "seq", None),
            P(),
            P(),
            P(),
            P(),
            P(),
            P(),
            P(),
            P(),
            P(),
            P(),
            P(),
            P(),
        ),
        check_vma=False,
    )
```

profile of v0, /device:TPU:0, one launch (start us, length us, event | category | flops | bytes accessed | tf_op | source)
XLA Modules:
  0.0 1089.1 jit_solution(12661519296311647016)
XLA Ops:
  66.2 17.5 %all-gather.21.cloned.1.call-done = bf16[1,1024,768]{2,1,0:T(8,128)(2,1)} async-done(((bf16[1,256,768]{2,1,0:T(8,128)(2,1)}), bf16[1,1024,768]{2,1,0:T(8,128)(2,1)}) %all-gather.21.cloned.1.call-update) | async-done | bytes 1572880 | tf_op jit(solution)/shard_map/all_gather | solution.py:91
  86.3 8.0 convolution_convert_fusion.8
  98.4 18.8 %all-gather.19.cloned.1.call-done = bf16[1,1024,768]{2,1,0:T(8,128)(2,1)} async-done(((bf16[1,256,768]{2,1,0:T(8,128)(2,1)}), bf16[1,1024,768]{2,1,0:T(8,128)(2,1)}) %all-gather.19.cloned.1.call-update) | async-done | bytes 1572880 | tf_op jit(solution)/shard_map/all_gather | solution.py:90
  128.2 22.2 %all-gather.17.cloned.1.call-done = bf16[1,1024,768]{2,1,0:T(8,128)(2,1)} async-done(((bf16[1,256,768]{2,1,0:T(8,128)(2,1)}), bf16[1,1024,768]{2,1,0:T(8,128)(2,1)}) %all-gather.17.cloned.1.call-update) | async-done | bytes 1572880 | tf_op jit(solution)/shard_map/all_gather | solution.py:91
  153.5 8.0 convolution_convert_fusion.9
  164.4 11.7 %multiply_convert_fusion.8 = (bf16[256,3072]{1,0:T(8,128)(2,1)}, f32[256,3072]{1,0:T(8,128)}, f32[256,3072]{1,0:T(8,128)}) fusion(f32[3072]{0:T(1024)S(1)} %copy-done.204, bf16[768,3072]{1,0:T(8,128)(2,1)} %param.26, f32[256,768]{1,0:T(8,128)S(1)} %copy-done.65, f32[256]{0:T(256)S(1)} %copy-done.192, f32[256]{0:T(256)S(1)} %copy-done.168, ...), kind=kOutput, calls=%fused_computation.67 | convolution fusion | flops 1260847104 | bytes 13389824 | tf_op jit(solution)/shard_map/td,df->tf/dot_general | solution.py:31
  176.1 11.2 %multiply_convert_fusion.9 = (bf16[256,3072]{1,0:T(8,128)(2,1)}, f32[256,3072]{1,0:T(8,128)}, f32[256,3072]{1,0:T(8,128)}) fusion(f32[3072]{0:T(1024)S(1)} %copy-done.204, bf16[768,3072]{1,0:T(8,128)(2,1)S(1)} %bitcast.575, f32[256,768]{1,0:T(8,128)S(1)} %get-tuple-element.156, f32[256]{0:T(256)S(1)} %fusion.181, f32[256]{0:T(256)S(1)} %broadcast_multiply_fusion.2, ...), kind=kOutput, calls=%fused_computation.80 | convolution fusion | flops 1260847104 | bytes 13389824 | tf_op jit(solution)/shard_map/td,df->tf/dot_general | solution.py:31
  199.3 16.6 %all-gather.13.cloned.1.call-done = bf16[1,1024,768]{2,1,0:T(8,128)(2,1)} async-done(((bf16[1,256,768]{2,1,0:T(8,128)(2,1)}), bf16[1,1024,768]{2,1,0:T(8,128)(2,1)}) %all-gather.13.cloned.1.call-update) | async-done | bytes 1572880 | tf_op jit(solution)/shard_map/all_gather | solution.py:91
  218.4 8.2 convolution_convert_fusion.10
  229.2 19.4 %all-gather.11.cloned.1.call-done = bf16[1,1024,768]{2,1,0:T(8,128)(2,1)} async-done(((bf16[1,256,768]{2,1,0:T(8,128)(2,1)}), bf16[1,1024,768]{2,1,0:T(8,128)(2,1)}) %all-gather.11.cloned.1.call-update) | async-done | bytes 1572880 | tf_op jit(solution)/shard_map/all_gather | solution.py:90
  262.0 11.8 %multiply_convert_fusion.10 = (bf16[256,3072]{1,0:T(8,128)(2,1)}, f32[256,3072]{1,0:T(8,128)}, f32[256,3072]{1,0:T(8,128)}) fusion(f32[3072]{0:T(1024)S(1)} %copy-done.205, bf16[768,3072]{1,0:T(8,128)(2,1)} %param.26, f32[256,768]{1,0:T(8,128)S(1)} %copy-done.31, f32[256]{0:T(256)S(1)} %fusion.179, f32[256]{0:T(256)S(1)} %broadcast_multiply_fusion.4, ...), kind=kOutput, calls=%fused_computation.93 | convolution fusion | flops 1260847104 | bytes 13389824 | tf_op jit(solution)/shard_map/td,df->tf/dot_general | solution.py:31
  273.8 7.7 all-gather.9.cloned.1.call-done
  284.1 8.1 convolution_convert_fusion.11
  294.3 12.2 %multiply_convert_fusion.11 = (bf16[256,3072]{1,0:T(8,128)(2,1)}, f32[256,3072]{1,0:T(8,128)}, f32[256,3072]{1,0:T(8,128)}) fusion(f32[3072]{0:T(1024)S(1)} %copy-done.206, bf16[768,3072]{1,0:T(8,128)(2,1)} %param.26, f32[256,768]{1,0:T(8,128)S(1)} %get-tuple-element.166, f32[768]{0:T(1024)S(1)} %copy-done.98, f32[768]{0:T(1024)S(1)} %copy-done.95, ...), kind=kOutput, calls=%fused_computation.106 | convolution fusion | flops 1260847104 | bytes 13389824 | tf_op jit(solution)/shard_map/td,df->tf/dot_general | solution.py:31
  338.4 9.0 convolution_convert_fusion.1
  347.5 9.6 multiply_reduce_fusion.1
  357.2 7.1 multiply_convert_fusion.1
  372.5 9.1 convolution_convert_fusion.3
  381.7 9.6 multiply_reduce_fusion.3
  391.3 7.1 multiply_convert_fusion.3
  406.6 9.2 convolution_convert_fusion.2
  415.8 10.8 multiply_reduce_fusion.2
  426.7 13.2 %multiply_convert_fusion.2 = bf16[12,256,1024]{2,1,0:T(8,128)(2,1)} fusion(f32[12,256,1024]{2,1,0:T(8,128)} %get-tuple-element.173, f32[12,256,1024]{2,1,0:T(8,128)} %copy-done.2, f32[12,256]{1,0:T(8,128)} %get-tuple-element.172, f32[12,256]{1,0:T(8,128)} %log_add_fusion.2, pred[256,1024]{1,0:T(8,128)(4,1)} %broadcast_compare_fusion.2), kind=kLoop, calls=%fused_computation.4 | loop fusion | flops 18874368 | bytes 31744000 | tf_op jit(solution)/shard_map/convert_element_type | solution.py:136
  443.2 5.5 multiply_convert_fusion.6
  448.7 11.6 %multiply_reduce_fusion = (f32[12,256]{1,0:T(8,128)S(1)}, f32[12,256,1024]{2,1,0:T(8,128)}) fusion(f32[12,256,1024]{2,1,0:T(8,128)} %copy-done.1, f32[12,256]{1,0:T(8,128)S(1)} %copy-done.109, pred[256,1024]{1,0:T(8,128)(4,1)S(1)} %copy-done.39, bf16[256,12,64]{0,2,1:T(8,128)(2,1)S(1)} %bitcast.550, bf16[1024,12,64]{0,2,1:T(8,128)(2,1)S(1)} %bitcast.495), kind=kOutput, calls=%fused_computation.1 | convolution fusion | flops 418378752 | bytes 27418624 | tf_op jit(solution)/shard_map/rqhd,rkhd->rhqk/dot_general | solution.py:31
  461.4 9.7 multiply_convert_fusion
  476.4 6.1 multiply_convert_fusion.4
  491.1 4.7 convolution_convert_fusion
  499.3 5.8 fusion.52
  505.1 5.0 fusion.125
  510.1 5.1 fusion.137
  515.2 5.0 fusion.131
  520.3 5.3 fusion.221
  525.7 5.3 fusion.219
  531.5 15.5 %add_add_fusion = f32[3072,768]{1,0:T(8,128)} fusion(f32[3072,768]{1,0:T(8,128)} %fusion.125, f32[3072,768]{1,0:T(8,128)} %fusion.137, f32[3072,768]{1,0:T(8,128)} %fusion.131, bf16[256,3072]{1,0:T(8,128)(2,1)} %get-tuple-element.92, bf16[4,1,256,768]{3,2,1,0:T(8,128)(2,1)} %param.17), kind=kOutput, calls=%fused_computation.24 | convolution fusion | flops 1215037440 | bytes 39714816 | tf_op jit(solution)/shard_map/tf,td->fd/dot_general | solution.py:31
  547.0 4.5 add_add_fusion.3
  551.6 7.1 fusion.220
  558.8 12.8 %add_add_fusion.1 = f32[768,3072]{1,0:T(8,128)} fusion(f32[768,3072]{1,0:T(8,128)S(1)} %bitcast.479, f32[768,3072]{1,0:T(8,128)} %fusion.219, f32[768,3072]{1,0:T(8,128)} %fusion.220, bf16[256,3072]{1,0:T(8,128)(2,1)S(1)} %copy-done.78, f32[256,768]{1,0:T(8,128)S(1)} %copy-done.67, f32[256]{0:T(256)S(1)} %copy-done.194, f32[256]{0:T(256)S(1)} %copy-done.170, ...), kind=kOutput, calls=%fused_computation.25 | convolution fusion | flops 1216020480 | bytes 40116224 | tf_op jit(solution)/shard_map/td,tf->df/dot_general | solution.py:31
  571.7 5.6 fusion.201
  577.3 5.6 fusion.205
  583.0 5.5 fusion.203
  588.5 27.5 %reduce-scatter.21.cloned.1.call-done = bf16[1,256,768]{1,2,0:T(8,128)(2,1)} async-done(((bf16[1,1024,768]{1,2,0:T(8,128)(2,1)}), bf16[1,256,768]{1,2,0:T(8,128)(2,1)}) %reduce-scatter.21.cloned.1.call-update) | async-done | bytes 393232 | tf_op jit(solution)/shard_map/reduce_scatter | solution.py:141
  616.0 11.9 %add_add_fusion.2 = f32[768,2304]{1,0:T(8,128)} fusion(f32[768,2304]{1,0:T(8,128)} %fusion.201, f32[768,2304]{1,0:T(8,128)} %fusion.205, f32[768,2304]{1,0:T(8,128)} %fusion.203, bf16[256,768]{0,1:T(8,128)(2,1)} %bitcast.522, bf16[256,768]{0,1:T(8,128)(2,1)} %bitcast.525, bf16[256,768]{0,1:T(8,128)(2,1)} %bitcast.510, f32[256]{0:T(256)S(1)} %copy-done.165, ...), kind=kOutput, calls=%fused_computation.26 | convolution fusion | flops 915996672 | bytes 29892608 | tf_op jit(solution)/shard_map/td,te->de/dot_general | solution.py:31
  633.2 4.9 fusion.57
  660.4 42.7 %all-reduce = (f32[768]{0:T(1024)}, f32[768]{0:T(1024)}, f32[1536]{0:T(1024)}, f32[768]{0:T(1024)}, f32[768]{0:T(1024)}, /*index=5*/f32[768]{0:T(1024)}, f32[3072]{0:T(1024)}, f32[768]{0:T(1024)}) all-reduce(f32[768]{0:T(1024)} %add_add_fusion.18, f32[768]{0:T(1024)} %add_add_fusion.17, ...), channel_id=1, replica_groups=mesh['dp'=8,'seq'=4] {'dp','seq'}, use_global_device_ids=true, to_apply=%region_64.65 | all-reduce | flops 9216 | bytes 73728 | tf_op jit(solution)/shard_map/psum | solution.py:193
  713.0 348.3 %all-reduce.4.cloned.1.call-done = (f32[768,2304]{1,0:T(8,128)}, f32[768,768]{1,0:T(8,128)}, f32[768,3072]{1,0:T(8,128)}, f32[3072,768]{1,0:T(8,128)}) async-done(((f32[768,2304]{1,0:T(8,128)}, f32[768,768]{1,0:T(8,128)}, f32[768,3072]{1,0:T(8,128)}, f32[3072,768]{1,0:T(8,128)}), (f32[768,2304]{1,0:T(8,128)}, f32[768,768]{1,0:T(8,128)}, f32[768,3072]{1,0:T(8,128)}, ...) | async-done | bytes 28311568 | tf_op jit(solution)/shard_map/psum | solution.py:193
  1061.3 6.6 copy.97
  1069.3 9.3 copy.99
  (701 shorter events, 228.6 us)
Async XLA Ops:
  7.2 47.6 %all-gather.23.cloned.1.call-start = ((), (), s32[]{:S(2)}) async-start(), calls=%async_computation.15 | async-start | bytes 1966080 | tf_op jit(solution)/shard_map/all_gather | solution.py:90
  10.0 16.5 %copy-start.115 = (f32[256]{0:T(256)}, f32[256]{0:T(256)S(1)}, u32[]{:S(2)}) copy-start(f32[256]{0:T(256)S(1)} %get-tuple-element.191) | copy-start | bytes 3076
  16.5 67.3 %all-gather.21.cloned.1.call-start = ((), (), s32[]{:S(2)}) async-start(), calls=%async_computation.14 | async-start | bytes 1966080 | tf_op jit(solution)/shard_map/all_gather | solution.py:91
  17.2 99.9 %all-gather.19.cloned.1.call-start = ((), (), s32[]{:S(2)}) async-start(), calls=%async_computation.13 | async-start | bytes 1966080 | tf_op jit(solution)/shard_map/all_gather | solution.py:90
  21.2 129.2 %all-gather.17.cloned.1.call-start = ((), (), s32[]{:S(2)}) async-start(), calls=%async_computation.12 | async-start | bytes 1966080 | tf_op jit(solution)/shard_map/all_gather | solution.py:91
  21.8 165.6 %all-gather.15.cloned.1.call-start = ((), (), s32[]{:S(2)}) async-start(), calls=%async_computation.11 | async-start | bytes 1966080 | tf_op jit(solution)/shard_map/all_gather | solution.py:90
  25.8 190.0 %all-gather.13.cloned.1.call-start = ((), (), s32[]{:S(2)}) async-start(), calls=%async_computation.10 | async-start | bytes 1966080 | tf_op jit(solution)/shard_map/all_gather | solution.py:91
  26.4 222.3 %all-gather.11.cloned.1.call-start = ((), (), s32[]{:S(2)}) async-start(), calls=%async_computation.9 | async-start | bytes 1966080 | tf_op jit(solution)/shard_map/all_gather | solution.py:90
  29.7 251.8 %all-gather.9.cloned.1.call-start = ((), (), s32[]{:S(2)}) async-start(), calls=%async_computation.8 | async-start | bytes 1966080 | tf_op jit(solution)/shard_map/all_gather | solution.py:91
  30.5 541.1 %reduce-scatter.19.cloned.1.call-start = ((), (), s32[]{:S(2)}) async-start(), calls=%async_computation.21 | async-start | bytes 1966080 | tf_op jit(solution)/shard_map/reduce_scatter | solution.py:147
  66.2 28.1 %copy-start.108 = (f32[12,256]{1,0:T(8,128)}, f32[12,256]{1,0:T(8,128)S(1)}, u32[]{:S(2)}) copy-start(f32[12,256]{1,0:T(8,128)S(1)} %log_add_fusion) | copy-start | bytes 36868
  128.2 25.3 %copy-start.112 = (f32[12,256]{1,0:T(8,128)}, f32[12,256]{1,0:T(8,128)S(1)}, u32[]{:S(2)}) copy-start(f32[12,256]{1,0:T(8,128)S(1)} %log_add_fusion.1) | copy-start | bytes 36868
  161.6 14.5 %copy-start.104 = (bf16[12,64,256]{2,1,0:T(8,128)(2,1)}, bf16[12,64,256]{2,1,0:T(8,128)(2,1)S(1)}, u32[]{:S(2)}) copy-start(bf16[12,64,256]{2,1,0:T(8,128)(2,1)S(1)} %convolution_convert_fusion.9) | copy-start | bytes 1179652
  161.7 14.4 %slice-start.18 = ((s8[4718592]{0:T(1024)(128)(4,1)}), s8[4194304]{0:T(1024)(128)(4,1)S(1)}, s32[]{:S(2)}) async-start(s8[4718592]{0:T(1024)(128)(4,1)} %bitcast.574), calls=%async_computation.43 | async-start | bytes 8388608
  163.5 12.6 %copy-start.27 = (f32[256,768]{1,0:T(8,128)}, f32[256,768]{1,0:T(8,128)S(1)}, u32[]{:S(2)}) copy-start(f32[256,768]{1,0:T(8,128)S(1)} %get-tuple-element.156) | copy-start | bytes 2359300
  229.2 101.9 %copy-start.127 = (f32[256]{0:T(256)}, f32[256]{0:T(256)S(1)}, u32[]{:S(2)}) copy-start(f32[256]{0:T(256)S(1)} %broadcast_multiply_fusion.4) | copy-start | bytes 3076
  284.1 22.4 %slice-start.22 = ((s8[4718592]{0:T(1024)(128)(4,1)}), s8[4194304]{0:T(1024)(128)(4,1)S(1)}, s32[]{:S(2)}) async-start(s8[4718592]{0:T(1024)(128)(4,1)} %bitcast.578), calls=%async_computation.47 | async-start | bytes 8388608
  284.1 25.3 %slice-start.20 = ((s8[4718592]{0:T(1024)(128)(4,1)}), s8[4194304]{0:T(1024)(128)(4,1)S(1)}, s32[]{:S(2)}) async-start(s8[4718592]{0:T(1024)(128)(4,1)} %bitcast.576), calls=%async_computation.45 | async-start | bytes 8388608
  292.2 14.3 %copy-start.106 = (bf16[12,64,256]{2,1,0:T(8,128)(2,1)}, bf16[12,64,256]{2,1,0:T(8,128)(2,1)S(1)}, u32[]{:S(2)}) copy-start(bf16[12,64,256]{2,1,0:T(8,128)(2,1)S(1)} %convolution_convert_fusion.11) | copy-start | bytes 1179652
  294.0 37.1 %copy-start.35 = (f32[256,768]{1,0:T(8,128)}, f32[256,768]{1,0:T(8,128)S(1)}, u32[]{:S(2)}) copy-start(f32[256,768]{1,0:T(8,128)S(1)} %get-tuple-element.166) | copy-start | bytes 2359300
  294.0 37.1 %copy-start.129 = (f32[256]{0:T(256)}, f32[256]{0:T(256)S(1)}, u32[]{:S(2)}) copy-start(f32[256]{0:T(256)S(1)} %broadcast_multiply_fusion.6) | copy-start | bytes 3076
  294.2 36.9 %copy-start.154 = (f32[256]{0:T(256)}, f32[256]{0:T(256)S(1)}, u32[]{:S(2)}) copy-start(f32[256]{0:T(256)S(1)} %fusion.177) | copy-start | bytes 3076
  294.3 12.3 %copy-start.14 = (bf16[4,1,256,768]{3,2,1,0:T(8,128)(2,1)S(1)}, bf16[4,1,256,768]{3,2,1,0:T(8,128)(2,1)}, u32[]{:S(2)}) copy-start(bf16[4,1,256,768]{3,2,1,0:T(8,128)(2,1)} %param.17) | copy-start | bytes 4718596
  294.3 12.3 %slice-start.23 = ((s8[4718592]{0:T(1024)(128)(4,1)}), s8[524288]{0:T(1024)(128)(4,1)S(1)}, s32[]{:S(2)}) async-start(s8[4718592]{0:T(1024)(128)(4,1)} %bitcast.578), calls=%async_computation.48 | async-start | bytes 1048576
  294.3 12.3 %copy-start.214 = (f32[256,3072]{1,0:T(8,128)S(1)}, f32[256,3072]{1,0:T(8,128)}, u32[]{:S(2)}) copy-start(f32[256,3072]{1,0:T(8,128)} %get-tuple-element.93) | copy-start | bytes 9437188
  294.3 12.3 %copy-start.215 = (f32[256,3072]{1,0:T(8,128)S(1)}, f32[256,3072]{1,0:T(8,128)}, u32[]{:S(2)}) copy-start(f32[256,3072]{1,0:T(8,128)} %get-tuple-element.152) | copy-start | bytes 9437188
  294.3 15.1 %slice-start.21 = ((s8[4718592]{0:T(1024)(128)(4,1)}), s8[524288]{0:T(1024)(128)(4,1)S(1)}, s32[]{:S(2)}) async-start(s8[4718592]{0:T(1024)(128)(4,1)} %bitcast.576), calls=%async_computation.46 | async-start | bytes 1048576
  347.4 224.2 %reduce-scatter.17.cloned.1.call-start = ((), (), s32[]{:S(2)}) async-start(), calls=%async_computation.20 | async-start | bytes 1966080 | tf_op jit(solution)/shard_map/reduce_scatter | solution.py:141
  367.5 209.8 %reduce-scatter.11.cloned.1.call-start = ((), (), s32[]{:S(2)}) async-start(), calls=%async_computation.17 | async-start | bytes 1966080 | tf_op jit(solution)/shard_map/reduce_scatter | solution.py:147
  381.6 195.7 %reduce-scatter.9.cloned.1.call-start = ((), (), s32[]{:S(2)}) async-start(), calls=%async_computation.16 | async-start | bytes 1966080 | tf_op jit(solution)/shard_map/reduce_scatter | solution.py:141
  401.6 181.4 %reduce-scatter.15.cloned.1.call-start = ((), (), s32[]{:S(2)}) async-start(), calls=%async_computation.19 | async-start | bytes 1966080 | tf_op jit(solution)/shard_map/reduce_scatter | solution.py:147
  426.7 156.3 %reduce-scatter.13.cloned.1.call-start = ((), (), s32[]{:S(2)}) async-start(), calls=%async_computation.18 | async-start | bytes 1966080 | tf_op jit(solution)/shard_map/reduce_scatter | solution.py:141
  426.7 13.3 %copy-start.13 = (bf16[768,768]{1,0:T(8,128)(2,1)S(1)}, bf16[768,768]{1,0:T(8,128)(2,1)}, u32[]{:S(2)}) copy-start(bf16[768,768]{1,0:T(8,128)(2,1)} %param.22) | copy-start | bytes 3538948
  426.7 13.2 %copy-start.56 = (bf16[256,768]{1,0:T(8,128)(2,1)S(1)}, bf16[256,768]{1,0:T(8,128)(2,1)}, u32[]{:S(2)}) copy-start(bf16[256,768]{1,0:T(8,128)(2,1)} %get-tuple-element.103) | copy-start | bytes 1179652
  448.7 12.7 %slice-start.2 = ((s8[12582912]{0:T(1024)(128)(4,1)}), s8[4194304]{0:T(1024)(128)(4,1)S(1)}, s32[]{:S(2)}) async-start(s8[12582912]{0:T(1024)(128)(4,1)} %bitcast.468), calls=%async_computation.27 | async-start | bytes 8388608
  471.1 117.4 %reduce-scatter.23.cloned.1.call-start = ((), (), s32[]{:S(2)}) async-start(), calls=%async_computation.23 | async-start | bytes 1966080 | tf_op jit(solution)/shard_map/reduce_scatter | solution.py:147
  476.4 11.8 %slice-start.8 = ((s8[6291456]{0:T(1024)(128)(4,1)}), s8[4194304]{0:T(1024)(128)(4,1)S(1)}, s32[]{:S(2)}) async-start(s8[6291456]{0:T(1024)(128)(4,1)} %bitcast.474), calls=%async_computation.33 | async-start | bytes 8388608
  495.9 120.1 %reduce-scatter.21.cloned.1.call-start = ((), (), s32[]{:S(2)}) async-start(), calls=%async_computation.22 | async-start | bytes 1966080 | tf_op jit(solution)/shard_map/reduce_scatter | solution.py:141
  531.0 530.3 %all-reduce.4.cloned.1.call-start = ((), (), s32[]{:S(2)}) async-start(), calls=%async_computation.24 | async-start | bytes 56623104 | tf_op jit(solution)/shard_map/psum | solution.py:193
  531.5 15.5 %copy-start.21 = (f32[768,768]{1,0:T(8,128)S(1)}, f32[768,768]{1,0:T(8,128)}, u32[]{:S(2)}) copy-start(f32[768,768]{1,0:T(8,128)} %fusion.251) | copy-start | bytes 7077892
  531.5 15.5 %copy-start.57 = (bf16[256,768]{1,0:T(8,128)(2,1)S(1)}, bf16[256,768]{1,0:T(8,128)(2,1)}, u32[]{:S(2)}) copy-start(bf16[256,768]{1,0:T(8,128)(2,1)} %get-tuple-element.103) | copy-start | bytes 1179652
  531.5 15.5 %copy-start.103 = (bf16[12,64,256]{2,1,0:T(8,128)(2,1)S(1)}, bf16[12,64,256]{2,1,0:T(8,128)(2,1)}, u32[]{:S(2)}) copy-start(bf16[12,64,256]{2,1,0:T(8,128)(2,1)} %copy-done.102) | copy-start | bytes 1179652
  547.0 11.7 %slice-start.12 = ((s8[9437184]{0:T(1024)(128)(4,1)}), s8[4194304]{0:T(1024)(128)(4,1)S(1)}, s32[]{:S(2)}) async-start(s8[9437184]{0:T(1024)(128)(4,1)} %bitcast.478), calls=%async_computation.37 | async-start | bytes 8388608
  558.8 12.8 %copy-start.94 = (f32[768]{0:T(1024)S(1)}, f32[768]{0:T(1024)}, u32[]{:S(2)}) copy-start(f32[768]{0:T(1024)} %param.18) | copy-start | bytes 9220
  558.8 12.8 %copy-start.101 = (f32[768]{0:T(1024)S(1)}, f32[768]{0:T(1024)}, u32[]{:S(2)}) copy-start(f32[768]{0:T(1024)} %param.19) | copy-start | bytes 9220
  582.9 33.1 %copy-start.136 = (f32[256]{0:T(256)S(1)}, f32[256]{0:T(256)}, u32[]{:S(2)}) copy-start(f32[256]{0:T(256)} %copy-done.135) | copy-start | bytes 3076
  582.9 33.1 %copy-start.165 = (f32[256]{0:T(256)S(1)}, f32[256]{0:T(256)}, u32[]{:S(2)}) copy-start(f32[256]{0:T(256)} %copy-done.164) | copy-start | bytes 3076
  628.6 13.6 %slice-start.24 = ((s8[4718592]{0:T(1024)(128)(4,1)}), s8[4194304]{0:T(1024)(128)(4,1)S(1)}, s32[]{:S(2)}) async-start(s8[4718592]{0:T(1024)(128)(4,1)} %bitcast.580), calls=%async_computation.49 | async-start | bytes 8388608
  (215 other events, 1002.6 us)
Sparse Core Ops, SparseCore 0:
  16.6 33.6 all-gather.22
  52.7 30.9 all-gather.20
  86.1 30.9 all-gather.18
  119.4 30.9 all-gather.16
  152.1 30.9 all-gather.14
  184.8 30.9 all-gather.12
  217.7 30.9 all-gather.10
  250.5 30.9 all-gather.8
  347.6 30.9 reduce-scatter.18
  381.4 30.9 reduce-scatter.16
  415.3 30.9 reduce-scatter.10
  449.1 30.8 reduce-scatter.8
  483.1 30.9 reduce-scatter.14
  516.9 30.8 reduce-scatter.12
  551.3 30.8 reduce-scatter.22
  585.1 30.9 reduce-scatter.20
  628.0 433.2 all-reduce.3
where the time goes:
time: 1100 us; the launch traced here: 1090 us
  waiting for transfers between devices  481 us (44%)
  matrix products  367 us (33%)
  other arithmetic  97.4 us (9%)
  local copies, waits for them, and re-layouts  81.6 us (7%)
  blocking collectives  42.7 us (4%)
  between operations  17.3 us (2%)
    dot_general x72, matrix products, matmul(): jnp.einsum(pattern, first_op, second_op, preferred_element_type=jnp.float32)  367 us
    psum x1, waiting for transfers between devices, shards(): lax.psum((attn_gain_sum, attn_shift_sum, qkv_weight_sum, qv_bias_sum, out...  348 us
    all_gather x4, waiting for transfers between devices, shards(): lax.all_gather(projected[:, :, 2 * features:], 'seq', axis=1, tiled=True)  64 us
    psum x1, blocking collectives, shards(): lax.psum((attn_gain_sum, attn_shift_sum, qkv_weight_sum, qv_bias_sum, out...  42.7 us
    unnamed x496, local copies, waits for them, and re-layouts  39 us
    all_gather x4, waiting for transfers between devices, shards(): lax.all_gather(projected[:, :, features:2 * features], 'seq', axis=1, til...  38.2 us
    convert_element_type x4, other arithmetic, shards(): score_grad = (chances * (chance_grad - row_delta)).astype(jnp.bfloat16)  37.2 us
    reduce_scatter x4, waiting for transfers between devices, shards(): lax.psum_scatter(key_terms.reshape(row_count, row_len, features).astype(j...  27.5 us
  transfers between devices with their start and end apart: 17, of which 8 were waited for; matrix products, arithmetic and copies ran while one was open for 39% of the time, Pallas kernels for 0%

commit v1 on v0

--- a/solution.py
+++ b/solution.py
@@ -1,6 +1,10 @@
+import functools
+
 import jax
 import jax.numpy as jnp
 from jax import lax
+from jax.experimental import pallas as pl
+from jax.experimental.pallas import tpu as pltpu
 from jax.sharding import PartitionSpec as P
 
 HEADS = 12
@@ -31,7 +35,7 @@
     return jnp.einsum(pattern, first_op, second_op, preferred_element_type=jnp.float32)
 
 
-def shards(
+def general_shards(
     tokens,
     image_lengths,
     cotangent,
@@ -209,6 +213,320 @@
     )
     return (jnp.stack(outputs_list), jnp.stack(grads_list)) + tuple(summed)
 
+F32 = jnp.float32
+BF = jnp.bfloat16
+BIG = 1e30
+
+
+def dot_rows(first_op, second_op):
+    return lax.dot_general(first_op, second_op, (((1,), (1,)), ((), ())), preferred_element_type=F32)
+
+
+def dot_plain(first_op, second_op):
+    return lax.dot_general(first_op, second_op, (((1,), (0,)), ((), ())), preferred_element_type=F32)
+
+
+def dot_tokens(first_op, second_op):
+    return lax.dot_general(first_op, second_op, (((0,), (0,)), ((), ())), preferred_element_type=F32)
+
+
+def attention_forward_kernel(block, q_ref, k_ref, v_ref, miss_ref, own_ref, out_ref, lse_ref):
+    lane = lax.broadcasted_iota(jnp.int32, (1, 128), 1)
+    first = lane < 64
+    keys, values, own = k_ref[...], v_ref[...], own_ref[...]
+    ones = jnp.ones_like(values)
+    keys_aug = [jnp.where(first, keys, own), jnp.where(first, own, keys)]
+    values_aug = [jnp.where(first, values, ones), jnp.where(first, ones, values)]
+    for step in range(q_ref.shape[0] // block):
+        rows = pl.ds(step * block, block)
+        queries, miss = q_ref[rows, :] * BF(0.125), miss_ref[rows, :]
+        outs, logs = [], []
+        for head in range(2):
+            queries_aug = jnp.where(first, queries, miss) if head == 0 else jnp.where(first, miss, queries)
+            scores = dot_rows(queries_aug, keys_aug[head])
+            largest = jnp.max(scores, axis=1, keepdims=True)
+            weights = jnp.exp(scores - largest).astype(BF)
+            mixed = dot_plain(weights, values_aug[head])
+            total = mixed[:, 64:65] if head == 0 else mixed[:, 0:1]
+            outs.append(mixed / total)
+            logs.append(largest + jnp.log(total))
+        out_ref[rows, :] = jnp.where(first, outs[0], outs[1]).astype(BF)
+        lse_ref[0, rows, :] = jnp.where(first, logs[0], logs[1])
+
+
+def attention_forward(projected, miss, own, block=256):
+    count, width = projected.shape
+    pairs = width // 384
+    column = lambda base: pl.BlockSpec((count, 128), lambda i: (0, i + base))
+    full = pl.BlockSpec((count, 128), lambda i: (0, 0))
+    return pl.pallas_call(
+        functools.partial(attention_forward_kernel, block),
+        grid=(pairs,),
+        in_specs=[column(0), column(pairs), column(2 * pairs), full, full],
+        out_specs=[column(0), pl.BlockSpec((1, count, 128), lambda i: (i, 0, 0))],
+        out_shape=[
+            jax.ShapeDtypeStruct((count, width // 3), BF),
+            jax.ShapeDtypeStruct((pairs, count, 128), F32),
+        ],
+        compiler_params=pltpu.CompilerParams(vmem_limit_bytes=40 * 2**20),
+        cost_estimate=pl.CostEstimate(flops=24 * 10**9, bytes_accessed=8 * 2**20, transcendentals=12 * 2**20),
+        name="attention_forward",
+    )(projected, projected, projected, miss, own)
+
+
+def three_parts(column):
+    high = column.astype(BF)
+    rest = column - high.astype(F32)
+    middle = rest.astype(BF)
+    return high, middle, (rest - middle.astype(F32)).astype(BF)
+
+
+def attention_backward_kernel(
+    block, q_ref, k_ref, v_ref, att_ref, grad_ref, lse_ref, miss_ref, own_ref,
+    dq_ref, dk_ref, dv_ref, dk_acc, dv_acc,
+):
+    lane = lax.broadcasted_iota(jnp.int32, (1, 128), 1)
+    first = lane < 64
+    half = lane % 64
+    keys, values, own = k_ref[...], v_ref[...], own_ref[...]
+    unit = jnp.where((half >= 8) & (half < 11), 1.0, 0.0).astype(BF)
+    own = own + unit
+    unit_rows = jnp.broadcast_to(unit, values.shape)
+    keys_aug = [jnp.where(first, keys, own), jnp.where(first, own, keys)]
+    values_aug = [jnp.where(first, values, unit_rows), jnp.where(first, unit_rows, values)]
+    keys_only = [jnp.where(first, keys, BF(0)), jnp.where(first, BF(0), keys)]
+    dk_acc[...] = jnp.zeros_like(dk_acc)
+    dv_acc[...] = jnp.zeros_like(dv_acc)
+
+    def spread(column):
+        high, middle, low = [part.astype(F32) for part in three_parts(-column)]
+        wide = jnp.where(half == 8, high, jnp.where(half == 9, middle, jnp.where(half == 10, low, 0.0)))
+        return wide.astype(BF)
+
+    def body(step, carry):
+        rows = pl.ds(pl.multiple_of(step * block, block), block)
+        queries, miss, grad = q_ref[rows, :] * BF(0.125), miss_ref[rows, :], grad_ref[rows, :]
+        both = att_ref[rows, :].astype(F32) * grad.astype(F32)
+        logs = lse_ref[0, rows, :]
+        queries_t, grad_t = queries.T, grad.T
+        dq = jnp.zeros((block, 128), F32)
+        for head in range(2):
+            mine = first if head == 0 else jnp.logical_not(first)
+            span = pl.ds(64 * head, 64)
+            delta = jnp.sum(jnp.where(mine, both, 0.0), axis=1, keepdims=True)
+            total = logs[:, 0:1] if head == 0 else logs[:, 64:65]
+            queries_aug = jnp.where(mine, queries, spread(total) + miss)
+            grad_aug = jnp.where(mine, grad, spread(delta))
+            probs = jnp.exp(dot_rows(queries_aug, keys_aug[head]))
+            score_grad = (probs * dot_rows(grad_aug, values_aug[head])).astype(BF)
+            dq = dq + dot_plain(score_grad, keys_only[head])
+            dk_acc[span, :] += dot_plain(queries_t[64 * head : 64 * head + 64], score_grad)
+            dv_acc[span, :] += dot_plain(grad_t[64 * head : 64 * head + 64], probs.astype(BF))
+        dq_ref[rows, :] = (dq * 0.125).astype(BF)
+        return carry
+
+    lax.fori_loop(0, q_ref.shape[0] // block, body, 0)
+    dk_ref[...] = dk_acc[...].T.astype(BF)
+    dv_ref[...] = dv_acc[...].T.astype(BF)
+
+
+def attention_backward(projected, attended, attended_grad, logs, miss, own, block=256):
+    count, width = projected.shape
+    pairs = width // 384
+    column = lambda base: pl.BlockSpec((count, 128), lambda i: (0, i + base))
+    full = pl.BlockSpec((count, 128), lambda i: (0, 0))
+    return pl.pallas_call(
+        functools.partial(attention_backward_kernel, block),
+        grid=(pairs,),
+        in_specs=[
+            column(0), column(pairs), column(2 * pairs), column(0), column(0),
+            pl.BlockSpec((1, count, 128), lambda i: (i, 0, 0)), full, full,
+        ],
+        out_specs=[column(0)] * 3,
+        out_shape=[jax.ShapeDtypeStruct((count, width // 3), BF)] * 3,
+        scratch_shapes=[pltpu.VMEM((128, count), F32)] * 2,
+        compiler_params=pltpu.CompilerParams(vmem_limit_bytes=40 * 2**20),
+        cost_estimate=pl.CostEstimate(flops=40 * 10**9, bytes_accessed=16 * 2**20, transcendentals=12 * 2**20),
+        name="attention_backward",
+    )(projected, projected, projected, attended, attended_grad, logs, miss, own)
+
+
+def segment_features(segment):
+    lane = jnp.arange(128) % 64
+    same = lane[None, :] == segment[:, None]
+    live = (lane < 8)[None, :]
+    return jnp.where(live & ~same, -BIG, 0.0).astype(BF), jnp.where(live & same, 1.0, 0.0).astype(BF)
+
+
+def gelu_parts(values):
+    size = jnp.abs(values)
+    bell = jnp.exp(-0.5 * values * values)
+    part = 1.0 / (1.0 + 0.3275911 * 0.7071067811865476 * size)
+    series = part * (
+        0.254829592
+        + part * (-0.284496736 + part * (1.421413741 + part * (-1.453152027 + part * 1.061405429)))
+    )
+    tail = 0.5 * series * bell
+    below = jnp.where(values >= 0, 1.0 - tail, tail)
+    return values * below, below + values * bell * 0.3989422804014327
+
+
+def swap(array, axis, bit):
+    count = lax.axis_size(axis)
+    return lax.ppermute(array, axis, [(i, i ^ bit) for i in range(count)])
+
+
+def pick(array, index):
+    return lax.dynamic_index_in_dim(array, index, 0, keepdims=False)
+
+
+def half_of(array, index):
+    size = array.shape[0] // 2
+    return lax.dynamic_slice_in_dim(array, index * size, size, 0)
+
+
+def join(own, other, bit):
+    size = own.shape[0]
+    both = jnp.zeros((2 * size,) + own.shape[1:], own.dtype)
+    both = lax.dynamic_update_slice_in_dim(both, own, bit * size, 0)
+    return lax.dynamic_update_slice_in_dim(both, other, (1 - bit) * size, 0)
+
+
+def reduce_everywhere(send, keep, stages):
+    axis, bit, mine = stages[0]
+    got = swap(send, axis, bit)
+    core = mine
+    for axis, bit, mine in stages[1:]:
+        out = (half_of(keep, 1 - mine).astype(F32) + half_of(got, 1 - mine).astype(F32)).astype(BF)
+        keep = (half_of(keep, mine).astype(F32) + half_of(got, mine).astype(F32)).astype(BF)
+        got = swap(out, axis, bit)
+    total = (keep.astype(F32) + got.astype(F32)).astype(BF)
+    for axis, bit, mine in reversed(stages[1:]):
+        total = join(total, swap(total, axis, bit), mine)
+    axis, bit, mine = stages[0]
+    return total, swap(total, axis, bit)
+
+
+def split_grad(left, right, core, stages):
+    size = right.shape[1] // 2
+    parts = [
+        dot_tokens(left, lax.dynamic_slice_in_dim(right, index * size, size, 1)).astype(BF)
+        for index in (1 - core, core)
+    ]
+    own, other = reduce_everywhere(parts[0], parts[1], stages)
+    low = jnp.where(core == 0, own, other)
+    high = jnp.where(core == 0, other, own)
+    return jnp.concatenate([low, high], axis=1).astype(F32)
+
+
+def fast_shards(
+    tokens, image_lengths, cotangent, attn_gain, attn_shift, qkv_weight, qv_bias, out_weight,
+    out_bias, mlp_gain, mlp_shift, fc1_weight, fc1_bias, fc2_weight, fc2_bias,
+):
+    micro_count, _, shard_len, features = tokens.shape
+    parties = micro_count
+    row_len = shard_len * parties
+    images = image_lengths.shape[2] - 1
+    me = lax.axis_index("seq")
+    depth = lax.axis_index("dp")
+    core = depth % 2
+
+    def bits(axis, index, low):
+        count = lax.axis_size(axis)
+        return [(axis, 1 << k, (index >> k) & 1) for k in range(low, count.bit_length() - 1)]
+
+    core_stage = [("dp", 1, core)]
+    flat_bits, deep_bits = bits("seq", me, 0), bits("dp", depth, 1)
+    orders = [core_stage + flat_bits + deep_bits, core_stage + flat_bits[::-1] + deep_bits]
+
+    def gather_row(array):
+        pieces = [pick(array, me)[0]]
+        for k in range(1, parties):
+            pieces.append(swap(pick(array, me ^ k)[0], "seq", k))
+        return jnp.concatenate(pieces, axis=0)
+
+    def scatter_row(array):
+        out = jnp.zeros(tokens.shape, BF)
+        for k in range(parties):
+            piece = array[k * shard_len : (k + 1) * shard_len]
+            if k:
+                piece = swap(piece, "seq", k)
+            out = lax.dynamic_update_slice(out, piece[None, None], (me ^ k, 0, 0, 0))
+        return out
+
+    seg_row = segment_ids(pick(image_lengths, me), row_len, images).reshape(parties, shard_len)
+    segment = jnp.concatenate([pick(seg_row, me ^ k) for k in range(parties)], axis=0)
+    miss, own = segment_features(segment)
+
+    inputs = gather_row(tokens).astype(F32)
+    incoming = gather_row(cotangent)
+    full_bias = jnp.concatenate([qv_bias[:features], jnp.zeros((features,), F32), qv_bias[features:]])
+    normed, first_pull = jax.vjp(layer_norm, inputs, attn_gain, attn_shift)
+    normed_low = normed.astype(BF)
+    projected = (dot_plain(normed_low, qkv_weight) + full_bias).astype(BF)
+    attended, logs = attention_forward(projected, miss, own)
+    middle = inputs + dot_plain(attended, out_weight) + out_bias
+    normed_two, second_pull = jax.vjp(layer_norm, middle, mlp_gain, mlp_shift)
+    normed_two_low = normed_two.astype(BF)
+    hidden_pre = dot_plain(normed_two_low, fc1_weight) + fc1_bias
+    hidden, slope = gelu_parts(hidden_pre)
+    hidden_low = hidden.astype(BF)
+    result = (middle + dot_plain(hidden_low, fc2_weight) + fc2_bias).astype(BF)
+    block_out = scatter_row(result)
+    hidden_grad = (dot_rows(incoming, fc2_weight) * slope).astype(BF)
+
+    half_hidden = hidden_low.shape[1] // 2
+    fc2_parts = [
+        dot_tokens(lax.dynamic_slice_in_dim(hidden_low, index * half_hidden, half_hidden, 1), incoming).astype(BF)
+        for index in (1 - core, core)
+    ]
+    fc2_own, fc2_other = reduce_everywhere(fc2_parts[0], fc2_parts[1], orders[0])
+    fc2_grad = jnp.concatenate(
+        [jnp.where(core == 0, fc2_own, fc2_other), jnp.where(core == 0, fc2_other, fc2_own)], axis=0
+    ).astype(F32)
+    fc1_grad = split_grad(normed_two_low, hidden_grad, core, orders[1])
+
+    back_two = dot_rows(hidden_grad, fc1_weight)
+    middle_norm, mlp_gain_part, mlp_shift_part = second_pull(back_two)
+    middle_grad = incoming.astype(F32) + middle_norm
+    branch_grad = middle_grad.astype(BF)
+    out_grad = split_grad(attended, branch_grad, core, orders[0])
+    attended_grad = dot_rows(branch_grad, out_weight).astype(BF)
+    pieces = attention_backward(projected, attended, attended_grad, logs, miss, own)
+    projected_grad = jnp.concatenate(pieces, axis=1)
+    qkv_grads = [split_grad(normed_low, piece, core, orders[i % 2]) for i, piece in enumerate(pieces)]
+    back_one = dot_rows(projected_grad, qkv_weight)
+    inputs_norm, attn_gain_part, attn_shift_part = first_pull(back_one)
+    tokens_grad = scatter_row((middle_grad + inputs_norm).astype(BF))
+
+    column = lambda array: jnp.sum(array.astype(F32), axis=0)
+    sums = [
+        attn_gain_part, attn_shift_part, column(pieces[0]), column(pieces[2]), column(branch_grad),
+        mlp_gain_part, mlp_shift_part, column(hidden_grad), column(incoming),
+    ]
+    vector = jnp.concatenate(sums)
+    for axis, bit, _ in orders[0]:
+        vector = vector + swap(vector, axis, bit)
+    cuts = []
+    for part in sums:
+        cuts.append(vector[: part.shape[0]])
+        vector = vector[part.shape[0] :]
+    return (
+        block_out, tokens_grad, cuts[0], cuts[1], jnp.concatenate(qkv_grads, axis=1),
+        jnp.concatenate(cuts[2:4]), out_grad, cuts[4], cuts[5], cuts[6], fc1_grad, cuts[7],
+        fc2_grad, cuts[8],
+    )
+
+
+def shards(tokens, *rest):
+    micro_count, row_count, shard_len, features = tokens.shape
+    sizes = (lax.axis_size("dp"), lax.axis_size("seq"))
+    powers = all(size & (size - 1) == 0 for size in sizes) and sizes[0] > 1
+    whole_rows = micro_count == sizes[1] and row_count == 1
+    if powers and whole_rows and shard_len % 128 == 0 and features == 64 * HEADS and HEADS % 2 == 0:
+        return fast_shards(tokens, *rest)
+    return general_shards(tokens, *rest)
+
 
 def solution(mesh):
     placed = (

time: 1100 us -> 537 us (0.49)
  waiting for transfers between devices: 481 us -> 156 us
  matrix products: 367 us -> 108 us
  starting transfers between devices: 2.1 us -> 74.5 us
  Pallas kernels: 0 us -> 66.6 us
  blocking collectives: 42.7 us -> 0 us
  other arithmetic: 97.4 us -> 56.1 us
  between operations: 17.3 us -> 3.07 us
  local copies, waits for them, and re-layouts: 81.6 us -> 68 us
    psum x1 -> x0, waiting for transfers between devices: 348 us -> none  [shards(): lax.psum((attn_gain_sum, attn_shift_sum, qkv_weight_sum, qv_bias_sum, out...]
    dot_general x72 -> x20, matrix products: 367 us -> 108 us  [the longest x4 41.1 us: dot_rows(): lax.dot_general(first_op, second_op, (((1,), (1,)), ((), ())), preferred_...]
    ppermute x0 -> x77, waiting for transfers between devices: none -> 156 us  [swap(): return lax.ppermute(array, axis, [(i, i ^ bit) for i in range(count)])]
    all_gather x8 -> x0, waiting for transfers between devices: 102 us -> none  [the longest x4 64 us: shards(): lax.all_gather(projected[:, :, 2 * features:], 'seq', axis=1, tiled=True)]
    ppermute x0 -> x77, starting transfers between devices: none -> 74.5 us  [swap(): return lax.ppermute(array, axis, [(i, i ^ bit) for i in range(count)])]
    pallas_call x0 -> x2, Pallas kernels: none -> 66.6 us  [the longest x1 41.2 us: attention_backward(): pl.pallas_call(functools.partial(attention_backward_kernel, block), grid=...]
    psum x1 -> x0, blocking collectives: 42.7 us -> none  [shards(): lax.psum((attn_gain_sum, attn_shift_sum, qkv_weight_sum, qv_bias_sum, out...]
    unnamed x496 -> x170, local copies, waits for them, and re-layouts: 39 us -> 4.42 us
  transfers between devices with their start and end apart: 17 -> 77, of which waited for: 8 -> 28; matrix products, arithmetic and copies ran while one was open for 39% -> 29% of each run, Pallas kernels for 0% -> 5%
where the time goes in v1:
time: 537 us; the launch traced here: 532 us
  waiting for transfers between devices  156 us (29%)
  matrix products  108 us (20%)
  starting transfers between devices  74.5 us (14%)
  local copies, waits for them, and re-layouts  68 us (13%)
  Pallas kernels  66.6 us (12%)
  other arithmetic  56.1 us (10%)
    ppermute x77, waiting for transfers between devices, swap(): return lax.ppermute(array, axis, [(i, i ^ bit) for i in range(count)])  156 us
    ppermute x77, starting transfers between devices, swap(): return lax.ppermute(array, axis, [(i, i ^ bit) for i in range(count)])  74.5 us
    pallas_call x1, Pallas kernels, attention_backward(): pl.pallas_call(functools.partial(attention_backward_kernel, block), grid=...  41.2 us
    dot_general x4, matrix products, dot_rows(): lax.dot_general(first_op, second_op, (((1,), (1,)), ((), ())), preferred_...  41.1 us
    dot_general x12, matrix products, dot_tokens(): lax.dot_general(first_op, second_op, (((0,), (0,)), ((), ())), preferred_...  33.4 us
    dot_general x4, matrix products, dot_plain(): lax.dot_general(first_op, second_op, (((1,), (0,)), ((), ())), preferred_...  33.2 us
    pallas_call x1, Pallas kernels, attention_forward(): pl.pallas_call(functools.partial(attention_forward_kernel, block), grid=(...  25.4 us
    dynamic_slice x10, local copies, waits for them, and re-layouts, pick(): return lax.dynamic_index_in_dim(array, index, 0, keepdims=False)  19.1 us
  transfers between devices with their start and end apart: 77, of which 28 were waited for; matrix products, arithmetic and copies ran while one was open for 29% of the time, Pallas kernels for 5%

profile of v1, /device:TPU:0, one launch (start us, length us, event | category | flops | bytes accessed | tf_op | source)
XLA Modules:
  0.0 532.3 jit_solution(6047247715149087086)
XLA Ops:
  0.7 3.7 constant_dynamic-slice_fusion.19
  6.3 3.9 collective-permute-start.2
  16.5 2.9 collective-permute-start.8
  37.2 4.2 add_convert_fusion.q_ref.k_ref.v_ref
  41.5 25.4 %attention_forward.1 = (bf16[1024,768]{1,0:T(8,128)(2,1)S(1)}, f32[6,1024,128]{2,1,0:T(8,128)S(1)}) custom-call(bf16[1024,2304]{1,0:T(8,128)(2,1)S(1)} %add_convert_fusion.q_ref.k_ref.v_ref, bf16[1024,2304]{1,0:T(8,128)(2,1)S(1)} %add_convert_fusion.q_ref.k_ref.v_ref, bf16[1024,2304]{1,0:T(8,128)(2,1)S(1)} %add_convert_fusion.q_ref.k_ref.v_ref, ...), custom_call_target="tpu_custom_call" | custom-call | flops 24000000000 | bytes 8388608 | tf_op jit(solution)/shard_map/attention_forward/pallas_call | solution.py:262
  66.9 3.6 fusion.68
  72.7 16.7 %multiply_convert_fusion = (bf16[1024,3072]{1,0:T(8,128)(2,1)}, f32[1024,3072]{1,0:T(8,128)}) fusion(f32[3072]{0:T(1024)S(1)} %copy-done.72, bf16[1024,768]{0,1:T(8,128)(2,1)S(1)} %add_convert_fusion.3, bf16[768,3072]{1,0:T(8,128)(2,1)S(1)} %bitcast.73), kind=kOutput, calls=%fused_computation.10 | convolution fusion | flops 4904189952 | bytes 25178112 | tf_op jit(solution)/shard_map/dot_general | solution.py:226
  89.4 22.2 %convert_reduce_fusion = (f32[3072]{0:T(1024)}, bf16[1024,3072]{1,0:T(8,128)(2,1)}) fusion(f32[1024,3072]{1,0:T(8,128)} %get-tuple-element.120, f32[3072]{0:T(1024)S(1)} %copy-done.72, bf16[3072,768]{1,0:T(8,128)(2,1)} %param.28, bf16[256,768]{0,1:T(8,128)(2,1)} %collective-permute-done.8, bf16[256,768]{0,1:T(8,128)(2,1)} %collective-permute-done.7, ...), kind=kOutput, calls=%fused_computation.9 | convolution fusion | flops 4926206976 | bytes 25190400 | tf_op jit(solution)/shard_map/dot_general | solution.py:222
  111.6 9.1 %fusion.70 = (f32[768]{0:T(1024)}, f32[1024,768]{1,0:T(8,128)}) fusion(bf16[1024,3072]{1,0:T(8,128)(2,1)} %get-tuple-element.126, bf16[768,3072]{1,0:T(8,128)(2,1)S(1)} %bitcast.73), kind=kOutput, calls=%fused_computation.294 | convolution fusion | flops 4832623616 | bytes 14158848 | tf_op jit(solution)/shard_map/dot_general | solution.py:222
  120.7 4.0 copy.63
  124.8 4.5 multiply_reduce_fusion
  130.6 3.2 convert_reduce_fusion.3
  136.9 41.2 %attention_backward.1 = (bf16[1024,768]{1,0:T(8,128)(2,1)S(1)}, bf16[1024,768]{1,0:T(8,128)(2,1)S(1)}, bf16[1024,768]{1,0:T(8,128)(2,1)S(1)}) custom-call(bf16[1024,2304]{1,0:T(8,128)(2,1)} %copy-done.14, bf16[1024,2304]{1,0:T(8,128)(2,1)} %copy-done.14, bf16[1024,2304]{1,0:T(8,128)(2,1)} %copy-done.14, bf16[1024,768]{1,0:T(8,128)(2,1)S(1)} %copy-done.10, ...), custom_call_target="tpu_custom_call" | custom-call | flops 40000000000 | bytes 16777216 | tf_op jit(solution)/shard_map/attention_backward/pallas_call | solution.py:338
  182.4 8.8 %add_convert_fusion.2 = bf16[1024,768]{0,1:T(8,128)(2,1)S(1)} fusion(f32[1024,768]{0,1:T(8,128)S(1)} %copy-done.18, bf16[1024,3072]{1,0:T(8,128)(2,1)} %get-tuple-element.119, bf16[3072,768]{1,0:T(8,128)(2,1)} %param.28, f32[768]{0:T(1024)S(1)} %copy-done.74), kind=kOutput, calls=%fused_computation.53 | convolution fusion | flops 4834197504 | bytes 15731712 | tf_op jit(solution)/shard_map/dot_general | solution.py:226
  197.7 2.3 convert_reduce_fusion.4
  200.0 8.5 %fusion.69 = (f32[768]{0:T(1024)}, f32[1024,768]{1,0:T(8,128)}) fusion(bf16[768,2304]{1,0:T(8,128)(2,1)S(1)} %copy-done, bf16[1024,768]{1,0:T(8,128)(2,1)} %copy-done.1, bf16[1024,768]{1,0:T(8,128)(2,1)} %copy-done.12, bf16[1024,768]{1,0:T(8,128)(2,1)} %copy-done.3), kind=kOutput, calls=%fused_computation.293 | convolution fusion | flops 3638820096 | bytes 11406336 | tf_op jit(solution)/shard_map/dot_general | solution.py:222
  208.5 3.6 copy.64
  212.1 3.0 fusion.23
  215.5 2.8 fusion.21
  218.4 3.2 add_convert_fusion.1
  226.6 3.9 convolution_convert_fusion.2
  230.5 4.1 convolution_convert_fusion.3
  234.6 5.2 convolution_convert_fusion
  239.8 5.3 %convolution_convert_fusion.1 = bf16[1536,768]{1,0:T(8,128)(2,1)} fusion(bf16[1024,3072]{1,0:T(8,128)(2,1)S(1)} %bitcast.77, s32[]{:T(128)S(6)} %select_n.376, bf16[256,768]{0,1:T(8,128)(2,1)} %collective-permute-done.8, bf16[256,768]{0,1:T(8,128)(2,1)} %collective-permute-done.7, bf16[256,768]{0,1:T(8,128)(2,1)S(1)} %copy-done.32, ...), kind=kOutput, calls=%fused_computation.34 | convolution fusion | flops 2423390208 | bytes 7077892 | tf_op jit(solution)/shard_map/dot_general | solution.py:230
  259.0 3.0 collective-permute-start.16
  278.0 4.8 collective-permute-done.4
  311.0 3.3 collective-permute-done.18
  316.2 4.5 collective-permute-done.38
  321.6 5.4 %collective-permute-done.48 = bf16[384,384]{1,0:T(8,128)(2,1)S(1)} collective-permute-done((bf16[384,384]{1,0:T(8,128)(2,1)S(1)}, bf16[384,384]{1,0:T(8,128)(2,1)S(1)}, u32[]{:S(2)}, u32[]{:S(2)}) %collective-permute-start.48) | collective-permute-done | bytes 294944 | tf_op jit(solution)/shard_map/ppermute | solution.py:376
  347.3 2.4 collective-permute-start.42
  355.1 2.2 add_convert_fusion.7
  357.4 2.2 collective-permute-start.58
  364.0 19.3 %collective-permute-done.58 = bf16[384,1536]{1,0:T(8,128)(2,1)S(1)} collective-permute-done((bf16[384,1536]{1,0:T(8,128)(2,1)S(1)}, bf16[384,1536]{1,0:T(8,128)(2,1)S(1)}, u32[]{:S(2)}, u32[]{:S(2)}) %collective-permute-start.58) | collective-permute-done | bytes 1179680 | tf_op jit(solution)/shard_map/ppermute | solution.py:376
  385.8 2.5 collective-permute-done.68
  389.6 9.8 %collective-permute-done.59 = bf16[192,1536]{1,0:T(8,128)(2,1)S(1)} collective-permute-done((bf16[192,1536]{1,0:T(8,128)(2,1)S(1)}, bf16[192,1536]{1,0:T(8,128)(2,1)S(1)}, u32[]{:S(2)}, u32[]{:S(2)}) %collective-permute-start.59) | collective-permute-done | bytes 589856 | tf_op jit(solution)/shard_map/ppermute | solution.py:376
  403.2 8.2 %collective-permute-done.60 = bf16[96,1536]{1,0:T(8,128)(2,1)S(1)} collective-permute-done((bf16[96,1536]{1,0:T(8,128)(2,1)S(1)}, bf16[96,1536]{1,0:T(8,128)(2,1)S(1)}, u32[]{:S(2)}, u32[]{:S(2)}) %collective-permute-start.60) | collective-permute-done | bytes 294944 | tf_op jit(solution)/shard_map/ppermute | solution.py:376
  413.5 6.8 %collective-permute-done.61 = bf16[48,1536]{1,0:T(8,128)(2,1)S(1)} collective-permute-done((bf16[48,1536]{1,0:T(8,128)(2,1)S(1)}, bf16[48,1536]{1,0:T(8,128)(2,1)S(1)}, u32[]{:S(2)}, u32[]{:S(2)}) %collective-permute-start.61) | collective-permute-done | bytes 147488 | tf_op jit(solution)/shard_map/ppermute | solution.py:376
  420.4 3.1 collective-permute-start.62
  423.5 7.3 %collective-permute-done.70 = bf16[192,768]{1,0:T(8,128)(2,1)S(1)} collective-permute-done((bf16[192,768]{1,0:T(8,128)(2,1)S(1)}, bf16[192,768]{1,0:T(8,128)(2,1)S(1)}, u32[]{:S(2)}, u32[]{:S(2)}) %collective-permute-start.70) | collective-permute-done | bytes 294944 | tf_op jit(solution)/shard_map/ppermute | solution.py:376
  432.5 7.1 %collective-permute-done.71 = bf16[96,768]{1,0:T(8,128)(2,1)S(1)} collective-permute-done((bf16[96,768]{1,0:T(8,128)(2,1)S(1)}, bf16[96,768]{1,0:T(8,128)(2,1)S(1)}, u32[]{:S(2)}, u32[]{:S(2)}) %collective-permute-start.71) | collective-permute-done | bytes 147488 | tf_op jit(solution)/shard_map/ppermute | solution.py:376
  439.8 7.6 %collective-permute-done.63 = bf16[96,1536]{1,0:T(8,128)(2,1)S(1)} collective-permute-done((bf16[96,1536]{1,0:T(8,128)(2,1)S(1)}, bf16[96,1536]{1,0:T(8,128)(2,1)S(1)}, u32[]{:S(2)}, u32[]{:S(2)}) %collective-permute-start.63) | collective-permute-done | bytes 294944 | tf_op jit(solution)/shard_map/ppermute | solution.py:376
  449.2 5.6 %collective-permute-done.72 = bf16[96,768]{1,0:T(8,128)(2,1)S(1)} collective-permute-done((bf16[96,768]{1,0:T(8,128)(2,1)S(1)}, bf16[96,768]{1,0:T(8,128)(2,1)S(1)}, u32[]{:S(2)}, u32[]{:S(2)}) %collective-permute-start.72) | collective-permute-done | bytes 147488 | tf_op jit(solution)/shard_map/ppermute | solution.py:376
  455.0 2.6 collective-permute-done.64
  462.8 23.8 %collective-permute-done.74 = bf16[384,768]{1,0:T(8,128)(2,1)S(1)} collective-permute-done((bf16[384,768]{1,0:T(8,128)(2,1)S(1)}, bf16[384,768]{1,0:T(8,128)(2,1)S(1)}, u32[]{:S(2)}, u32[]{:S(2)}) %collective-permute-start.74) | collective-permute-done | bytes 589856 | tf_op jit(solution)/shard_map/ppermute | solution.py:376
  489.7 25.4 %collective-permute-done.75 = bf16[768,768]{1,0:T(8,128)(2,1)S(1)} collective-permute-done((bf16[768,768]{1,0:T(8,128)(2,1)S(1)}, bf16[768,768]{1,0:T(8,128)(2,1)S(1)}, u32[]{:S(2)}, u32[]{:S(2)}) %collective-permute-start.75) | collective-permute-done | bytes 1179680 | tf_op jit(solution)/shard_map/ppermute | solution.py:376
  516.2 3.5 concatenate.47
  522.0 5.0 maximum_convert_fusion
  527.3 4.5 maximum_convert_fusion.1
  (486 shorter events, 164.1 us)
Async XLA Ops:
  6.3 24.4 %collective-permute-start.2 = (bf16[256,768]{0,1:T(8,128)(2,1)}, bf16[256,768]{0,1:T(8,128)(2,1)}, u32[]{:S(2)}, u32[]{:S(2)}) collective-permute-start(bf16[256,768]{0,1:T(8,128)(2,1)} %bitcast.65), channel_id=1, source_target_pairs={{0,3},{1,2},{2,1},{3,0},{4,7},{5,6},{6,5},{7,4},{8,11},{9,10},{10,... | collective-permute-start | bytes 1179656 | tf_op jit(solution)/shard_map/ppermute | solution.py:376
  12.1 18.8 %collective-permute-start.1 = (bf16[256,768]{0,1:T(8,128)(2,1)}, bf16[256,768]{0,1:T(8,128)(2,1)}, u32[]{:S(2)}, u32[]{:S(2)}) collective-permute-start(bf16[256,768]{0,1:T(8,128)(2,1)} %bitcast.64), channel_id=1, source_target_pairs={{0,2},{1,3},{2,0},{3,1},{4,6},{5,7},{6,4},{7,5},{8,10},{9,11},{10,... | collective-permute-start | bytes 1179656 | tf_op jit(solution)/shard_map/ppermute | solution.py:376
  14.5 16.3 %collective-permute-start = (bf16[256,768]{0,1:T(8,128)(2,1)}, bf16[256,768]{0,1:T(8,128)(2,1)}, u32[]{:S(2)}, u32[]{:S(2)}) collective-permute-start(bf16[256,768]{0,1:T(8,128)(2,1)} %bitcast.66), channel_id=1, source_target_pairs={{0,1},{1,0},{2,3},{3,2},{4,5},{5,4},{6,7},{7,6},{8,9},{9,8},{10,11... | collective-permute-start | bytes 1179656 | tf_op jit(solution)/shard_map/ppermute | solution.py:376
  16.5 72.9 %collective-permute-start.8 = (bf16[256,768]{0,1:T(8,128)(2,1)}, bf16[256,768]{0,1:T(8,128)(2,1)}, u32[]{:S(2)}, u32[]{:S(2)}) collective-permute-start(bf16[256,768]{0,1:T(8,128)(2,1)} %bitcast.62), channel_id=1, source_target_pairs={{0,3},{1,2},{2,1},{3,0},{4,7},{5,6},{6,5},{7,4},{8,11},{9,10},{10,... | collective-permute-start | bytes 1179656 | tf_op jit(solution)/shard_map/ppermute | solution.py:376
  21.3 68.1 %collective-permute-start.7 = (bf16[256,768]{0,1:T(8,128)(2,1)}, bf16[256,768]{0,1:T(8,128)(2,1)}, u32[]{:S(2)}, u32[]{:S(2)}) collective-permute-start(bf16[256,768]{0,1:T(8,128)(2,1)} %bitcast.63), channel_id=1, source_target_pairs={{0,2},{1,3},{2,0},{3,1},{4,6},{5,7},{6,4},{7,5},{8,10},{9,11},{10,... | collective-permute-start | bytes 1179656 | tf_op jit(solution)/shard_map/ppermute | solution.py:376
  30.7 58.7 %collective-permute-start.6 = (bf16[256,768]{0,1:T(8,128)(2,1)}, bf16[256,768]{0,1:T(8,128)(2,1)S(1)}, u32[]{:S(2)}, u32[]{:S(2)}) collective-permute-start(bf16[256,768]{0,1:T(8,128)(2,1)} %bitcast.67), channel_id=1, source_target_pairs={{0,1},{1,0},{2,3},{3,2},{4,5},{5,4},{6,7},{7,6},{8,9},{9,8},{10,11... | collective-permute-start | bytes 1179656 | tf_op jit(solution)/shard_map/ppermute | solution.py:376
  194.3 71.6 %collective-permute-start.3 = (bf16[256,768]{0,1:T(8,128)(2,1)}, bf16[256,768]{0,1:T(8,128)(2,1)}, u32[]{:S(2)}, u32[]{:S(2)}) collective-permute-start(bf16[256,768]{0,1:T(8,128)(2,1)} %get-tuple-element.67), channel_id=1, source_target_pairs={{0,1},{1,0},{2,3},{3,2},{4,5},{5,4},{6,7},{7,6},{8,9},{9,8},{10,11... | collective-permute-start | bytes 1179656 | tf_op jit(solution)/shard_map/ppermute | solution.py:376
  196.3 88.6 %collective-permute-start.5 = (bf16[256,768]{0,1:T(8,128)(2,1)}, bf16[256,768]{0,1:T(8,128)(2,1)}, u32[]{:S(2)}, u32[]{:S(2)}) collective-permute-start(bf16[256,768]{0,1:T(8,128)(2,1)} %get-tuple-element.65), channel_id=1, source_target_pairs={{0,3},{1,2},{2,1},{3,0},{4,7},{5,6},{6,5},{7,4},{8,11},{9,10},{10,... | collective-permute-start | bytes 1179656 | tf_op jit(solution)/shard_map/ppermute | solution.py:376
  222.9 64.3 %collective-permute-start.9 = (bf16[256,768]{0,1:T(8,128)(2,1)}, bf16[256,768]{0,1:T(8,128)(2,1)}, u32[]{:S(2)}, u32[]{:S(2)}) collective-permute-start(bf16[256,768]{0,1:T(8,128)(2,1)} %get-tuple-element.59), channel_id=1, source_target_pairs={{0,1},{1,0},{2,3},{3,2},{4,5},{5,4},{6,7},{7,6},{8,9},{9,8},{10,11... | collective-permute-start | bytes 1179656 | tf_op jit(solution)/shard_map/ppermute | solution.py:376
  224.6 22.3 %collective-permute-start.12 = (f32[9216]{0:T(1024)S(1)}, f32[9216]{0:T(1024)S(1)}, u32[]{:S(2)}, u32[]{:S(2)}) collective-permute-start(f32[9216]{0:T(1024)S(1)} %constant_dynamic-update-slice_fusion.59), channel_id=1, source_target_pairs={{0,4},{4,0},{8,12},{12,8},{16,20},{20,16},{24,28},{28,24},{1,5},{5... | collective-permute-start | bytes 110600 | tf_op jit(solution)/shard_map/ppermute | solution.py:376
  263.9 19.0 %collective-permute-start.4 = (bf16[256,768]{0,1:T(8,128)(2,1)}, bf16[256,768]{0,1:T(8,128)(2,1)}, u32[]{:S(2)}, u32[]{:S(2)}) collective-permute-start(bf16[256,768]{0,1:T(8,128)(2,1)} %get-tuple-element.66), channel_id=1, source_target_pairs={{0,2},{1,3},{2,0},{3,1},{4,6},{5,7},{6,4},{7,5},{8,10},{9,11},{10,... | collective-permute-start | bytes 1179656 | tf_op jit(solution)/shard_map/ppermute | solution.py:376
  264.2 25.0 %collective-permute-start.10 = (bf16[256,768]{0,1:T(8,128)(2,1)}, bf16[256,768]{0,1:T(8,128)(2,1)}, u32[]{:S(2)}, u32[]{:S(2)}) collective-permute-start(bf16[256,768]{0,1:T(8,128)(2,1)} %get-tuple-element.58), channel_id=1, source_target_pairs={{0,2},{1,3},{2,0},{3,1},{4,6},{5,7},{6,4},{7,5},{8,10},{9,11},{10,... | collective-permute-start | bytes 1179656 | tf_op jit(solution)/shard_map/ppermute | solution.py:376
  265.9 25.7 %collective-permute-start.11 = (bf16[256,768]{0,1:T(8,128)(2,1)}, bf16[256,768]{0,1:T(8,128)(2,1)}, u32[]{:S(2)}, u32[]{:S(2)}) collective-permute-start(bf16[256,768]{0,1:T(8,128)(2,1)} %get-tuple-element.57), channel_id=1, source_target_pairs={{0,3},{1,2},{2,1},{3,0},{4,7},{5,6},{6,5},{7,4},{8,11},{9,10},{10,... | collective-permute-start | bytes 1179656 | tf_op jit(solution)/shard_map/ppermute | solution.py:376
  282.9 19.6 %collective-permute-start.17 = (bf16[768,384]{1,0:T(8,128)(2,1)}, bf16[768,384]{1,0:T(8,128)(2,1)}, u32[]{:S(2)}, u32[]{:S(2)}) collective-permute-start(bf16[768,384]{1,0:T(8,128)(2,1)} %convolution_convert_fusion.11), channel_id=1, source_target_pairs={{0,4},{4,0},{8,12},{12,8},{16,20},{20,16},{24,28},{28,24},{1,5},{5... | collective-permute-start | bytes 1769480 | tf_op jit(solution)/shard_map/ppermute | solution.py:376
  284.8 19.6 %collective-permute-start.27 = (bf16[768,384]{1,0:T(8,128)(2,1)}, bf16[768,384]{1,0:T(8,128)(2,1)}, u32[]{:S(2)}, u32[]{:S(2)}) collective-permute-start(bf16[768,384]{1,0:T(8,128)(2,1)} %convolution_convert_fusion.9), channel_id=1, source_target_pairs={{0,4},{4,0},{8,12},{12,8},{16,20},{20,16},{24,28},{28,24},{1,5},{5... | collective-permute-start | bytes 1769480 | tf_op jit(solution)/shard_map/ppermute | solution.py:376
  287.2 19.3 %collective-permute-start.37 = (bf16[768,384]{1,0:T(8,128)(2,1)}, bf16[768,384]{1,0:T(8,128)(2,1)}, u32[]{:S(2)}, u32[]{:S(2)}) collective-permute-start(bf16[768,384]{1,0:T(8,128)(2,1)} %convolution_convert_fusion.7), channel_id=1, source_target_pairs={{0,4},{4,0},{8,12},{12,8},{16,20},{20,16},{24,28},{28,24},{1,5},{5... | collective-permute-start | bytes 1769480 | tf_op jit(solution)/shard_map/ppermute | solution.py:376
  289.2 19.4 %collective-permute-start.47 = (bf16[768,384]{1,0:T(8,128)(2,1)}, bf16[768,384]{1,0:T(8,128)(2,1)}, u32[]{:S(2)}, u32[]{:S(2)}) collective-permute-start(bf16[768,384]{1,0:T(8,128)(2,1)} %convolution_convert_fusion.5), channel_id=1, source_target_pairs={{0,4},{4,0},{8,12},{12,8},{16,20},{20,16},{24,28},{28,24},{1,5},{5... | collective-permute-start | bytes 1769480 | tf_op jit(solution)/shard_map/ppermute | solution.py:376
  291.6 62.7 %collective-permute-start.57 = (bf16[768,1536]{1,0:T(8,128)(2,1)}, bf16[768,1536]{1,0:T(8,128)(2,1)}, u32[]{:S(2)}, u32[]{:S(2)}) collective-permute-start(bf16[768,1536]{1,0:T(8,128)(2,1)} %convolution_convert_fusion.2), channel_id=1, source_target_pairs={{0,4},{4,0},{8,12},{12,8},{16,20},{20,16},{24,28},{28,24},{1,5},{5... | collective-permute-start | bytes 7077896 | tf_op jit(solution)/shard_map/ppermute | solution.py:376
  302.5 57.4 %collective-permute-start.67 = (bf16[1536,768]{1,0:T(8,128)(2,1)S(1)}, bf16[1536,768]{1,0:T(8,128)(2,1)S(1)}, u32[]{:S(2)}, u32[]{:S(2)}) collective-permute-start(bf16[1536,768]{1,0:T(8,128)(2,1)S(1)} %copy-done.69), channel_id=1, source_target_pairs={{0,4},{4,0},{8,12},{12,8},{16,20},{20,16},{24,28},{28,24},{1,5},{5... | collective-permute-start | bytes 7077896 | tf_op jit(solution)/shard_map/ppermute | solution.py:376
  308.6 12.1 %collective-permute-start.38 = (bf16[384,384]{1,0:T(8,128)(2,1)S(1)}, bf16[384,384]{1,0:T(8,128)(2,1)S(1)}, u32[]{:S(2)}, u32[]{:S(2)}) collective-permute-start(bf16[384,384]{1,0:T(8,128)(2,1)S(1)} %get-tuple-element.82), channel_id=1, source_target_pairs={{0,1},{1,0},{2,3},{3,2},{4,5},{5,4},{6,7},{7,6},{8,9},{9,8},{10,11... | collective-permute-start | bytes 884744 | tf_op jit(solution)/shard_map/ppermute | solution.py:376
  314.3 12.6 %collective-permute-start.48 = (bf16[384,384]{1,0:T(8,128)(2,1)S(1)}, bf16[384,384]{1,0:T(8,128)(2,1)S(1)}, u32[]{:S(2)}, u32[]{:S(2)}) collective-permute-start(bf16[384,384]{1,0:T(8,128)(2,1)S(1)} %get-tuple-element.80), channel_id=1, source_target_pairs={{0,1},{1,0},{2,3},{3,2},{4,5},{5,4},{6,7},{7,6},{8,9},{9,8},{10,11... | collective-permute-start | bytes 884744 | tf_op jit(solution)/shard_map/ppermute | solution.py:376
  315.3 12.5 %collective-permute-start.19 = (bf16[192,384]{1,0:T(8,128)(2,1)S(1)}, bf16[192,384]{1,0:T(8,128)(2,1)S(1)}, u32[]{:S(2)}, u32[]{:S(2)}) collective-permute-start(bf16[192,384]{1,0:T(8,128)(2,1)S(1)} %get-tuple-element.94), channel_id=1, source_target_pairs={{0,2},{1,3},{2,0},{3,1},{4,6},{5,7},{6,4},{7,5},{8,10},{9,11},{10,... | collective-permute-start | bytes 442376 | tf_op jit(solution)/shard_map/ppermute | solution.py:376
  357.4 25.9 %collective-permute-start.58 = (bf16[384,1536]{1,0:T(8,128)(2,1)S(1)}, bf16[384,1536]{1,0:T(8,128)(2,1)S(1)}, u32[]{:S(2)}, u32[]{:S(2)}) collective-permute-start(bf16[384,1536]{1,0:T(8,128)(2,1)S(1)} %get-tuple-element.51), channel_id=1, source_target_pairs={{0,2},{1,3},{2,0},{3,1},{4,6},{5,7},{6,4},{7,5},{8,10},{9,11},{10,... | collective-permute-start | bytes 3538952 | tf_op jit(solution)/shard_map/ppermute | solution.py:376
  359.8 24.8 %collective-permute-start.53 = (bf16[96,384]{1,0:T(8,128)(2,1)S(1)}, bf16[96,384]{1,0:T(8,128)(2,1)S(1)}, u32[]{:S(2)}, u32[]{:S(2)}) collective-permute-start(bf16[96,384]{1,0:T(8,128)(2,1)S(1)} %constant_dynamic-update-slice_fusion.15), channel_id=1, source_target_pairs={{0,8},{4,12},{8,0},{12,4},{16,24},{20,28},{24,16},{28,20},{1,9},{5... | collective-permute-start | bytes 221192 | tf_op jit(solution)/shard_map/ppermute | solution.py:376
  360.8 27.5 %collective-permute-start.68 = (bf16[768,768]{1,0:T(8,128)(2,1)S(1)}, bf16[768,768]{1,0:T(8,128)(2,1)S(1)}, u32[]{:S(2)}, u32[]{:S(2)}) collective-permute-start(bf16[768,768]{1,0:T(8,128)(2,1)S(1)} %get-tuple-element.47), channel_id=1, source_target_pairs={{0,1},{1,0},{2,3},{3,2},{4,5},{5,4},{6,7},{7,6},{8,9},{9,8},{10,11... | collective-permute-start | bytes 3538952 | tf_op jit(solution)/shard_map/ppermute | solution.py:376
  361.8 38.7 %collective-permute-start.24 = (bf16[192,384]{1,0:T(8,128)(2,1)S(1)}, bf16[192,384]{1,0:T(8,128)(2,1)S(1)}, u32[]{:S(2)}, u32[]{:S(2)}) collective-permute-start(bf16[192,384]{1,0:T(8,128)(2,1)S(1)} %constant_dynamic-update-slice_fusion.41), channel_id=1, source_target_pairs={{0,2},{1,3},{2,0},{3,1},{4,6},{5,7},{6,4},{7,5},{8,10},{9,11},{10,... | collective-permute-start | bytes 442376 | tf_op jit(solution)/shard_map/ppermute | solution.py:376
  362.6 39.5 %collective-permute-start.34 = (bf16[192,384]{1,0:T(8,128)(2,1)S(1)}, bf16[192,384]{1,0:T(8,128)(2,1)S(1)}, u32[]{:S(2)}, u32[]{:S(2)}) collective-permute-start(bf16[192,384]{1,0:T(8,128)(2,1)S(1)} %constant_dynamic-update-slice_fusion.30), channel_id=1, source_target_pairs={{0,1},{1,0},{2,3},{3,2},{4,5},{5,4},{6,7},{7,6},{8,9},{9,8},{10,11... | collective-permute-start | bytes 442376 | tf_op jit(solution)/shard_map/ppermute | solution.py:376
  383.3 37.2 %collective-permute-start.44 = (bf16[192,384]{1,0:T(8,128)(2,1)S(1)}, bf16[192,384]{1,0:T(8,128)(2,1)S(1)}, u32[]{:S(2)}, u32[]{:S(2)}) collective-permute-start(bf16[192,384]{1,0:T(8,128)(2,1)S(1)} %constant_dynamic-update-slice_fusion.22), channel_id=1, source_target_pairs={{0,2},{1,3},{2,0},{3,1},{4,6},{5,7},{6,4},{7,5},{8,10},{9,11},{10,... | collective-permute-start | bytes 442376 | tf_op jit(solution)/shard_map/ppermute | solution.py:376
  384.7 14.7 %collective-permute-start.59 = (bf16[192,1536]{1,0:T(8,128)(2,1)S(1)}, bf16[192,1536]{1,0:T(8,128)(2,1)S(1)}, u32[]{:S(2)}, u32[]{:S(2)}) collective-permute-start(bf16[192,1536]{1,0:T(8,128)(2,1)S(1)} %get-tuple-element.55), channel_id=1, source_target_pairs={{0,1},{1,0},{2,3},{3,2},{4,5},{5,4},{6,7},{7,6},{8,9},{9,8},{10,11... | collective-permute-start | bytes 1769480 | tf_op jit(solution)/shard_map/ppermute | solution.py:376
  388.3 59.4 %collective-permute-start.54 = (bf16[192,384]{1,0:T(8,128)(2,1)S(1)}, bf16[192,384]{1,0:T(8,128)(2,1)S(1)}, u32[]{:S(2)}, u32[]{:S(2)}) collective-permute-start(bf16[192,384]{1,0:T(8,128)(2,1)S(1)} %constant_dynamic-update-slice_fusion.13), channel_id=1, source_target_pairs={{0,2},{1,3},{2,0},{3,1},{4,6},{5,7},{6,4},{7,5},{8,10},{9,11},{10,... | collective-permute-start | bytes 442376 | tf_op jit(solution)/shard_map/ppermute | solution.py:376
  399.4 12.8 %collective-permute-start.69 = (bf16[384,768]{1,0:T(8,128)(2,1)S(1)}, bf16[384,768]{1,0:T(8,128)(2,1)S(1)}, u32[]{:S(2)}, u32[]{:S(2)}) collective-permute-start(bf16[384,768]{1,0:T(8,128)(2,1)S(1)} %get-tuple-element.53), channel_id=1, source_target_pairs={{0,2},{1,3},{2,0},{3,1},{4,6},{5,7},{6,4},{7,5},{8,10},{9,11},{10,... | collective-permute-start | bytes 1769480 | tf_op jit(solution)/shard_map/ppermute | solution.py:376
  400.5 10.9 %collective-permute-start.60 = (bf16[96,1536]{1,0:T(8,128)(2,1)S(1)}, bf16[96,1536]{1,0:T(8,128)(2,1)S(1)}, u32[]{:S(2)}, u32[]{:S(2)}) collective-permute-start(bf16[96,1536]{1,0:T(8,128)(2,1)S(1)} %get-tuple-element.76), channel_id=1, source_target_pairs={{0,8},{4,12},{8,0},{12,4},{16,24},{20,28},{24,16},{28,20},{1,9},{5... | collective-permute-start | bytes 884744 | tf_op jit(solution)/shard_map/ppermute | solution.py:376
  402.1 55.7 %collective-permute-start.25 = (bf16[384,384]{1,0:T(8,128)(2,1)S(1)}, bf16[384,384]{1,0:T(8,128)(2,1)S(1)}, u32[]{:S(2)}, u32[]{:S(2)}) collective-permute-start(bf16[384,384]{1,0:T(8,128)(2,1)S(1)} %constant_dynamic-update-slice_fusion.39), channel_id=1, source_target_pairs={{0,1},{1,0},{2,3},{3,2},{4,5},{5,4},{6,7},{7,6},{8,9},{9,8},{10,11... | collective-permute-start | bytes 884744 | tf_op jit(solution)/shard_map/ppermute | solution.py:376
  412.2 49.5 %collective-permute-start.35 = (bf16[384,384]{1,0:T(8,128)(2,1)S(1)}, bf16[384,384]{1,0:T(8,128)(2,1)S(1)}, u32[]{:S(2)}, u32[]{:S(2)}) collective-permute-start(bf16[384,384]{1,0:T(8,128)(2,1)S(1)} %constant_dynamic-update-slice_fusion.28), channel_id=1, source_target_pairs={{0,2},{1,3},{2,0},{3,1},{4,6},{5,7},{6,4},{7,5},{8,10},{9,11},{10,... | collective-permute-start | bytes 884744 | tf_op jit(solution)/shard_map/ppermute | solution.py:376
  420.3 10.5 %collective-permute-start.70 = (bf16[192,768]{1,0:T(8,128)(2,1)S(1)}, bf16[192,768]{1,0:T(8,128)(2,1)S(1)}, u32[]{:S(2)}, u32[]{:S(2)}) collective-permute-start(bf16[192,768]{1,0:T(8,128)(2,1)S(1)} %get-tuple-element.74), channel_id=1, source_target_pairs={{0,8},{4,12},{8,0},{12,4},{16,24},{20,28},{24,16},{28,20},{1,9},{5... | collective-permute-start | bytes 884744 | tf_op jit(solution)/shard_map/ppermute | solution.py:376
  420.4 11.7 %collective-permute-start.62 = (bf16[48,1536]{1,0:T(8,128)(2,1)S(1)}, bf16[48,1536]{1,0:T(8,128)(2,1)S(1)}, u32[]{:S(2)}, u32[]{:S(2)}) collective-permute-start(bf16[48,1536]{1,0:T(8,128)(2,1)S(1)} %get-tuple-element.31), channel_id=1, source_target_pairs={{0,16},{4,20},{8,24},{12,28},{16,0},{20,4},{24,8},{28,12},{1,17},{... | collective-permute-start | bytes 442376 | tf_op jit(solution)/shard_map/ppermute | solution.py:376
  430.8 31.0 %collective-permute-start.45 = (bf16[384,384]{1,0:T(8,128)(2,1)S(1)}, bf16[384,384]{1,0:T(8,128)(2,1)S(1)}, u32[]{:S(2)}, u32[]{:S(2)}) collective-permute-start(bf16[384,384]{1,0:T(8,128)(2,1)S(1)} %constant_dynamic-update-slice_fusion.20), channel_id=1, source_target_pairs={{0,1},{1,0},{2,3},{3,2},{4,5},{5,4},{6,7},{7,6},{8,9},{9,8},{10,11... | collective-permute-start | bytes 884744 | tf_op jit(solution)/shard_map/ppermute | solution.py:376
  447.7 9.9 %collective-permute-start.64 = (bf16[192,1536]{1,0:T(8,128)(2,1)S(1)}, bf16[192,1536]{1,0:T(8,128)(2,1)S(1)}, u32[]{:S(2)}, u32[]{:S(2)}) collective-permute-start(bf16[192,1536]{1,0:T(8,128)(2,1)S(1)} %constant_dynamic-update-slice_fusion), channel_id=1, source_target_pairs={{0,1},{1,0},{2,3},{3,2},{4,5},{5,4},{6,7},{7,6},{8,9},{9,8},{10,11... | collective-permute-start | bytes 1769480 | tf_op jit(solution)/shard_map/ppermute | solution.py:376
  457.7 29.0 %collective-permute-start.65 = (bf16[384,1536]{1,0:T(8,128)(2,1)S(1)}, bf16[384,1536]{1,0:T(8,128)(2,1)S(1)}, u32[]{:S(2)}, u32[]{:S(2)}) collective-permute-start(bf16[384,1536]{1,0:T(8,128)(2,1)S(1)} %constant_dynamic-update-slice_fusion.45), channel_id=1, source_target_pairs={{0,2},{1,3},{2,0},{3,1},{4,6},{5,7},{6,4},{7,5},{8,10},{9,11},{10,... | collective-permute-start | bytes 3538952 | tf_op jit(solution)/shard_map/ppermute | solution.py:376
  457.9 30.2 %collective-permute-start.55 = (bf16[384,384]{1,0:T(8,128)(2,1)S(1)}, bf16[384,384]{1,0:T(8,128)(2,1)S(1)}, u32[]{:S(2)}, u32[]{:S(2)}) collective-permute-start(bf16[384,384]{1,0:T(8,128)(2,1)S(1)} %constant_dynamic-update-slice_fusion.11), channel_id=1, source_target_pairs={{0,1},{1,0},{2,3},{3,2},{4,5},{5,4},{6,7},{7,6},{8,9},{9,8},{10,11... | collective-permute-start | bytes 884744 | tf_op jit(solution)/shard_map/ppermute | solution.py:376
  461.6 26.8 %collective-permute-start.26 = (bf16[768,384]{1,0:T(8,128)(2,1)S(1)}, bf16[768,384]{1,0:T(8,128)(2,1)S(1)}, u32[]{:S(2)}, u32[]{:S(2)}) collective-permute-start(bf16[768,384]{1,0:T(8,128)(2,1)S(1)} %constant_dynamic-update-slice_fusion.37), channel_id=1, source_target_pairs={{0,4},{4,0},{8,12},{12,8},{16,20},{20,16},{24,28},{28,24},{1,5},{5... | collective-permute-start | bytes 1769480 | tf_op jit(solution)/shard_map/ppermute | solution.py:376
  461.6 24.9 %collective-permute-start.74 = (bf16[384,768]{1,0:T(8,128)(2,1)S(1)}, bf16[384,768]{1,0:T(8,128)(2,1)S(1)}, u32[]{:S(2)}, u32[]{:S(2)}) collective-permute-start(bf16[384,768]{1,0:T(8,128)(2,1)S(1)} %constant_dynamic-update-slice_fusion.36), channel_id=1, source_target_pairs={{0,2},{1,3},{2,0},{3,1},{4,6},{5,7},{6,4},{7,5},{8,10},{9,11},{10,... | collective-permute-start | bytes 1769480 | tf_op jit(solution)/shard_map/ppermute | solution.py:376
  461.8 27.4 %collective-permute-start.36 = (bf16[768,384]{1,0:T(8,128)(2,1)S(1)}, bf16[768,384]{1,0:T(8,128)(2,1)S(1)}, u32[]{:S(2)}, u32[]{:S(2)}) collective-permute-start(bf16[768,384]{1,0:T(8,128)(2,1)S(1)} %constant_dynamic-update-slice_fusion.26), channel_id=1, source_target_pairs={{0,4},{4,0},{8,12},{12,8},{16,20},{20,16},{24,28},{28,24},{1,5},{5... | collective-permute-start | bytes 1769480 | tf_op jit(solution)/shard_map/ppermute | solution.py:376
  486.6 28.9 %collective-permute-start.46 = (bf16[768,384]{1,0:T(8,128)(2,1)S(1)}, bf16[768,384]{1,0:T(8,128)(2,1)S(1)}, u32[]{:S(2)}, u32[]{:S(2)}) collective-permute-start(bf16[768,384]{1,0:T(8,128)(2,1)S(1)} %constant_dynamic-update-slice_fusion.18), channel_id=1, source_target_pairs={{0,4},{4,0},{8,12},{12,8},{16,20},{20,16},{24,28},{28,24},{1,5},{5... | collective-permute-start | bytes 1769480 | tf_op jit(solution)/shard_map/ppermute | solution.py:376
  486.7 28.4 %collective-permute-start.75 = (bf16[768,768]{1,0:T(8,128)(2,1)S(1)}, bf16[768,768]{1,0:T(8,128)(2,1)S(1)}, u32[]{:S(2)}, u32[]{:S(2)}) collective-permute-start(bf16[768,768]{1,0:T(8,128)(2,1)S(1)} %constant_dynamic-update-slice_fusion.6), channel_id=1, source_target_pairs={{0,1},{1,0},{2,3},{3,2},{4,5},{5,4},{6,7},{7,6},{8,9},{9,8},{10,11... | collective-permute-start | bytes 3538952 | tf_op jit(solution)/shard_map/ppermute | solution.py:376
  488.1 33.3 %collective-permute-start.66 = (bf16[768,1536]{1,0:T(8,128)(2,1)S(1)}, bf16[768,1536]{1,0:T(8,128)(2,1)S(1)}, u32[]{:S(2)}, u32[]{:S(2)}) collective-permute-start(bf16[768,1536]{1,0:T(8,128)(2,1)S(1)} %constant_dynamic-update-slice_fusion.34), channel_id=1, source_target_pairs={{0,4},{4,0},{8,12},{12,8},{16,20},{20,16},{24,28},{28,24},{1,5},{5... | collective-permute-start | bytes 7077896 | tf_op jit(solution)/shard_map/ppermute | solution.py:376
  488.4 31.2 %collective-permute-start.56 = (bf16[768,384]{1,0:T(8,128)(2,1)S(1)}, bf16[768,384]{1,0:T(8,128)(2,1)S(1)}, u32[]{:S(2)}, u32[]{:S(2)}) collective-permute-start(bf16[768,384]{1,0:T(8,128)(2,1)S(1)} %constant_dynamic-update-slice_fusion.9), channel_id=1, source_target_pairs={{0,4},{4,0},{8,12},{12,8},{16,20},{20,16},{24,28},{28,24},{1,5},{5... | collective-permute-start | bytes 1769480 | tf_op jit(solution)/shard_map/ppermute | solution.py:376
  515.2 11.8 %collective-permute-start.76 = (bf16[1536,768]{1,0:T(8,128)(2,1)S(1)}, bf16[1536,768]{1,0:T(8,128)(2,1)S(1)}, u32[]{:S(2)}, u32[]{:S(2)}) collective-permute-start(bf16[1536,768]{1,0:T(8,128)(2,1)S(1)} %constant_dynamic-update-slice_fusion.5), channel_id=1, source_target_pairs={{0,4},{4,0},{8,12},{12,8},{16,20},{20,16},{24,28},{28,24},{1,5},{5... | collective-permute-start | bytes 7077896 | tf_op jit(solution)/shard_map/ppermute | solution.py:376
  (110 other events, 893.6 us)

commit v2 on v0

--- a/solution.py
+++ b/solution.py
@@ -1,6 +1,10 @@
+import functools
+
 import jax
 import jax.numpy as jnp
 from jax import lax
+from jax.experimental import pallas as pl
+from jax.experimental.pallas import tpu as pltpu
 from jax.sharding import PartitionSpec as P
 
 HEADS = 12
@@ -31,7 +35,7 @@
     return jnp.einsum(pattern, first_op, second_op, preferred_element_type=jnp.float32)
 
 
-def shards(
+def general_shards(
     tokens,
     image_lengths,
     cotangent,
@@ -209,6 +213,1075 @@
     )
     return (jnp.stack(outputs_list), jnp.stack(grads_list)) + tuple(summed)
 
+F32 = jnp.float32
+BF = jnp.bfloat16
+BIG = 1e30
+MESH = pl.DeviceIdType.MESH
+VMEM_GRANT = 60 * 2**20
+ANY = pl.BlockSpec(memory_space=pl.ANY)
+
+
+def dot_rows(first_op, second_op):
+    return lax.dot_general(first_op, second_op, (((1,), (1,)), ((), ())), preferred_element_type=F32)
+
+
+def dot_plain(first_op, second_op):
+    return lax.dot_general(first_op, second_op, (((1,), (0,)), ((), ())), preferred_element_type=F32)
+
+
+def dot_tokens(first_op, second_op):
+    return lax.dot_general(first_op, second_op, (((0,), (0,)), ((), ())), preferred_element_type=F32)
+
+
+def once(shape, index=None):
+    place = index if index is not None else (lambda *_: (0,) * len(shape))
+    return pl.BlockSpec(shape, place, pipeline_mode=pl.Buffered(1))
+
+
+def total_rows(array):
+    return jnp.sum(array, axis=0, keepdims=True)
+
+
+def unit_norm(values):
+    center = values - jnp.mean(values, axis=-1, keepdims=True)
+    inverse = lax.rsqrt(jnp.mean(center * center, axis=-1, keepdims=True) + EPS)
+    return center * inverse, inverse
+
+
+def norm_back(unit, inverse, incoming, gain):
+    scaled = incoming * gain
+    return inverse * (
+        scaled
+        - jnp.mean(scaled, axis=-1, keepdims=True)
+        - unit * jnp.mean(scaled * unit, axis=-1, keepdims=True)
+    )
+
+
+def row_of(ref):
+    return ref[...].reshape(1, -1)
+
+
+def enter_kernel(
+    tokens_ref, cot_ref, gain_ref, shift_ref, weight_ref, bias_ref,
+    row_out, normed_out, projected_out, cot0, cot1, cot2, cot3,
+    landed, weight_s, normed_s, projected_s, cot_s, send_sem, recv_sem, load_sem, cot_sem, out_sem,
+):
+    me, depth = lax.axis_index("seq"), lax.axis_index("dp")
+    high, low = me // 2, me % 2
+    peers = [me, 2 * high + 1 - low, 2 * (1 - high) + low, 3 - me]
+    shard, features = landed.shape[1:]
+    barrier = pltpu.get_barrier_semaphore()
+    for peer in peers[1:]:
+        pl.semaphore_signal(barrier, inc=1, device_id=(depth, peer), device_id_type=MESH)
+    own = pltpu.make_async_copy(tokens_ref.at[me, 0], landed.at[0], load_sem.at[0])
+    weight = pltpu.make_async_copy(weight_ref, weight_s, load_sem.at[1])
+    own.start()
+    weight.start()
+    pl.semaphore_wait(barrier, 3)
+
+    def remote(at, k, start, size):
+        rows = pl.ds(start, size)
+        return pltpu.make_async_remote_copy(
+            src_ref=tokens_ref.at[peers[k], 0, rows], dst_ref=landed.at[k, rows],
+            send_sem=send_sem.at[at], recv_sem=recv_sem.at[at], device_id=(depth, peers[k]), device_id_type=MESH,
+        )
+
+    copies = [remote(k - 1, k, 0, shard) for k in (1, 2, 3)]
+    for copy in copies[:2]:
+        copy.start()
+    loads = [pltpu.make_async_copy(cot_ref.at[peers[k], 0], cot_s.at[k], cot_sem.at[k]) for k in range(4)]
+    stores = [
+        pltpu.make_async_copy(cot_s.at[k], out, cot_sem.at[k]) for k, out in enumerate((cot0, cot1, cot2, cot3))
+    ]
+    for copy in loads:
+        copy.start()
+    bias = row_of(bias_ref)
+    bias = jnp.concatenate([bias[:, :features], jnp.zeros((1, features), F32), bias[:, features:]], axis=1)
+
+    def outs(k):
+        rows = pl.ds(pl.multiple_of(k * shard, shard), shard)
+        pairs = (
+            (landed.at[k], row_out), (normed_s.at[rows], normed_out), (projected_s.at[rows], projected_out),
+        )
+        return [
+            pltpu.make_async_copy(src, dst.at[rows], out_sem.at[3 * k + n]) for n, (src, dst) in enumerate(pairs)
+        ]
+
+    def body(k, carry):
+        @pl.when(k == 0)
+        def _():
+            own.wait()
+            weight.wait()
+
+        @pl.when(k == 1)
+        def _():
+            for load, store in zip(loads, stores):
+                load.wait()
+                store.start()
+            for copy in copies[:2]:
+                copy.wait_send()
+            copies[2].start()
+
+        for piece in (1, 2, 3):
+
+            @pl.when(k == piece)
+            def _():
+                copies[piece - 1].wait_recv()
+
+        unit, _ = unit_norm(landed[k].astype(F32))
+        normed = (unit * row_of(gain_ref) + row_of(shift_ref)).astype(BF)
+        rows = pl.ds(pl.multiple_of(k * shard, shard), shard)
+        normed_s[rows, :] = normed
+        projected_s[rows, :] = (dot_plain(normed, weight_s[...]) + bias).astype(BF)
+        for copy in outs(k):
+            copy.start()
+        return carry
+
+    lax.fori_loop(0, 4, body, 0)
+    for copy in stores:
+        copy.wait()
+    for k in range(4):
+        for copy in outs(k):
+            copy.wait()
+    copies[2].wait_send()
+
+
+def enter(tokens, cotangent, gain, shift, weight, bias):
+    _, _, shard, features = tokens.shape
+    count, wide = 4 * shard, weight.shape[1]
+    shape = jax.ShapeDtypeStruct
+    vmem = pl.BlockSpec(memory_space=pltpu.VMEM)
+    dma = pltpu.SemaphoreType.DMA
+    return pl.pallas_call(
+        enter_kernel,
+        in_specs=[ANY, ANY, vmem, vmem, ANY, vmem],
+        out_specs=[ANY] * 7,
+        out_shape=[shape((count, features), BF), shape((count, features), BF), shape((count, wide), BF)]
+        + [shape((shard, features), BF)] * 4,
+        scratch_shapes=[
+            pltpu.VMEM((4, shard, features), BF), pltpu.VMEM(weight.shape, BF), pltpu.VMEM((count, features), BF),
+            pltpu.VMEM((count, wide), BF), pltpu.VMEM((4, shard, features), BF),
+            dma((3,)), dma((3,)), dma((2,)), dma((4,)), dma((12,)),
+        ],
+        compiler_params=pltpu.CompilerParams(collective_id=0, has_side_effects=True, vmem_limit_bytes=VMEM_GRANT),
+        cost_estimate=pl.CostEstimate(flops=4 * 10**9, bytes_accessed=20 * 2**20, transcendentals=0),
+        name="enter",
+    )(tokens, cotangent, gain, shift, weight, bias)
+
+
+def attention_forward_kernel(block, q_ref, k_ref, v_ref, miss_ref, own_ref, out_ref, lse_ref):
+    lane = lax.broadcasted_iota(jnp.int32, (1, 128), 1)
+    first = lane < 64
+    keys, values, own = k_ref[...], v_ref[...], own_ref[...]
+    ones = jnp.ones_like(values)
+    keys_aug = [jnp.where(first, keys, own), jnp.where(first, own, keys)]
+    values_aug = [jnp.where(first, values, ones), jnp.where(first, ones, values)]
+
+    def body(step, carry):
+        rows = pl.ds(pl.multiple_of(step * block, block), block)
+        queries, miss = q_ref[rows, :] * BF(0.125), miss_ref[rows, :]
+        outs, logs = [], []
+        for head in range(2):
+            queries_aug = jnp.where(first, queries, miss) if head == 0 else jnp.where(first, miss, queries)
+            scores = dot_rows(queries_aug, keys_aug[head])
+            largest = jnp.max(scores, axis=1, keepdims=True)
+            weights = jnp.exp(scores - largest).astype(BF)
+            mixed = dot_plain(weights, values_aug[head])
+            total = mixed[:, 64:65] if head == 0 else mixed[:, 0:1]
+            outs.append(mixed / total)
+            logs.append(largest + jnp.log(total))
+        out_ref[rows, :] = jnp.where(first, outs[0], outs[1]).astype(BF)
+        lse_ref[0, rows, :] = jnp.where(first, logs[0], logs[1])
+        return carry
+
+    lax.fori_loop(0, q_ref.shape[0] // block, body, 0)
+
+
+def attention_forward(projected, miss, own, block=256):
+    count, width = projected.shape
+    pairs = width // 384
+    column = lambda base: pl.BlockSpec((count, 128), lambda i: (0, i + base))
+    full = pl.BlockSpec((count, 128), lambda i: (0, 0))
+    return pl.pallas_call(
+        functools.partial(attention_forward_kernel, block),
+        grid=(pairs,),
+        in_specs=[column(0), column(pairs), column(2 * pairs), full, full],
+        out_specs=[column(0), pl.BlockSpec((1, count, 128), lambda i: (i, 0, 0))],
+        out_shape=[
+            jax.ShapeDtypeStruct((count, width // 3), BF),
+            jax.ShapeDtypeStruct((pairs, count, 128), F32),
+        ],
+        compiler_params=pltpu.CompilerParams(vmem_limit_bytes=VMEM_GRANT),
+        cost_estimate=pl.CostEstimate(flops=24 * 10**9, bytes_accessed=8 * 2**20, transcendentals=12 * 2**20),
+        name="attention_forward",
+    )(projected, projected, projected, miss, own)
+
+
+def three_parts(column):
+    high = column.astype(BF)
+    rest = column - high.astype(F32)
+    middle = rest.astype(BF)
+    return high, middle, (rest - middle.astype(F32)).astype(BF)
+
+
+def segment_features(segment):
+    lane = jnp.arange(128) % 64
+    same = lane[None, :] == segment[:, None]
+    live = (lane < 8)[None, :]
+    return jnp.where(live & ~same, -BIG, 0.0).astype(BF), jnp.where(live & same, 1.0, 0.0).astype(BF)
+
+
+def flipped(static, bits):
+    total = 0
+    for at, bit in enumerate(bits):
+        weight = 1 << (len(bits) - 1 - at)
+        total = total + weight * ((1 - bit) if static & weight else bit)
+    return total
+
+
+def own_bits(order):
+    me, deep = lax.axis_index("seq"), lax.axis_index("dp") // 2
+    parts = {"low": [me % 2], "high": [me // 2], "deep": [deep // 2, deep % 2]}
+    return [bit for name in order for bit in parts[name]]
+
+
+def scatter_part(out_ref, values, order, part, base=0):
+    size = values.shape[0] // 8
+    top, *bits = own_bits(order)
+    first = 8 * (part + top - 2 * part * top)
+    for a in range(8):
+        rows = pl.ds(pl.multiple_of((first + flipped(a, bits)) * size, 16), size)
+        out_ref[rows, base : base + values.shape[1]] = values[a * size : (a + 1) * size].astype(out_ref.dtype)
+
+
+def peer_ids():
+    me, depth = lax.axis_index("seq"), lax.axis_index("dp")
+    high, low = me // 2, me % 2
+    core, deep = depth % 2, depth // 2
+    upper, lower = deep // 2, deep % 2
+    return {
+        ("core", 1): (2 * deep + 1 - core, me),
+        ("low", 1): (depth, 2 * high + 1 - low),
+        ("high", 1): (depth, 2 * (1 - high) + low),
+        ("both", 1): (depth, 3 - me),
+        ("deep", 1): (2 * (2 * upper + 1 - lower) + core, me),
+        ("deep", 2): (2 * (2 * (1 - upper) + lower) + core, me),
+        ("deep", 3): (2 * (3 - deep) + core, me),
+    }
+
+
+LOW_FIRST = ("low", "high", "deep")
+HIGH_FIRST = ("high", "low", "deep")
+DEEP_FIRST = ("deep", "high", "low")
+FAN = {"low": 2, "high": 2, "deep": 4}
+SEMS = 12
+
+
+def landing_rows(order, rows):
+    sizes = []
+    for name in order:
+        rows //= FAN[name]
+        sizes.append((FAN[name] - 1) * rows)
+    return sizes
+
+
+class Sum:
+    def __init__(self, order, rows, send, keep, core_buf, bufs, own, other, send_sems, recv_sems, local_sem):
+        self.order, self.rows, self.send, self.keep = order, rows, send, keep
+        self.core_buf, self.bufs, self.own, self.other = core_buf, bufs, own, other
+        self.send_sems, self.recv_sems, self.local_sem = send_sems, recv_sems, local_sem
+        self.sizes = []
+        for name in order:
+            rows //= FAN[name]
+            self.sizes.append(rows)
+        self.peers = peer_ids()
+
+    def stage(self, at):
+        if at == 0:
+            moves = [(self.send, self.core_buf, ("core", 1))]
+        elif at <= 3:
+            name, size, buf = self.order[at - 1], self.sizes[at - 1], self.bufs[at - 1]
+            moves = [
+                (self.keep.at[pl.ds(k * size, size)], buf.at[pl.ds((k - 1) * size, size)], (name, k))
+                for k in range(1, FAN[name])
+            ]
+        elif at <= 6:
+            name, size = self.order[6 - at], self.sizes[6 - at]
+            src = self.keep if at == 4 else self.own
+            moves = [
+                (src.at[pl.ds(0, size)], self.own.at[pl.ds(k * size, size)], (name, k)) for k in range(1, FAN[name])
+            ]
+        else:
+            moves = [(self.own, self.other, ("core", 1))]
+        counts = [1] + [FAN[name] - 1 for name in self.order]
+        base = sum((counts + counts[:0:-1])[:at])
+        return [
+            pltpu.make_async_remote_copy(
+                src_ref=src, dst_ref=dst, send_sem=self.send_sems.at[base + k], recv_sem=self.recv_sems.at[base + k],
+                device_id=self.peers[peer], device_id_type=MESH,
+            )
+            for k, (src, dst, peer) in enumerate(moves)
+        ]
+
+    def local(self):
+        rows = pl.ds(0, self.sizes[2])
+        return pltpu.make_async_copy(self.keep.at[rows], self.own.at[rows], self.local_sem)
+
+    def start(self, stage):
+        for copy in self.stage(stage):
+            copy.start()
+
+    def arrived(self, stage):
+        for copy in self.stage(stage):
+            copy.wait_recv()
+
+    def left(self, first, last):
+        for stage in range(first, last):
+            for copy in self.stage(stage):
+                copy.wait_send()
+
+    def add(self, start, size, sources):
+        chunk = next(rows for rows in (64, 48, 32) if size % rows == 0)
+
+        def body(at, carry):
+            rows = lambda base: pl.ds(pl.multiple_of(base + at * chunk, 16), chunk)
+            total = self.keep[rows(start), :].astype(F32)
+            for buf, offset in sources:
+                total = total + buf[rows(offset + start), :].astype(F32)
+            self.keep[rows(start), :] = total.astype(self.keep.dtype)
+            return carry
+
+        lax.fori_loop(0, size // chunk, body, 0)
+
+    def sources(self, stage):
+        if stage == 0:
+            return [(self.core_buf, 0)]
+        size = self.sizes[stage - 1]
+        return [(self.bufs[stage - 1], k * size) for k in range(FAN[self.order[stage - 1]] - 1)]
+
+    def settle(self, stage):
+        self.arrived(stage)
+        self.add(0, self.rows if stage == 0 else self.sizes[stage - 1], self.sources(stage))
+
+    def tick(self, at, resumed=False):
+        if at == 0 or resumed:
+            self.start(at)
+        elif at <= 3:
+            self.arrived(at - 1)
+            sources, size = self.sources(at - 1), self.sizes[at - 1]
+            self.add(size, (self.rows if at == 1 else self.sizes[at - 2]) - size, sources)
+            self.start(at)
+            self.add(0, size, sources)
+        elif at == 4:
+            self.settle(3)
+            self.local().start()
+            self.start(4)
+        elif at <= 7:
+            self.arrived(at - 1)
+            if at == 5:
+                self.local().wait()
+            self.start(at)
+        else:
+            self.arrived(7)
+
+
+UNITS = 3
+
+
+def gelu_parts(values):
+    size = jnp.abs(values)
+    bell = jnp.exp(-0.5 * values * values)
+    part = 1.0 / (1.0 + 0.3275911 * 0.7071067811865476 * size)
+    series = part * (
+        0.127414796
+        + part * (-0.142248368 + part * (0.7107068705 + part * (-0.7265760135 + part * 0.5307027145)))
+    )
+    tail = series * bell
+    below = jnp.where(values >= 0, 1.0 - tail, tail)
+    return values * below, below + values * (bell * 0.3989422804014327)
+
+
+FEED_PLAN = {
+    (3, 0): [(0, 0)],
+    (3, 1): [(0, 1)],
+    (5, 0): [(1, 0)],
+    (5, 1): [(1, 1), (0, 2)],
+    (6, 1): [(1, 2)],
+}
+
+
+def feed_kernel(
+    row_ref, att_ref, g0, g1, g2, g3, out_weight_ref, out_bias_ref, gain_ref, shift_ref, fc2_bias_ref,
+    w1_ref, bias_ref, w2_ref, *refs
+):
+    outs, refs = refs[:17], refs[17:]
+    results, (branch_out, att_grad_out), sums_out = outs[:4], outs[4:6], outs[6:10]
+    last_out, vec_ref = outs[10:16], outs[16]
+    (
+        n2_s, mid_s, acc_s, back_s, grad_s, hidden_s, hidden_grad_s, result_s, branch_s, att_grad_s,
+        d1_s, d2_s, do_s, bias_s, core1, core2, near1, near2, next1, next2, send_sems, recv_sems, load_sems, out_sems,
+    ) = refs
+    step = pl.program_id(0)
+    core = lax.axis_index("dp") % 2
+    count = row_ref.shape[0]
+    size = w1_ref.shape[1]
+    shard = count // 4
+    half = do_s.shape[2]
+    blocks = [pl.ds(i * shard, shard) for i in range(4)]
+    peers = peer_ids()
+
+    def job(unit, which):
+        slot = 2 * unit + which
+        d, bufs = (d1_s, (core1, near1, next1)) if which == 0 else (d2_s, (core2, near2, next2))
+        return Sum(
+            (LOW_FIRST, HIGH_FIRST)[which], d.shape[1], d.at[2 * unit], d.at[2 * unit + 1], bufs[0].at[unit],
+            [bufs[1].at[unit], bufs[2].at[unit], None], None, None, send_sems.at[slot], recv_sems.at[slot], None,
+        )
+
+    def ticks(at, place):
+        for unit, tick in FEED_PLAN.get((at, place), []):
+            for which in range(2):
+                job(unit, which).tick(tick)
+
+    def load(k):
+        return pltpu.make_async_copy((g0, g1, g2, g3)[k], grad_s.at[blocks[k]], load_sems.at[k])
+
+    def stores(first, last_store):
+        pairs = [(result_s.at[rows], out) for rows, out in zip(blocks, results)]
+        pairs += [(branch_s, branch_out), (att_grad_s, att_grad_out)]
+        last = 2 * (UNITS - 1)
+        pairs += [(d1_s.at[last], last_out[0]), (d1_s.at[last + 1], last_out[1])]
+        pairs += [(d2_s.at[last], last_out[2]), (d2_s.at[last + 1], last_out[3])]
+        pairs += [(do_s.at[0], last_out[4]), (do_s.at[1], last_out[5])]
+        for unit in range(2):
+            for which, d in enumerate((d1_s, d2_s)):
+                rows = pl.ds(0, d.shape[1] // 4)
+                pairs.append((d.at[2 * unit + 1, rows], sums_out[2 * unit + which]))
+        return [pltpu.make_async_copy(src, dst, out_sems.at[n]) for n, (src, dst) in enumerate(pairs) if first <= n < last_store]
+
+    @pl.when(step == 0)
+    def _():
+        barrier = pltpu.get_barrier_semaphore()
+        for name in ("core", "low", "high"):
+            pl.semaphore_signal(barrier, inc=1, device_id=peers[name, 1], device_id_type=MESH)
+        for k in range(4):
+            load(k).start()
+        vec_ref[...] = jnp.zeros_like(vec_ref)
+        for at in range(2 * UNITS):
+            bias_s[at : at + 1, :] = bias_ref[at * size : (at + 1) * size].reshape(1, -1)
+
+        def project(i, carry):
+            rows = pl.ds(pl.multiple_of(i * shard, shard), shard)
+            mid = row_ref[rows, :].astype(F32) + (dot_plain(att_ref[rows, :], out_weight_ref[...]) + row_of(out_bias_ref))
+            mid_s[rows, :] = mid
+            acc_s[rows, :] = mid + row_of(fc2_bias_ref)
+            unit, _ = unit_norm(mid)
+            n2_s[rows, :] = (unit * row_of(gain_ref) + row_of(shift_ref)).astype(BF)
+            return carry
+
+        lax.fori_loop(0, 4, project, 0)
+        back_s[...] = jnp.zeros_like(back_s)
+        for k in range(4):
+            load(k).wait()
+
+    @pl.when(step == 2)
+    def _():
+        pl.semaphore_wait(pltpu.get_barrier_semaphore(), 3)
+
+    for at in range(1, 2 * UNITS + 1):
+        unit, keeping = (at - 1) // 2, (at - 1) % 2
+
+        @pl.when(step == at)
+        def _():
+            ticks(at, 0)
+
+    last_step = step == 2 * UNITS
+
+    at_chunk = jnp.maximum(step - 1, 0)
+    chunk_row = 2 * (at_chunk // 2) + (core + 1 + at_chunk % 2) % 2
+
+    @pl.when(step > 0)
+    def _():
+        bias = bias_s[pl.ds(chunk_row, 1), :]
+
+        def body(i, total):
+            rows = pl.ds(pl.multiple_of(i * shard, shard), shard)
+            pre = dot_plain(n2_s[rows, :], w1_ref[...]) + bias
+            back = dot_rows(grad_s[rows, :], w2_ref[...])
+            hidden, slope = gelu_parts(pre)
+            hidden, hidden_grad = hidden.astype(BF), (back * slope).astype(BF)
+            hidden_s[rows, :] = hidden
+            hidden_grad_s[rows, :] = hidden_grad
+            acc_s[rows, :] += dot_plain(hidden, w2_ref[...])
+            back_s[rows, :] += dot_rows(hidden_grad, w1_ref[...])
+            return total + total_rows(hidden_grad.astype(F32))
+
+        total = lax.fori_loop(0, 4, body, jnp.zeros((1, size), F32))
+        vec_ref[pl.ds(4 + chunk_row, 1), 0:size] = total
+
+    @pl.when(last_step)
+    def _():
+        def body(i, sums):
+            rows = pl.ds(pl.multiple_of(i * shard, shard), shard)
+            result_s[rows, :] = acc_s[rows, :].astype(BF)
+            back = back_s[rows, :]
+            unit, inverse = unit_norm(mid_s[rows, :])
+            wide = grad_s[rows, :].astype(F32)
+            branch = (wide + norm_back(unit, inverse, back, row_of(gain_ref))).astype(BF)
+            branch_s[rows, :] = branch
+            att_grad_s[rows, :] = dot_rows(branch, out_weight_ref[...]).astype(BF)
+            parts = (back * unit, back, branch.astype(F32), wide)
+            return tuple(old + total_rows(part) for old, part in zip(sums, parts))
+
+        sums = lax.fori_loop(0, 4, body, (jnp.zeros((1, n2_s.shape[1]), F32),) * 4)
+        for at, part in enumerate(sums):
+            vec_ref[at + 10 : at + 11, :] = part
+        for copy in stores(0, 6):
+            copy.start()
+
+    for at in range(1, 2 * UNITS + 1):
+
+        @pl.when(step == at)
+        def _():
+            ticks(at, 1)
+
+    @pl.when(step > 0)
+    def _():
+        def body(part, carry):
+            wide, narrow = n2_s.shape[1] // 2, size // 2
+            left = n2_s[:, pl.ds(pl.multiple_of(part * wide, 128), wide)]
+            scatter_part(d1_s.at[step - 1], dot_tokens(left, hidden_grad_s[...]), LOW_FIRST, part)
+            left = hidden_s[:, pl.ds(pl.multiple_of(part * narrow, 128), narrow)]
+            scatter_part(d2_s.at[step - 1], dot_tokens(left, grad_s[...]), HIGH_FIRST, part)
+            return carry
+
+        lax.fori_loop(0, 2, body, 0)
+
+    @pl.when(last_step)
+    def _():
+        def body(at, carry):
+            slot, part = at // 2, at % 2
+            wide = att_ref.shape[1] // 2
+            columns = pl.ds(pl.multiple_of(((core + 1 + slot) % 2) * half, 128), half)
+            left = att_ref[:, pl.ds(pl.multiple_of(part * wide, 128), wide)]
+            scatter_part(do_s.at[slot], dot_tokens(left, branch_s[:, columns]), ORDERS[6], part)
+            return carry
+
+        lax.fori_loop(0, 4, body, 0)
+        for copy in stores(6, 12):
+            copy.start()
+        for unit in range(2):
+            for which in range(2):
+                job(unit, which).settle(2)
+        for copy in stores(12, 16):
+            copy.start()
+        for copy in stores(0, 16):
+            copy.wait()
+        for unit in range(2):
+            for which in range(2):
+                job(unit, which).left(0, 3)
+
+
+def feed(row, attended, grads, out_weight, out_bias, gain, shift, fc1_weight, fc1_bias, fc2_weight, fc2_bias):
+    count, features = row.shape
+    size = fc1_weight.shape[1] // (2 * UNITS)
+    half = features // 2
+    shape = jax.ShapeDtypeStruct
+    wide, line = once((count, features)), once((features,))
+    vmem, dma = pltpu.VMEM, pltpu.SemaphoreType.DMA
+
+    def chunk(i):
+        at = jnp.maximum(i - 1, 0)
+        return 2 * (at // 2) + (lax.axis_index("dp") % 2 + 1 + at % 2) % 2
+
+    return pl.pallas_call(
+        feed_kernel,
+        grid=(2 * UNITS + 1,),
+        in_specs=[wide, wide] + [ANY] * 4 + [once(out_weight.shape), line, line, line, line]
+        + [
+            pl.BlockSpec((features, size), lambda i: (0, chunk(i))),
+            once(fc1_bias.shape),
+            pl.BlockSpec((size, features), lambda i: (chunk(i), 0)),
+        ],
+        out_specs=[ANY] * 16 + [once((16, features))],
+        out_shape=[shape(grads[0].shape, BF)] * 4 + [shape((count, features), BF)] * 2
+        + [shape((features // 4, size), BF), shape((size // 4, features), BF)] * 2
+        + [shape((features, size), BF)] * 2 + [shape((size, features), BF)] * 2
+        + [shape((features, half), BF)] * 2 + [shape((16, features), F32)],
+        scratch_shapes=[vmem((count, features), BF)] + [vmem((count, features), F32)] * 3
+        + [vmem((count, features), BF), vmem((count, size), BF), vmem((count, size), BF)]
+        + [vmem((count, features), BF)] * 3
+        + [
+            vmem((2 * UNITS, features, size), BF), vmem((2 * UNITS, size, features), BF), vmem((2, features, half), BF),
+            vmem((8, size), F32),
+            vmem((2, features, size), BF), vmem((2, size, features), BF),
+            vmem((2, features // 2, size), BF), vmem((2, size // 2, features), BF),
+            vmem((2, features // 4, size), BF), vmem((2, size // 4, features), BF),
+            dma((4, SEMS)), dma((4, SEMS)), dma((4,)), dma((16,)),
+        ],
+        compiler_params=pltpu.CompilerParams(collective_id=2, has_side_effects=True, vmem_limit_bytes=VMEM_GRANT),
+        cost_estimate=pl.CostEstimate(flops=35 * 10**9, bytes_accessed=40 * 2**20, transcendentals=0),
+        name="feed",
+    )(
+        row, attended, *grads, out_weight, out_bias, gain, shift, fc2_bias, fc1_weight, fc1_bias, fc2_weight,
+    )
+
+
+ORDERS = (
+    LOW_FIRST, HIGH_FIRST, LOW_FIRST, HIGH_FIRST, LOW_FIRST, HIGH_FIRST, DEEP_FIRST, LOW_FIRST, LOW_FIRST, LOW_FIRST
+)
+PLAN = {
+    (0, 0): [(4, 0), (5, 0), (6, 0), (0, 3), (1, 3), (2, 3), (3, 3)],
+    (0, 1): [(4, 1), (5, 1), (6, 1), (0, 4)],
+    (1, 0): [(1, 4)],
+    (1, 1): [(4, 2), (5, 2), (2, 4), (3, 4)],
+    (2, 0): [(7, 0)],
+    (2, 1): [(7, 1)],
+    (3, 1): [(6, 2), (0, 5)],
+    (4, 0): [(8, 0), (4, 3), (5, 3), (1, 5)],
+    (4, 1): [(8, 1), (7, 2), (6, 3), (2, 5), (3, 5), (0, 6)],
+    (5, 0): [(1, 6)],
+    (5, 1): [(8, 2), (7, 3), (4, 4), (5, 4), (6, 4), (2, 6)],
+    (6, 0): [(9, 0)],
+    "tail": [
+        (9, 1), (7, 4), (4, 5), (3, 6), (1, 7), (8, 3), (0, 7), (6, 5), (5, 5), (7, 5), (8, 4), (2, 7),
+        (8, 5), (4, 6), (3, 7), (6, 6), (9, 2), (7, 6), (8, 6), (5, 6), (9, 3), (6, 7), (4, 7), (9, 4),
+        (5, 7), (7, 7), (9, 5), (9, 6), (8, 7), (9, 7),
+    ],
+}
+BLOCK_OUT_AT = 0
+
+
+def three_parts(column):
+    high = column.astype(BF)
+    rest = column - high.astype(F32)
+    middle = rest.astype(BF)
+    return high, middle, (rest - middle.astype(F32)).astype(BF)
+
+
+def pair_backward(refs, outs, dk_acc, dv_acc, pair, block):
+    q_ref, k_ref, v_ref, att_ref, grad_ref, lse_ref, miss_ref, own_ref = refs
+    lane = lax.broadcasted_iota(jnp.int32, (1, 128), 1)
+    first = lane < 64
+    half = lane % 64
+    keys, values, own = k_ref[...], v_ref[...], own_ref[...]
+    unit = jnp.where((half >= 8) & (half < 11), 1.0, 0.0).astype(BF)
+    own = own + unit
+    unit_rows = jnp.broadcast_to(unit, values.shape)
+    keys_aug = [jnp.where(first, keys, own), jnp.where(first, own, keys)]
+    values_aug = [jnp.where(first, values, unit_rows), jnp.where(first, unit_rows, values)]
+    keys_only = [jnp.where(first, keys, BF(0)), jnp.where(first, BF(0), keys)]
+    dk_acc[...] = jnp.zeros_like(dk_acc)
+    dv_acc[...] = jnp.zeros_like(dv_acc)
+    columns = pl.ds(pl.multiple_of(pair * 128, 128), 128)
+
+    def spread(column):
+        high, middle, low = [part.astype(F32) for part in three_parts(-column)]
+        wide = jnp.where(half == 8, high, jnp.where(half == 9, middle, jnp.where(half == 10, low, 0.0)))
+        return wide.astype(BF)
+
+    def body(step, carry):
+        rows = pl.ds(pl.multiple_of(step * block, block), block)
+        queries, miss, grad = q_ref[rows, :] * BF(0.125), miss_ref[rows, :], grad_ref[rows, :]
+        both = att_ref[rows, :].astype(F32) * grad.astype(F32)
+        logs = lse_ref[0, rows, :]
+        queries_t, grad_t = queries.T, grad.T
+        dq = jnp.zeros((block, 128), F32)
+        for head in range(2):
+            mine = first if head == 0 else jnp.logical_not(first)
+            span = pl.ds(64 * head, 64)
+            delta = jnp.sum(jnp.where(mine, both, 0.0), axis=1, keepdims=True)
+            total = logs[:, 0:1] if head == 0 else logs[:, 64:65]
+            queries_aug = jnp.where(mine, queries, spread(total) + miss)
+            grad_aug = jnp.where(mine, grad, spread(delta))
+            probs = jnp.exp(dot_rows(queries_aug, keys_aug[head]))
+            score_grad = (probs * dot_rows(grad_aug, values_aug[head])).astype(BF)
+            dq = dq + dot_plain(score_grad, keys_only[head])
+            dk_acc[span, :] += dot_plain(queries_t[64 * head : 64 * head + 64], score_grad)
+            dv_acc[span, :] += dot_plain(grad_t[64 * head : 64 * head + 64], probs.astype(BF))
+        outs[0][rows, columns] = (dq * 0.125).astype(BF)
+        return carry
+
+    lax.fori_loop(0, q_ref.shape[0] // block, body, 0)
+    outs[1][:, columns] = dk_acc[...].T.astype(BF)
+    outs[2][:, columns] = dv_acc[...].T.astype(BF)
+
+
+def backward_kernel(*refs):
+    (
+        q_ref, k_ref, v_ref, att_ref, grad_ref, lse_ref, miss_ref, own_ref, normed_ref,
+        weight_ref, row_ref, branch_ref, gain_ref, vec_in_ref,
+    ) = refs[:14]
+    results, sums_in, last_in = refs[14:18], refs[18:22], refs[22:28]
+    block_out, tokens_out, vec_out = refs[28:31]
+    owns, others = refs[31:41], refs[41:51]
+    (
+        dq_s, dk_s, dv_s, dk_acc, dv_acc, qkv_s, own_result, grad_s, vec_s, vec_got,
+        send_sems, recv_sems, local_sems, load_sems, side_send, side_recv, vec_send, vec_recv,
+    ) = refs[51:69]
+    held = refs[69:76]
+    landing = refs[76:]
+    step = pl.program_id(0)
+    me, depth = lax.axis_index("seq"), lax.axis_index("dp")
+    core = depth % 2
+    peers = peer_ids()
+    shard = results[0].shape[0]
+    features = row_ref.shape[1]
+
+    def job(n):
+        sems = send_sems.at[n], recv_sems.at[n], local_sems.at[n]
+        if n < 4:
+            return Sum(
+                ORDERS[n], 4 * held[n].shape[0], None, held[n], None, [None, None, landing[n]], owns[n], others[n], *sems
+            )
+        send = last_in[2 * (n - 4)] if n < 7 else qkv_s.at[2 * (n - 7)]
+        keep = held[n] if n < 7 else qkv_s.at[2 * (n - 7) + 1]
+        core_buf, *bufs = landing[4 * (n - 3) : 4 * (n - 2)]
+        return Sum(ORDERS[n], keep.shape[0], send, keep, core_buf, bufs, owns[n], others[n], *sems)
+
+    def load(n):
+        if n == 7:
+            return pltpu.make_async_copy(results[0], own_result, load_sems.at[7])
+        src = sums_in[n] if n < 4 else last_in[2 * (n - 4) + 1]
+        return pltpu.make_async_copy(src, held[n], load_sems.at[n])
+
+    def store():
+        return pltpu.make_async_copy(own_result, block_out.at[me, 0], load_sems.at[7])
+
+    def token_store():
+        return pltpu.make_async_copy(grad_s.at[0], tokens_out.at[me, 0], load_sems.at[8])
+
+    kinds = [("low", 1), ("high", 1), ("both", 1)]
+
+    def spread_row(number, k, piece, out):
+        return pltpu.make_async_remote_copy(
+            src_ref=piece, dst_ref=out.at[me, 0], send_sem=side_send.at[number, k - 1],
+            recv_sem=side_recv.at[number, k - 1], device_id=peers[kinds[k - 1]], device_id_type=MESH,
+        )
+
+    def block_copy(k):
+        return spread_row(0, k, results[k], block_out)
+
+    def token_copy(k):
+        return spread_row(1, k, grad_s.at[k], tokens_out)
+
+    vec_names = [[("core", 1)], kinds, [("deep", 1), ("deep", 2), ("deep", 3)]]
+
+    def vec_stage(stage):
+        return [
+            pltpu.make_async_remote_copy(
+                src_ref=vec_s.at[stage], dst_ref=vec_got.at[stage, k],
+                send_sem=vec_send.at[stage, k], recv_sem=vec_recv.at[stage, k],
+                device_id=peers[name], device_id_type=MESH,
+            )
+            for k, name in enumerate(vec_names[stage])
+        ]
+
+    def vec_step(stage):
+        for copy in vec_stage(stage):
+            copy.wait_recv()
+        total = vec_s[stage]
+        for k in range(len(vec_names[stage])):
+            total = total + vec_got[stage, k]
+        if stage == 2:
+            vec_out[...] = total
+        else:
+            vec_s[stage + 1] = total
+            for copy in vec_stage(stage + 1):
+                copy.start()
+
+    def ticks(at, place):
+        for n, tick in PLAN.get((at, place), []):
+            resumed = n < 4 and tick == 3
+            if resumed or (4 <= n < 7 and tick == 1):
+                load(n).wait()
+            job(n).tick(tick, resumed)
+
+    @pl.when(step == 0)
+    def _():
+        barrier = pltpu.get_barrier_semaphore()
+        for peer in peers.values():
+            pl.semaphore_signal(barrier, inc=1, device_id=peer, device_id_type=MESH)
+        for n in range(8):
+            load(n).start()
+        pl.semaphore_wait(barrier, len(peers))
+
+    for at in range(7):
+
+        @pl.when(step == at)
+        def _():
+            ticks(at, 0)
+            if at == 2:
+                load(7).wait()
+                store().start()
+
+    @pl.when(step < 6)
+    def _():
+        pair = 2 * (step // 2) + (core + 1 + step % 2) % 2
+        pair_backward(
+            (q_ref, k_ref, v_ref, att_ref, grad_ref, lse_ref, miss_ref, own_ref),
+            (dq_s, dk_s, dv_s), dk_acc, dv_acc, pair, 256,
+        )
+
+    for at in range(6):
+
+        @pl.when(step == at)
+        def _():
+            ticks(at, 1)
+            if at == BLOCK_OUT_AT:
+                for k in (1, 2, 3):
+                    block_copy(k).start()
+
+    @pl.when(step < 6)
+    def _():
+        pair = 2 * (step // 2) + (core + 1 + step % 2) % 2
+        columns = pl.ds(pl.multiple_of(pair * 128, 128), 128)
+        grads = jnp.concatenate([part[:, columns] for part in (dq_s, dk_s, dv_s)], axis=1)
+        vec_out[2:3, columns] = total_rows(grads[:, :128].astype(F32))
+        vec_out[3:4, columns] = total_rows(grads[:, 256:].astype(F32))
+
+        def body(part, carry):
+            left = normed_ref[:, pl.ds(pl.multiple_of(part * (features // 2), 128), features // 2)]
+            scatter_part(qkv_s.at[step], dot_tokens(left, grads), ORDERS[7], part)
+            return carry
+
+        lax.fori_loop(0, 2, body, 0)
+
+    @pl.when(step == 6)
+    def _():
+        def body(at, sums):
+            k = 3 - at
+            rows = pl.ds(pl.multiple_of(k * shard, shard), shard)
+            back = dot_rows(dq_s[rows, :], weight_ref[:, :features])
+            back = back + dot_rows(dk_s[rows, :], weight_ref[:, features : 2 * features])
+            back = back + dot_rows(dv_s[rows, :], weight_ref[:, 2 * features :])
+            unit, inverse = unit_norm(row_ref[rows, :].astype(F32))
+            grad_s[k] = (branch_ref[rows, :].astype(F32) + norm_back(unit, inverse, back, row_of(gain_ref))).astype(BF)
+            for piece in range(4):
+
+                @pl.when(k == piece)
+                def _():
+                    if piece:
+                        token_copy(piece).start()
+                    else:
+                        token_store().start()
+
+            return tuple(old + total_rows(part) for old, part in zip(sums, (back * unit, back)))
+
+        gain_sum, shift_sum = lax.fori_loop(0, 4, body, (jnp.zeros((1, features), F32),) * 2)
+        vec_s[0] = vec_in_ref[...]
+        vec_s[0, 0:1, :] = gain_sum
+        vec_s[0, 1:2, :] = shift_sum
+        vec_s[0, 2:4, :] = vec_out[2:4, :]
+        vec_stage(0)[0].start()
+
+    @pl.when(step == 7)
+    def _():
+        for index, (n, tick) in enumerate(PLAN["tail"]):
+            if index in (3, 8, 13):
+                vec_step((index - 3) // 5)
+            job(n).tick(tick)
+        for n in range(10):
+            job(n).arrived(7)
+        for n in range(10):
+            job(n).left(3 if n < 4 else 0, 8)
+        store().wait()
+        token_store().wait()
+        for k in (1, 2, 3):
+            block_copy(k).wait()
+            token_copy(k).wait()
+        for stage in range(3):
+            for copy in vec_stage(stage):
+                copy.wait_send()
+
+
+def backward(
+    projected, attended, attended_grad, logs, miss, own, normed, qkv_weight, row, branch, gain, vec_in,
+    results, sums_in, last_in,
+):
+    count, width = projected.shape
+    features = width // 3
+    pairs = width // 384
+    half = features // 2
+    shard = count // 4
+
+    def pair(i):
+        at = jnp.minimum(i, 5)
+        return 2 * (at // 2) + (lax.axis_index("dp") % 2 + 1 + at % 2) % 2
+
+    column = lambda base: pl.BlockSpec((count, 128), lambda i: (0, pair(i) + base))
+    shape = jax.ShapeDtypeStruct
+    wide = once((count, features))
+    full = once((count, 128))
+    vmem, dma = pltpu.VMEM, pltpu.SemaphoreType.DMA
+    sizes = [last_in[0].shape, last_in[2].shape] * UNITS + [(features, half)] * 4
+    held = [vmem(array.shape, BF) for array in (*sums_in, *last_in[1::2])]
+    landing = []
+    for n, (rows, columns) in enumerate(sizes):
+        lands = landing_rows(ORDERS[n], rows)
+        landing += [vmem((lands[2], columns), BF)] if n < 4 else [vmem((size, columns), BF) for size in [rows] + lands]
+    return pl.pallas_call(
+        backward_kernel,
+        grid=(8,),
+        in_specs=[
+            column(0), column(pairs), column(2 * pairs), column(0), column(0),
+            pl.BlockSpec((1, count, 128), lambda i: (pair(i), 0, 0)),
+            full, full, wide, once(qkv_weight.shape), wide, wide, once((features,)), once((16, features)),
+        ]
+        + [ANY] * 14,
+        out_specs=[ANY, ANY, once((16, features))] + [ANY] * 20,
+        out_shape=[shape((4, 1, shard, features), BF)] * 2 + [shape((16, features), F32)]
+        + [shape(size, BF) for size in sizes] * 2,
+        scratch_shapes=[vmem((count, features), BF)] * 3
+        + [vmem((128, count), F32)] * 2
+        + [vmem((6, features, half), BF)]
+        + [
+            vmem((shard, features), BF), vmem((4, shard, features), BF),
+            vmem((3, 16, features), F32), vmem((3, 3, 16, features), F32),
+            dma((10, SEMS)), dma((10, SEMS)), dma((10,)), dma((9,)), dma((2, 3)), dma((2, 3)), dma((3, 3)), dma((3, 3)),
+        ]
+        + held + landing,
+        compiler_params=pltpu.CompilerParams(collective_id=1, has_side_effects=True, vmem_limit_bytes=VMEM_GRANT),
+        cost_estimate=pl.CostEstimate(flops=60 * 10**9, bytes_accessed=60 * 2**20, transcendentals=12 * 2**20),
+        name="backward",
+    )(
+        projected, projected, projected, attended, attended_grad, logs, miss, own, normed, qkv_weight, row, branch,
+        gain, vec_in, *results, *sums_in, *last_in,
+    )
+
+
+STEPS = 8
+
+
+def own_group(order):
+    total = 0
+    for bit in own_bits(order):
+        total = 2 * total + bit
+    return total
+
+
+def assemble_kernel(*refs):
+    ins, vec_ref = refs[:20], refs[20]
+    d1_ref, d2_ref, out_ref, qkv_ref = refs[21:25]
+    vecs = refs[25:]
+    core = lax.axis_index("dp") % 2
+    features = out_ref.shape[1]
+    size = ins[0].shape[1]
+    half = features // 2
+
+    def ordered(n):
+        ref, last = ins[n], own_bits(ORDERS[n // 2])[3]
+        rows = ref.shape[0] // 2
+        return jnp.concatenate(
+            [ref[pl.ds(pl.multiple_of((a + last - 2 * a * last) * rows, 16), rows), :] for a in range(2)], axis=0
+        ).astype(F32)
+
+    for side in range(2):
+        home = core if side == 0 else 1 - core
+        for unit in range(UNITS):
+            columns = pl.ds(pl.multiple_of((2 * unit + home) * size, 128), size)
+            d1_ref[:, columns] = ordered(4 * unit + side)
+            d2_ref[unit, home] = ordered(4 * unit + 2 + side)
+        out_ref[:, pl.ds(pl.multiple_of(home * half, 128), half)] = ordered(12 + side)
+        for group in range(3):
+            values = ordered(14 + 2 * group + side)
+            for part in range(3):
+                at = part * features + (2 * group + home) * 128
+                qkv_ref[:, pl.ds(pl.multiple_of(at, 128), 128)] = values[:, part * 128 : (part + 1) * 128]
+
+    @pl.when(pl.program_id(0) == 0)
+    def _():
+        for ref, row in zip(vecs, (0, 1, 12, 10, 11, 13)):
+            ref[...] = vec_ref[row, :]
+        qv_ref, fc1_ref = vecs[6:]
+        for at in range(2):
+            qv_ref[at * features : (at + 1) * features] = vec_ref[2 + at, :]
+        for at in range(2 * UNITS):
+            fc1_ref[at * size : (at + 1) * size] = vec_ref[4 + at, 0:size]
+
+
+def assemble(parts, vector):
+    features, size = parts[0].shape
+    half = features // 2
+    wide = 2 * UNITS * size
+    shape = jax.ShapeDtypeStruct
+
+    def spec(n):
+        rows, columns = parts[n].shape
+        return pl.BlockSpec((rows // STEPS, columns), lambda i: (i ^ (own_group(ORDERS[n // 2]) // 2), 0))
+
+    lines = [features] * 6 + [2 * features, wide]
+    d1, d2, out, qkv, *vecs = pl.pallas_call(
+        assemble_kernel,
+        grid=(STEPS,),
+        in_specs=[spec(n) for n in range(20)] + [once(vector.shape)],
+        out_specs=[
+            pl.BlockSpec((features // STEPS, wide), lambda i: (i, 0)),
+            pl.BlockSpec((UNITS, 2, size // STEPS, features), lambda i: (0, 0, i, 0)),
+            pl.BlockSpec((features // STEPS, features), lambda i: (i, 0)),
+            pl.BlockSpec((features // STEPS, 3 * features), lambda i: (i, 0)),
+        ]
+        + [once((line,)) for line in lines],
+        out_shape=[
+            shape((features, wide), F32), shape((UNITS, 2, size, features), F32), shape((features, features), F32),
+            shape((features, 3 * features), F32),
+        ]
+        + [shape((line,), F32) for line in lines],
+        compiler_params=pltpu.CompilerParams(vmem_limit_bytes=VMEM_GRANT),
+        cost_estimate=pl.CostEstimate(flops=0, bytes_accessed=45 * 2**20, transcendentals=0),
+        name="assemble",
+    )(*parts, vector)
+    return d1, d2.reshape(wide, features), out, qkv, vecs
+
+
+def swap(array, axis, bit):
+    count = lax.axis_size(axis)
+    return lax.ppermute(array, axis, [(i, i ^ bit) for i in range(count)])
+
+
+def fast_shards(
+    tokens, image_lengths, cotangent, attn_gain, attn_shift, qkv_weight, qv_bias, out_weight,
+    out_bias, mlp_gain, mlp_shift, fc1_weight, fc1_bias, fc2_weight, fc2_bias,
+):
+    shard_len = tokens.shape[2]
+    parties = lax.axis_size("seq")
+    row_len = shard_len * parties
+    images = image_lengths.shape[2] - 1
+    me = lax.axis_index("seq")
+
+    row, normed, projected, *cots = enter(tokens, cotangent, attn_gain, attn_shift, qkv_weight, qv_bias)
+    seg_row = segment_ids(lax.dynamic_index_in_dim(image_lengths, me, 0, keepdims=False), row_len, images)
+    seg_row = seg_row.reshape(parties, shard_len)
+    segment = jnp.concatenate([seg_row[me ^ k] for k in range(parties)], axis=0)
+    miss, own = segment_features(segment)
+    attended, logs = attention_forward(projected, miss, own)
+    grads = [cots[0]] + [swap(cots[k], "seq", k) for k in (1, 2, 3)]
+    fed = feed(
+        row, attended, grads, out_weight, out_bias, mlp_gain, mlp_shift, fc1_weight, fc1_bias, fc2_weight, fc2_bias
+    )
+    results, (branch, attended_grad), sums, last, vec = fed[:4], fed[4:6], fed[6:10], fed[10:16], fed[16]
+    block_out, tokens_grad, vector, *summed = backward(
+        projected, attended, attended_grad, logs, miss, own, normed, qkv_weight, row, branch, attn_gain, vec,
+        results, sums, last,
+    )
+    paired = [part for n in range(10) for part in (summed[n], summed[10 + n])]
+    fc1_grad, fc2_grad, out_grad, qkv_grad, vecs = assemble(paired, vector)
+    gain, shift, out_sum, mlp_gain_sum, mlp_shift_sum, fc2_sum, qv_sum, fc1_sum = vecs
+    return (
+        block_out, tokens_grad, gain, shift, qkv_grad, qv_sum, out_grad, out_sum, mlp_gain_sum, mlp_shift_sum,
+        fc1_grad, fc1_sum, fc2_grad, fc2_sum,
+    )
+
+
+def shards(tokens, *rest):
+    micro_count, row_count, shard_len, features = tokens.shape
+    whole_rows = micro_count == 4 and row_count == 1 and shard_len % 128 == 0
+    sizes = lax.axis_size("dp") == 8 and lax.axis_size("seq") == 4
+    hidden = rest[10].shape[1]
+    if sizes and whole_rows and features == 64 * HEADS == 768 and hidden == 4 * features:
+        return fast_shards(tokens, *rest)
+    return general_shards(tokens, *rest)
+
 
 def solution(mesh):
     placed = (

time: 1100 us -> 306 us (0.28)
  waiting for transfers between devices: 481 us -> 0.01 us
  matrix products: 367 us -> 0 us
  Pallas kernels: 0 us -> 295 us
  other arithmetic: 97.4 us -> 1.36 us
  local copies, waits for them, and re-layouts: 81.6 us -> 4.11 us
  blocking collectives: 42.7 us -> 0 us
  between operations: 17.3 us -> 0.81 us
    dot_general x72 -> x0, matrix products: 367 us -> none  [matmul(): jnp.einsum(pattern, first_op, second_op, preferred_element_type=jnp.float32)]
    psum x1 -> x0, waiting for transfers between devices: 348 us -> none  [shards(): lax.psum((attn_gain_sum, attn_shift_sum, qkv_weight_sum, qv_bias_sum, out...]
    pallas_call x0 -> x5, Pallas kernels: none -> 295 us  [the longest x1 159 us: backward(): pl.pallas_call(backward_kernel, grid=(8,), in_specs=[column(0), column(pa...]
    all_gather x8 -> x0, waiting for transfers between devices: 102 us -> none  [the longest x4 64 us: shards(): lax.all_gather(projected[:, :, 2 * features:], 'seq', axis=1, tiled=True)]
    psum x1 -> x0, blocking collectives: 42.7 us -> none  [shards(): lax.psum((attn_gain_sum, attn_shift_sum, qkv_weight_sum, qv_bias_sum, out...]
    convert_element_type x4 -> x1, other arithmetic: 37.2 us -> 1.04 us  [segment_features(): jnp.where(live & same, 1.0, 0.0).astype(BF)]
    unnamed x496 -> x16, local copies, waits for them, and re-layouts: 39 us -> 4.08 us
    reduce_scatter x8 -> x0, waiting for transfers between devices: 27.5 us -> none  [the longest x4 27.5 us: shards(): lax.psum_scatter(key_terms.reshape(row_count, row_len, features).astype(j...]
  transfers between devices with their start and end apart: 17 -> 3, of which waited for: 8 -> 0; matrix products, arithmetic and copies ran while one was open for 39% -> 0% of each run, Pallas kernels for 0% -> 10%
where the time goes in v2:
time: 306 us; the launch traced here: 305 us
  Pallas kernels  295 us (96%)
  local copies, waits for them, and re-layouts  4.11 us (1%)
  starting transfers between devices  3.55 us (1%)
    pallas_call x1, Pallas kernels, backward(): pl.pallas_call(backward_kernel, grid=(8,), in_specs=[column(0), column(pa...  159 us
    pallas_call x1, Pallas kernels, feed(): pl.pallas_call(feed_kernel, grid=(2 * UNITS + 1,), in_specs=[wide, wide]...  63.1 us
    pallas_call x1, Pallas kernels, attention_forward(): pl.pallas_call(functools.partial(attention_forward_kernel, block), grid=(...  31.1 us
    pallas_call x1, Pallas kernels, enter(): pl.pallas_call(enter_kernel, in_specs=[ANY, ANY, vmem, vmem, ANY, vmem],...  25.2 us
    pallas_call x1, Pallas kernels, assemble(): pl.pallas_call(assemble_kernel, grid=(STEPS,), in_specs=[spec(n) for n in...  17 us
  transfers between devices with their start and end apart: 3, of which 0 were waited for; matrix products, arithmetic and copies ran while one was open for 0% of the time, Pallas kernels for 10%

profile of v2, /device:TPU:0, one launch (start us, length us, event | category | flops | bytes accessed | tf_op | source)
XLA Modules:
  0.0 305.3 jit_solution(10850984809979940743)
XLA Ops:
  0.6 0.0 copy-start
  0.7 25.2 %enter.1 = (bf16[1024,768]{1,0:T(8,128)(2,1)}, bf16[1024,768]{1,0:T(8,128)(2,1)}, bf16[1024,2304]{1,0:T(8,128)(2,1)}, bf16[256,768]{1,0:T(8,128)(2,1)}, bf16[256...) custom-call(bf16[4,1,256,768]{3,2,1,0:T(8,128)(2,1)} %tokens_ref.1, ...), custom_call_target="tpu_custom_call" | custom-call | flops 4000000000 | bytes 20971520 | tf_op jit(solution)/shard_map/enter/pallas_call | solution.py:355
  25.9 1.5 collective-permute-start
  27.4 1.5 collective-permute-start.1
  28.9 0.6 collective-permute-start.2
  29.4 0.0 copy-done
  29.5 0.2 reduce-window.7
  29.6 0.1 fusion.1
  29.8 1.0 select_convert_fusion
  30.9 31.1 %attention_forward.1 = (bf16[1024,768]{1,0:T(8,128)(2,1)}, f32[6,1024,128]{2,1,0:T(8,128)}) custom-call(bf16[1024,2304]{1,0:T(8,128)(2,1)} %get-tuple-element.75.q_ref.k_ref.v_ref.refs_0_.refs_1_.refs_2_, bf16[1024,2304]{1,0:T(8,128)(2,1)} %get-tuple-element.75.q_ref.k_ref.v_ref.refs_0_.refs_1_.refs_2_, ...), custom_call_target="tpu_custom_call" | custom-call | flops 24000000000 | bytes 8388608 | tf_op jit(solution)/shard_map/attention_forward/pallas_call | solution.py:405
  62.0 0.0 collective-permute-done.g1
  62.0 0.0 copy-start.4
  62.0 0.0 collective-permute-done.1.g2
  62.0 0.0 copy-start.5
  62.1 0.0 collective-permute-done.2.g3
  62.1 0.0 copy-start.6
  62.1 0.7 copy-done.4
  62.8 0.1 copy-done.5
  62.9 0.1 copy-done.6
  63.0 63.1 %feed.1 = (bf16[256,768]{1,0:T(8,128)(2,1)}, bf16[256,768]{1,0:T(8,128)(2,1)}, bf16[256,768]{1,0:T(8,128)(2,1)}, bf16[256,768]{1,0:T(8,128)(2,1)}, bf16[1024,768...) custom-call(bf16[1024,768]{1,0:T(8,128)(2,1)} %get-tuple-element.77., ...), custom_call_target="tpu_custom_call" | custom-call | flops 35000000512 | bytes 41943040 | tf_op jit(solution)/shard_map/feed/pallas_call | solution.py:797
  126.2 159.1 %backward.1 = (bf16[4,1,256,768]{3,2,1,0:T(8,128)(2,1)}, bf16[4,1,256,768]{3,2,1,0:T(8,128)(2,1)}, f32[16,768]{1,0:T(8,128)}, bf16[768,512]{1,0:T(8,128)(2,1)}, ...) custom-call(bf16[1024,2304]{1,0:T(8,128)(2,1)} %get-tuple-element.75, ...), custom_call_target="tpu_custom_call" | custom-call | flops 60000002048 | bytes 62914560 | tf_op jit(solution)/shard_map/backward/pallas_call | solution.py:1123
  285.2 0.0 copy-start.3
  285.2 17.0 %assemble.1 = (f32[768,3072]{1,0:T(8,128)}, f32[3,2,512,768]{3,2,1,0:T(8,128)}, f32[768,768]{1,0:T(8,128)}, f32[768,2304]{1,0:T(8,128)}, f32[768]{0:T(1024)}, /*...) custom-call(bf16[768,512]{1,0:T(8,128)(2,1)} %get-tuple-element.103., ...), custom_call_target="tpu_custom_call" | custom-call | bytes 47185920 | tf_op jit(solution)/shard_map/assemble/pallas_call | solution.py:1214
  302.2 0.0 copy-done.3
  302.2 0.0 copy-start.2
  302.2 0.0 copy-start.1
  302.2 1.1 copy.31
  303.4 0.8 copy-done.2
  304.2 1.1 copy.32
  305.3 0.0 copy-done.1
  (8 shorter events, 0.1 us)
Async XLA Ops:
  0.6 28.8 %copy-start = (s32[4,1,5]{2,1,0:T(1,128)S(1)}, s32[4,1,5]{2,1,0:T(1,128)}, u32[]{:S(2)}) copy-start(s32[4,1,5]{2,1,0:T(1,128)} %param.16) | copy-start | bytes 244
  25.9 36.1 %collective-permute-start = (bf16[256,768]{1,0:T(8,128)(2,1)}, bf16[256,768]{1,0:T(8,128)(2,1)S(1)}, u32[]{:S(2)}, u32[]{:S(2)}) collective-permute-start(bf16[256,768]{1,0:T(8,128)(2,1)} %get-tuple-element.79), channel_id=1, source_target_pairs={{0,1},{1,0},{2,3},{3,2},{4,5},{5,4},{6,7},{7,6},{8,9},{9,8},{10,11... | collective-permute-start | bytes 1179656 | tf_op jit(solution)/shard_map/ppermute | solution.py:1239
  27.4 34.6 %collective-permute-start.1 = (bf16[256,768]{1,0:T(8,128)(2,1)}, bf16[256,768]{1,0:T(8,128)(2,1)S(1)}, u32[]{:S(2)}, u32[]{:S(2)}) collective-permute-start(bf16[256,768]{1,0:T(8,128)(2,1)} %get-tuple-element.80), channel_id=1, source_target_pairs={{0,2},{1,3},{2,0},{3,1},{4,6},{5,7},{6,4},{7,5},{8,10},{9,11},{10,... | collective-permute-start | bytes 1179656 | tf_op jit(solution)/shard_map/ppermute | solution.py:1239
  28.9 33.2 %collective-permute-start.2 = (bf16[256,768]{1,0:T(8,128)(2,1)}, bf16[256,768]{1,0:T(8,128)(2,1)S(1)}, u32[]{:S(2)}, u32[]{:S(2)}) collective-permute-start(bf16[256,768]{1,0:T(8,128)(2,1)} %get-tuple-element.81), channel_id=1, source_target_pairs={{0,3},{1,2},{2,1},{3,0},{4,7},{5,6},{6,5},{7,4},{8,11},{9,10},{10,... | collective-permute-start | bytes 1179656 | tf_op jit(solution)/shard_map/ppermute | solution.py:1239
  62.0 0.7 copy-start.4
  62.0 0.9 copy-start.5
  62.1 1.0 copy-start.6
  285.2 17.0 %copy-start.3 = (bf16[4,1,256,768]{3,2,1,0:T(8,128)(2,1)S(1)}, bf16[4,1,256,768]{3,2,1,0:T(8,128)(2,1)}, u32[]{:S(2)}) copy-start(bf16[4,1,256,768]{3,2,1,0:T(8,128)(2,1)} %get-tuple-element.156) | copy-start | bytes 4718596
  302.2 2.0 copy-start.2
  302.2 3.1 %copy-start.1 = (s32[4,1,5]{2,1,0:T(1,128)S(1)}, s32[4,1,5]{2,1,0:T(1,128)}, u32[]{:S(2)}) copy-start(s32[4,1,5]{2,1,0:T(1,128)} %param.16) | copy-start | bytes 244

commit v3 on v2

--- a/solution.py
+++ b/solution.py
@@ -369,32 +369,48 @@
     )(tokens, cotangent, gain, shift, weight, bias)
 
 
-def attention_forward_kernel(block, q_ref, k_ref, v_ref, miss_ref, own_ref, out_ref, lse_ref):
+def attention_forward_kernel(
+    block, q_ref, k_ref, v_ref, miss_ref, own_ref, out_ref, lse_ref, scores_s, weights_s, mixed_s, largest_s
+):
     lane = lax.broadcasted_iota(jnp.int32, (1, 128), 1)
     first = lane < 64
     keys, values, own = k_ref[...], v_ref[...], own_ref[...]
     ones = jnp.ones_like(values)
     keys_aug = [jnp.where(first, keys, own), jnp.where(first, own, keys)]
     values_aug = [jnp.where(first, values, ones), jnp.where(first, ones, values)]
-
-    def body(step, carry):
-        rows = pl.ds(pl.multiple_of(step * block, block), block)
+    units = [(pl.ds(i * block, block), head) for i in range(q_ref.shape[0] // block) for head in range(2)]
+
+    def score(n):
+        rows, head = units[n]
         queries, miss = q_ref[rows, :] * BF(0.125), miss_ref[rows, :]
-        outs, logs = [], []
-        for head in range(2):
-            queries_aug = jnp.where(first, queries, miss) if head == 0 else jnp.where(first, miss, queries)
-            scores = dot_rows(queries_aug, keys_aug[head])
-            largest = jnp.max(scores, axis=1, keepdims=True)
-            weights = jnp.exp(scores - largest).astype(BF)
-            mixed = dot_plain(weights, values_aug[head])
-            total = mixed[:, 64:65] if head == 0 else mixed[:, 0:1]
-            outs.append(mixed / total)
-            logs.append(largest + jnp.log(total))
-        out_ref[rows, :] = jnp.where(first, outs[0], outs[1]).astype(BF)
-        lse_ref[0, rows, :] = jnp.where(first, logs[0], logs[1])
-        return carry
-
-    lax.fori_loop(0, q_ref.shape[0] // block, body, 0)
+        queries_aug = jnp.where(first, queries, miss) if head == 0 else jnp.where(first, miss, queries)
+        scores_s[n % 2] = dot_rows(queries_aug, keys_aug[head])
+
+    def weigh(n):
+        scores = scores_s[n % 2]
+        largest = jnp.max(scores, axis=1, keepdims=True)
+        weights_s[n % 2] = jnp.exp(scores - largest).astype(BF)
+        largest_s[n % 2] = jnp.broadcast_to(largest, largest_s.shape[1:])
+
+    def mix(n):
+        rows, head = units[n]
+        mixed = dot_plain(weights_s[n % 2], values_aug[head])
+        total = mixed[:, 64:65] if head == 0 else mixed[:, 0:1]
+        out, log = mixed / total, largest_s[n % 2] + jnp.log(total)
+        if head == 0:
+            mixed_s[0] = out
+            mixed_s[1] = log
+        else:
+            out_ref[rows, :] = jnp.where(first, mixed_s[0], out).astype(BF)
+            lse_ref[0, rows, :] = jnp.where(first, mixed_s[1], log)
+
+    for turn in range(len(units) + 2):
+        if turn < len(units):
+            score(turn)
+        if turn >= 2:
+            mix(turn - 2)
+        if 1 <= turn <= len(units):
+            weigh(turn - 1)
 
 
 def attention_forward(projected, miss, own, block=256):
@@ -411,6 +427,10 @@
             jax.ShapeDtypeStruct((count, width // 3), BF),
             jax.ShapeDtypeStruct((pairs, count, 128), F32),
         ],
+        scratch_shapes=[
+            pltpu.VMEM((2, block, count), F32), pltpu.VMEM((2, block, count), BF), pltpu.VMEM((2, block, 128), F32),
+            pltpu.VMEM((2, block, 128), F32),
+        ],
         compiler_params=pltpu.CompilerParams(vmem_limit_bytes=VMEM_GRANT),
         cost_estimate=pl.CostEstimate(flops=24 * 10**9, bytes_accessed=8 * 2**20, transcendentals=12 * 2**20),
         name="attention_forward",
@@ -445,9 +465,23 @@
     return [bit for name in order for bit in parts[name]]
 
 
+def blended(orders, which):
+    if len(set(orders)) == 1:
+        return own_bits(orders[0])
+    last = len(orders) - 1
+    total = [0] * 4
+    for at, order in enumerate(orders):
+        if last == 1:
+            here = which if at else 1 - which
+        else:
+            here = ((2 - which) * (1 - which) // 2, which * (2 - which), which * (which - 1) // 2)[at]
+        total = [old + here * bit for old, bit in zip(total, own_bits(order))]
+    return total
+
+
 def scatter_part(out_ref, values, order, part, base=0):
     size = values.shape[0] // 8
-    top, *bits = own_bits(order)
+    top, *bits = order if isinstance(order, list) else own_bits(order)
     first = 8 * (part + top - 2 * part * top)
     for a in range(8):
         rows = pl.ds(pl.multiple_of((first + flipped(a, bits)) * size, 16), size)
@@ -619,7 +653,7 @@
     last_out, vec_ref = outs[10:16], outs[16]
     (
         n2_s, mid_s, acc_s, back_s, grad_s, hidden_s, hidden_grad_s, result_s, branch_s, att_grad_s,
-        d1_s, d2_s, do_s, bias_s, core1, core2, near1, near2, next1, next2, send_sems, recv_sems, load_sems, out_sems,
+        d1_s, d2_s, do_s, pre_s, down_s, bias_s, core1, core2, near1, near2, next1, next2, send_sems, recv_sems, load_sems, out_sems,
     ) = refs
     step = pl.program_id(0)
     core = lax.axis_index("dp") % 2
@@ -704,19 +738,17 @@
     def _():
         bias = bias_s[pl.ds(chunk_row, 1), :]
 
-        def body(i, total):
-            rows = pl.ds(pl.multiple_of(i * shard, shard), shard)
-            pre = dot_plain(n2_s[rows, :], w1_ref[...]) + bias
-            back = dot_rows(grad_s[rows, :], w2_ref[...])
-            hidden, slope = gelu_parts(pre)
-            hidden, hidden_grad = hidden.astype(BF), (back * slope).astype(BF)
-            hidden_s[rows, :] = hidden
+        pre_s[...] = dot_plain(n2_s[...], w1_ref[...]) + bias
+        down_s[...] = dot_rows(grad_s[...], w2_ref[...])
+        total = jnp.zeros((1, size), F32)
+        for rows in blocks:
+            hidden, slope = gelu_parts(pre_s[rows, :])
+            hidden_grad = (down_s[rows, :] * slope).astype(BF)
+            hidden_s[rows, :] = hidden.astype(BF)
             hidden_grad_s[rows, :] = hidden_grad
-            acc_s[rows, :] += dot_plain(hidden, w2_ref[...])
-            back_s[rows, :] += dot_rows(hidden_grad, w1_ref[...])
-            return total + total_rows(hidden_grad.astype(F32))
-
-        total = lax.fori_loop(0, 4, body, jnp.zeros((1, size), F32))
+            total = total + total_rows(hidden_grad.astype(F32))
+        acc_s[...] += dot_plain(hidden_s[...], w2_ref[...])
+        back_s[...] += dot_rows(hidden_grad_s[...], w1_ref[...])
         vec_ref[pl.ds(4 + chunk_row, 1), 0:size] = total
 
     @pl.when(last_step)
@@ -729,13 +761,13 @@
             wide = grad_s[rows, :].astype(F32)
             branch = (wide + norm_back(unit, inverse, back, row_of(gain_ref))).astype(BF)
             branch_s[rows, :] = branch
-            att_grad_s[rows, :] = dot_rows(branch, out_weight_ref[...]).astype(BF)
             parts = (back * unit, back, branch.astype(F32), wide)
             return tuple(old + total_rows(part) for old, part in zip(sums, parts))
 
         sums = lax.fori_loop(0, 4, body, (jnp.zeros((1, n2_s.shape[1]), F32),) * 4)
         for at, part in enumerate(sums):
             vec_ref[at + 10 : at + 11, :] = part
+        att_grad_s[...] = dot_rows(branch_s[...], out_weight_ref[...]).astype(BF)
         for copy in stores(0, 6):
             copy.start()
 
@@ -747,15 +779,14 @@
 
     @pl.when(step > 0)
     def _():
-        def body(part, carry):
-            wide, narrow = n2_s.shape[1] // 2, size // 2
-            left = n2_s[:, pl.ds(pl.multiple_of(part * wide, 128), wide)]
+        wide, narrow = n2_s.shape[1] // 2, size // 2
+        order = blended(ORDERS[1:6:2], (step - 1) // 2)
+        for part in range(2):
+            left = n2_s[:, part * wide : (part + 1) * wide]
             scatter_part(d1_s.at[step - 1], dot_tokens(left, hidden_grad_s[...]), LOW_FIRST, part)
-            left = hidden_s[:, pl.ds(pl.multiple_of(part * narrow, 128), narrow)]
-            scatter_part(d2_s.at[step - 1], dot_tokens(left, grad_s[...]), HIGH_FIRST, part)
-            return carry
-
-        lax.fori_loop(0, 2, body, 0)
+        for part in range(2):
+            left = hidden_s[:, part * narrow : (part + 1) * narrow]
+            scatter_part(d2_s.at[step - 1], dot_tokens(left, grad_s[...]), order, part)
 
     @pl.when(last_step)
     def _():
@@ -813,7 +844,7 @@
         + [vmem((count, features), BF)] * 3
         + [
             vmem((2 * UNITS, features, size), BF), vmem((2 * UNITS, size, features), BF), vmem((2, features, half), BF),
-            vmem((8, size), F32),
+            vmem((count, size), F32), vmem((count, size), F32), vmem((8, size), F32),
             vmem((2, features, size), BF), vmem((2, size, features), BF),
             vmem((2, features // 2, size), BF), vmem((2, size // 2, features), BF),
             vmem((2, features // 4, size), BF), vmem((2, size // 4, features), BF),
@@ -828,28 +859,32 @@
 
 
 ORDERS = (
-    LOW_FIRST, HIGH_FIRST, LOW_FIRST, HIGH_FIRST, LOW_FIRST, HIGH_FIRST, DEEP_FIRST, LOW_FIRST, LOW_FIRST, LOW_FIRST
+    LOW_FIRST, HIGH_FIRST, LOW_FIRST, HIGH_FIRST, LOW_FIRST, HIGH_FIRST, HIGH_FIRST, LOW_FIRST, DEEP_FIRST, HIGH_FIRST,
 )
 PLAN = {
-    (0, 0): [(4, 0), (5, 0), (6, 0), (0, 3), (1, 3), (2, 3), (3, 3)],
-    (0, 1): [(4, 1), (5, 1), (6, 1), (0, 4)],
-    (1, 0): [(1, 4)],
-    (1, 1): [(4, 2), (5, 2), (2, 4), (3, 4)],
-    (2, 0): [(7, 0)],
-    (2, 1): [(7, 1)],
-    (3, 1): [(6, 2), (0, 5)],
-    (4, 0): [(8, 0), (4, 3), (5, 3), (1, 5)],
-    (4, 1): [(8, 1), (7, 2), (6, 3), (2, 5), (3, 5), (0, 6)],
-    (5, 0): [(1, 6)],
-    (5, 1): [(8, 2), (7, 3), (4, 4), (5, 4), (6, 4), (2, 6)],
-    (6, 0): [(9, 0)],
+    (0, 0): [(0, 3)],
+    (1, 0): [(4, 0), (1, 3), (5, 0), (6, 0)],
+    (1, 1): [(0, 4)],
+    (2, 0): [(2, 3), (4, 1), (5, 1), (1, 4), (6, 1)],
+    (3, 1): [(3, 3)],
+    (4, 0): [(0, 5), (7, 0)],
+    (5, 0): [(7, 1), (2, 4), (1, 5)],
+    (5, 1): [(4, 2), (3, 4)],
+    (7, 0): [(2, 5)],
+    (7, 1): [(3, 5), (6, 2), (7, 2), (1, 6)],
+    (8, 0): [(8, 0), (0, 6)],
+    (9, 0): [(8, 1), (5, 2)],
+    (9, 1): [(6, 3), (4, 3), (3, 6)],
+    (11, 0): [(7, 3), (2, 6)],
+    (11, 1): [(5, 3)],
+    (12, 0): [(9, 0)],
     "tail": [
-        (9, 1), (7, 4), (4, 5), (3, 6), (1, 7), (8, 3), (0, 7), (6, 5), (5, 5), (7, 5), (8, 4), (2, 7),
-        (8, 5), (4, 6), (3, 7), (6, 6), (9, 2), (7, 6), (8, 6), (5, 6), (9, 3), (6, 7), (4, 7), (9, 4),
-        (5, 7), (7, 7), (9, 5), (9, 6), (8, 7), (9, 7),
+        (9, 1), (0, 7), (6, 4), (1, 7), (4, 4), (7, 4), (3, 7), (2, 7), (5, 4), (9, 2), (8, 2), (6, 5),
+        (7, 5), (4, 5), (8, 3), (5, 5), (9, 3), (6, 6), (8, 4), (9, 4), (8, 5), (5, 6), (7, 6), (9, 5),
+        (4, 6), (8, 6), (7, 7), (9, 6), (6, 7), (4, 7), (5, 7), (8, 7), (9, 7),
     ],
 }
-BLOCK_OUT_AT = 0
+BLOCK_OUT_AT = (0, 0)
 
 
 def three_parts(column):
@@ -859,7 +894,7 @@
     return high, middle, (rest - middle.astype(F32)).astype(BF)
 
 
-def pair_backward(refs, outs, dk_acc, dv_acc, pair, block):
+def pair_backward(refs, outs, dk_acc, dv_acc, pair, part, block):
     q_ref, k_ref, v_ref, att_ref, grad_ref, lse_ref, miss_ref, own_ref = refs
     lane = lax.broadcasted_iota(jnp.int32, (1, 128), 1)
     first = lane < 64
@@ -871,8 +906,12 @@
     keys_aug = [jnp.where(first, keys, own), jnp.where(first, own, keys)]
     values_aug = [jnp.where(first, values, unit_rows), jnp.where(first, unit_rows, values)]
     keys_only = [jnp.where(first, keys, BF(0)), jnp.where(first, BF(0), keys)]
-    dk_acc[...] = jnp.zeros_like(dk_acc)
-    dv_acc[...] = jnp.zeros_like(dv_acc)
+
+    @pl.when(part == 0)
+    def _():
+        dk_acc[...] = jnp.zeros_like(dk_acc)
+        dv_acc[...] = jnp.zeros_like(dv_acc)
+
     columns = pl.ds(pl.multiple_of(pair * 128, 128), 128)
 
     def spread(column):
@@ -902,9 +941,13 @@
         outs[0][rows, columns] = (dq * 0.125).astype(BF)
         return carry
 
-    lax.fori_loop(0, q_ref.shape[0] // block, body, 0)
-    outs[1][:, columns] = dk_acc[...].T.astype(BF)
-    outs[2][:, columns] = dv_acc[...].T.astype(BF)
+    steps = q_ref.shape[0] // block // 2
+    lax.fori_loop(part * steps, (part + 1) * steps, body, 0)
+
+    @pl.when(part == 1)
+    def _():
+        outs[1][:, columns] = dk_acc[...].T.astype(BF)
+        outs[2][:, columns] = dv_acc[...].T.astype(BF)
 
 
 def backward_kernel(*refs):
@@ -1006,35 +1049,39 @@
             load(n).start()
         pl.semaphore_wait(barrier, len(peers))
 
-    for at in range(7):
+    for at in range(13):
 
         @pl.when(step == at)
         def _():
+            if (at, 0) == BLOCK_OUT_AT:
+                for k in (1, 2, 3):
+                    block_copy(k).start()
             ticks(at, 0)
             if at == 2:
                 load(7).wait()
                 store().start()
 
-    @pl.when(step < 6)
+    turn = step // 2
+    pair = 2 * (turn // 2) + (core + 1 + turn % 2) % 2
+
+    @pl.when(step < 12)
     def _():
-        pair = 2 * (step // 2) + (core + 1 + step % 2) % 2
         pair_backward(
             (q_ref, k_ref, v_ref, att_ref, grad_ref, lse_ref, miss_ref, own_ref),
-            (dq_s, dk_s, dv_s), dk_acc, dv_acc, pair, 256,
+            (dq_s, dk_s, dv_s), dk_acc, dv_acc, pair, step % 2, 256,
         )
 
-    for at in range(6):
+    for at in range(1, 12, 2):
 
         @pl.when(step == at)
         def _():
-            ticks(at, 1)
-            if at == BLOCK_OUT_AT:
+            if (at, 1) == BLOCK_OUT_AT:
                 for k in (1, 2, 3):
                     block_copy(k).start()
-
-    @pl.when(step < 6)
+            ticks(at, 1)
+
+    @pl.when((step < 12) & (step % 2 == 1))
     def _():
-        pair = 2 * (step // 2) + (core + 1 + step % 2) % 2
         columns = pl.ds(pl.multiple_of(pair * 128, 128), 128)
         grads = jnp.concatenate([part[:, columns] for part in (dq_s, dk_s, dv_s)], axis=1)
         vec_out[2:3, columns] = total_rows(grads[:, :128].astype(F32))
@@ -1042,12 +1089,12 @@
 
         def body(part, carry):
             left = normed_ref[:, pl.ds(pl.multiple_of(part * (features // 2), 128), features // 2)]
-            scatter_part(qkv_s.at[step], dot_tokens(left, grads), ORDERS[7], part)
+            scatter_part(qkv_s.at[turn], dot_tokens(left, grads), blended(ORDERS[7:10], turn // 2), part)
             return carry
 
         lax.fori_loop(0, 2, body, 0)
 
-    @pl.when(step == 6)
+    @pl.when(step == 12)
     def _():
         def body(at, sums):
             k = 3 - at
@@ -1075,7 +1122,7 @@
         vec_s[0, 2:4, :] = vec_out[2:4, :]
         vec_stage(0)[0].start()
 
-    @pl.when(step == 7)
+    @pl.when(step == 13)
     def _():
         for index, (n, tick) in enumerate(PLAN["tail"]):
             if index in (3, 8, 13):
@@ -1106,7 +1153,7 @@
     shard = count // 4
 
     def pair(i):
-        at = jnp.minimum(i, 5)
+        at = jnp.minimum(i // 2, 5)
         return 2 * (at // 2) + (lax.axis_index("dp") % 2 + 1 + at % 2) % 2
 
     column = lambda base: pl.BlockSpec((count, 128), lambda i: (0, pair(i) + base))
@@ -1122,7 +1169,7 @@
         landing += [vmem((lands[2], columns), BF)] if n < 4 else [vmem((size, columns), BF) for size in [rows] + lands]
     return pl.pallas_call(
         backward_kernel,
-        grid=(8,),
+        grid=(14,),
         in_specs=[
             column(0), column(pairs), column(2 * pairs), column(0), column(0),
             pl.BlockSpec((1, count, 128), lambda i: (pair(i), 0, 0)),

time: 306 us -> 270 us (0.88)
  Pallas kernels: 295 us -> 259 us
    pallas_call x1, Pallas kernels: 159 us -> 140 us  [backward(): pl.pallas_call(backward_kernel, grid=(14,), in_specs=[column(0), column(p...]
    pallas_call x1, Pallas kernels: 31.1 us -> 19.4 us  [attention_forward(): pl.pallas_call(functools.partial(attention_forward_kernel, block), grid=(...]
    pallas_call x1, Pallas kernels: 63.1 us -> 57.8 us  [feed(): pl.pallas_call(feed_kernel, grid=(2 * UNITS + 1,), in_specs=[wide, wide]...]
  transfers between devices with their start and end apart: 3 -> 3, of which waited for: 0 -> 0; matrix products, arithmetic and copies ran while one was open for 0% -> 1% of each run, Pallas kernels for 10% -> 7%
where the time goes in v3:
time: 270 us; the launch traced here: 269 us
  Pallas kernels  259 us (96%)
  local copies, waits for them, and re-layouts  4.11 us (2%)
  starting transfers between devices  3.55 us (1%)
    pallas_call x1, Pallas kernels, backward(): pl.pallas_call(backward_kernel, grid=(14,), in_specs=[column(0), column(p...  140 us
    pallas_call x1, Pallas kernels, feed(): pl.pallas_call(feed_kernel, grid=(2 * UNITS + 1,), in_specs=[wide, wide]...  57.8 us
    pallas_call x1, Pallas kernels, enter(): pl.pallas_call(enter_kernel, in_specs=[ANY, ANY, vmem, vmem, ANY, vmem],...  25.2 us
    pallas_call x1, Pallas kernels, attention_forward(): pl.pallas_call(functools.partial(attention_forward_kernel, block), grid=(...  19.4 us
    pallas_call x1, Pallas kernels, assemble(): pl.pallas_call(assemble_kernel, grid=(STEPS,), in_specs=[spec(n) for n in...  17 us
  transfers between devices with their start and end apart: 3, of which 0 were waited for; matrix products, arithmetic and copies ran while one was open for 1% of the time, Pallas kernels for 7%

profile of v3, /device:TPU:0, one launch (start us, length us, event | category | flops | bytes accessed | tf_op | source)
XLA Modules:
  0.0 269.0 jit_solution(695744046039534720)
XLA Ops:
  0.6 0.0 copy-start
  0.7 25.2 %enter.1 = (bf16[1024,768]{1,0:T(8,128)(2,1)}, bf16[1024,768]{1,0:T(8,128)(2,1)}, bf16[1024,2304]{1,0:T(8,128)(2,1)}, bf16[256,768]{1,0:T(8,128)(2,1)}, bf16[256...) custom-call(bf16[4,1,256,768]{3,2,1,0:T(8,128)(2,1)} %tokens_ref.1, ...), custom_call_target="tpu_custom_call" | custom-call | flops 4000000000 | bytes 20971520 | tf_op jit(solution)/shard_map/enter/pallas_call | solution.py:355
  25.9 1.5 collective-permute-start
  27.4 1.5 collective-permute-start.1
  28.9 0.6 collective-permute-start.2
  29.4 0.0 copy-done
  29.5 0.2 reduce-window.7
  29.6 0.1 fusion.1
  29.8 1.0 select_convert_fusion
  30.9 19.4 %attention_forward.1 = (bf16[1024,768]{1,0:T(8,128)(2,1)}, f32[6,1024,128]{2,1,0:T(8,128)}) custom-call(bf16[1024,2304]{1,0:T(8,128)(2,1)} %get-tuple-element.75.q_ref.k_ref.v_ref.refs_0_.refs_1_.refs_2_, bf16[1024,2304]{1,0:T(8,128)(2,1)} %get-tuple-element.75.q_ref.k_ref.v_ref.refs_0_.refs_1_.refs_2_, ...), custom_call_target="tpu_custom_call" | custom-call | flops 24000000000 | bytes 8388608 | tf_op jit(solution)/shard_map/attention_forward/pallas_call | solution.py:421
  50.2 0.0 collective-permute-done.g1
  50.2 0.0 copy-start.4
  50.3 0.0 collective-permute-done.1.g2
  50.3 0.0 copy-start.5
  50.3 0.0 collective-permute-done.2.g3
  50.3 0.0 copy-start.6
  50.3 0.7 copy-done.4
  51.0 0.1 copy-done.5
  51.1 0.1 copy-done.6
  51.2 57.8 %feed.1 = (bf16[256,768]{1,0:T(8,128)(2,1)}, bf16[256,768]{1,0:T(8,128)(2,1)}, bf16[256,768]{1,0:T(8,128)(2,1)}, bf16[256,768]{1,0:T(8,128)(2,1)}, bf16[1024,768...) custom-call(bf16[1024,768]{1,0:T(8,128)(2,1)} %get-tuple-element.77., ...), custom_call_target="tpu_custom_call" | custom-call | flops 35000000512 | bytes 41943040 | tf_op jit(solution)/shard_map/feed/pallas_call | solution.py:828
  109.1 139.7 %backward.1 = (bf16[4,1,256,768]{3,2,1,0:T(8,128)(2,1)}, bf16[4,1,256,768]{3,2,1,0:T(8,128)(2,1)}, f32[16,768]{1,0:T(8,128)}, bf16[768,512]{1,0:T(8,128)(2,1)}, ...) custom-call(bf16[1024,2304]{1,0:T(8,128)(2,1)} %get-tuple-element.75, ...), custom_call_target="tpu_custom_call" | custom-call | flops 60000002048 | bytes 62914560 | tf_op jit(solution)/shard_map/backward/pallas_call | solution.py:1170
  248.8 0.0 copy-start.3
  248.8 17.0 %assemble.1 = (f32[768,3072]{1,0:T(8,128)}, f32[3,2,512,768]{3,2,1,0:T(8,128)}, f32[768,768]{1,0:T(8,128)}, f32[768,2304]{1,0:T(8,128)}, f32[768]{0:T(1024)}, /*...) custom-call(bf16[768,512]{1,0:T(8,128)(2,1)} %get-tuple-element.103., ...), custom_call_target="tpu_custom_call" | custom-call | bytes 47185920 | tf_op jit(solution)/shard_map/assemble/pallas_call | solution.py:1261
  265.8 0.0 copy-done.3
  265.8 0.0 copy-start.2
  265.8 0.0 copy-start.1
  265.9 1.1 copy.31
  267.0 0.8 copy-done.2
  267.8 1.1 copy.32
  268.9 0.0 copy-done.1
  (8 shorter events, 0.1 us)
Async XLA Ops:
  0.6 28.8 %copy-start = (s32[4,1,5]{2,1,0:T(1,128)S(1)}, s32[4,1,5]{2,1,0:T(1,128)}, u32[]{:S(2)}) copy-start(s32[4,1,5]{2,1,0:T(1,128)} %param.16) | copy-start | bytes 244
  25.9 24.4 %collective-permute-start = (bf16[256,768]{1,0:T(8,128)(2,1)}, bf16[256,768]{1,0:T(8,128)(2,1)S(1)}, u32[]{:S(2)}, u32[]{:S(2)}) collective-permute-start(bf16[256,768]{1,0:T(8,128)(2,1)} %get-tuple-element.79), channel_id=1, source_target_pairs={{0,1},{1,0},{2,3},{3,2},{4,5},{5,4},{6,7},{7,6},{8,9},{9,8},{10,11... | collective-permute-start | bytes 1179656 | tf_op jit(solution)/shard_map/ppermute | solution.py:1286
  27.4 22.9 %collective-permute-start.1 = (bf16[256,768]{1,0:T(8,128)(2,1)}, bf16[256,768]{1,0:T(8,128)(2,1)S(1)}, u32[]{:S(2)}, u32[]{:S(2)}) collective-permute-start(bf16[256,768]{1,0:T(8,128)(2,1)} %get-tuple-element.80), channel_id=1, source_target_pairs={{0,2},{1,3},{2,0},{3,1},{4,6},{5,7},{6,4},{7,5},{8,10},{9,11},{10,... | collective-permute-start | bytes 1179656 | tf_op jit(solution)/shard_map/ppermute | solution.py:1286
  28.9 21.4 %collective-permute-start.2 = (bf16[256,768]{1,0:T(8,128)(2,1)}, bf16[256,768]{1,0:T(8,128)(2,1)S(1)}, u32[]{:S(2)}, u32[]{:S(2)}) collective-permute-start(bf16[256,768]{1,0:T(8,128)(2,1)} %get-tuple-element.81), channel_id=1, source_target_pairs={{0,3},{1,2},{2,1},{3,0},{4,7},{5,6},{6,5},{7,4},{8,11},{9,10},{10,... | collective-permute-start | bytes 1179656 | tf_op jit(solution)/shard_map/ppermute | solution.py:1286
  50.2 0.7 copy-start.4
  50.3 0.9 copy-start.5
  50.3 1.0 copy-start.6
  248.8 17.0 %copy-start.3 = (bf16[4,1,256,768]{3,2,1,0:T(8,128)(2,1)S(1)}, bf16[4,1,256,768]{3,2,1,0:T(8,128)(2,1)}, u32[]{:S(2)}) copy-start(bf16[4,1,256,768]{3,2,1,0:T(8,128)(2,1)} %get-tuple-element.156) | copy-start | bytes 4718596
  265.8 2.0 copy-start.2
  265.8 3.1 %copy-start.1 = (s32[4,1,5]{2,1,0:T(1,128)S(1)}, s32[4,1,5]{2,1,0:T(1,128)}, u32[]{:S(2)}) copy-start(s32[4,1,5]{2,1,0:T(1,128)} %param.16) | copy-start | bytes 244

commit v4 on v3

--- a/solution.py
+++ b/solution.py
@@ -262,9 +262,9 @@
 
 
 def enter_kernel(
-    tokens_ref, cot_ref, gain_ref, shift_ref, weight_ref, bias_ref,
-    row_out, normed_out, projected_out, cot0, cot1, cot2, cot3,
-    landed, weight_s, normed_s, projected_s, cot_s, send_sem, recv_sem, load_sem, cot_sem, out_sem,
+    tokens_ref, gain_ref, shift_ref, weight_ref, bias_ref,
+    row_out, normed_out, projected_out,
+    landed, weight_s, normed_s, projected_s, send_sem, recv_sem, load_sem, out_sem,
 ):
     me, depth = lax.axis_index("seq"), lax.axis_index("dp")
     high, low = me // 2, me % 2
@@ -289,12 +289,6 @@
     copies = [remote(k - 1, k, 0, shard) for k in (1, 2, 3)]
     for copy in copies[:2]:
         copy.start()
-    loads = [pltpu.make_async_copy(cot_ref.at[peers[k], 0], cot_s.at[k], cot_sem.at[k]) for k in range(4)]
-    stores = [
-        pltpu.make_async_copy(cot_s.at[k], out, cot_sem.at[k]) for k, out in enumerate((cot0, cot1, cot2, cot3))
-    ]
-    for copy in loads:
-        copy.start()
     bias = row_of(bias_ref)
     bias = jnp.concatenate([bias[:, :features], jnp.zeros((1, features), F32), bias[:, features:]], axis=1)
 
@@ -315,9 +309,6 @@
 
         @pl.when(k == 1)
         def _():
-            for load, store in zip(loads, stores):
-                load.wait()
-                store.start()
             for copy in copies[:2]:
                 copy.wait_send()
             copies[2].start()
@@ -338,15 +329,13 @@
         return carry
 
     lax.fori_loop(0, 4, body, 0)
-    for copy in stores:
-        copy.wait()
     for k in range(4):
         for copy in outs(k):
             copy.wait()
     copies[2].wait_send()
 
 
-def enter(tokens, cotangent, gain, shift, weight, bias):
+def enter(tokens, gain, shift, weight, bias):
     _, _, shard, features = tokens.shape
     count, wide = 4 * shard, weight.shape[1]
     shape = jax.ShapeDtypeStruct
@@ -354,24 +343,60 @@
     dma = pltpu.SemaphoreType.DMA
     return pl.pallas_call(
         enter_kernel,
-        in_specs=[ANY, ANY, vmem, vmem, ANY, vmem],
-        out_specs=[ANY] * 7,
-        out_shape=[shape((count, features), BF), shape((count, features), BF), shape((count, wide), BF)]
-        + [shape((shard, features), BF)] * 4,
+        in_specs=[ANY, vmem, vmem, ANY, vmem],
+        out_specs=[ANY] * 3,
+        out_shape=[shape((count, features), BF), shape((count, features), BF), shape((count, wide), BF)],
         scratch_shapes=[
             pltpu.VMEM((4, shard, features), BF), pltpu.VMEM(weight.shape, BF), pltpu.VMEM((count, features), BF),
-            pltpu.VMEM((count, wide), BF), pltpu.VMEM((4, shard, features), BF),
-            dma((3,)), dma((3,)), dma((2,)), dma((4,)), dma((12,)),
+            pltpu.VMEM((count, wide), BF),
+            dma((3,)), dma((3,)), dma((2,)), dma((12,)),
         ],
         compiler_params=pltpu.CompilerParams(collective_id=0, has_side_effects=True, vmem_limit_bytes=VMEM_GRANT),
         cost_estimate=pl.CostEstimate(flops=4 * 10**9, bytes_accessed=20 * 2**20, transcendentals=0),
         name="enter",
-    )(tokens, cotangent, gain, shift, weight, bias)
+    )(tokens, gain, shift, weight, bias)
 
 
 def attention_forward_kernel(
-    block, q_ref, k_ref, v_ref, miss_ref, own_ref, out_ref, lse_ref, scores_s, weights_s, mixed_s, largest_s
+    block, q_ref, k_ref, v_ref, miss_ref, own_ref, cot_ref, out_ref, lse_ref, grad_out,
+    scores_s, weights_s, mixed_s, largest_s, piece_s, send_sem, recv_sem, own_sem,
 ):
+    step = pl.program_id(0)
+    me = lax.axis_index("seq")
+    peers = peer_ids()
+    kinds = [("low", 1), ("high", 1), ("both", 1)]
+    shard = piece_s.shape[0]
+
+    def exchange():
+        return [
+            pltpu.make_async_remote_copy(
+                src_ref=cot_ref.at[peers[name][1], 0], dst_ref=grad_out.at[pl.ds((k + 1) * shard, shard)],
+                send_sem=send_sem.at[k], recv_sem=recv_sem.at[k], device_id=peers[name], device_id_type=MESH,
+            )
+            for k, name in enumerate(kinds)
+        ]
+
+    def load():
+        return pltpu.make_async_copy(cot_ref.at[me, 0], piece_s, own_sem)
+
+    def store():
+        return pltpu.make_async_copy(piece_s, grad_out.at[pl.ds(0, shard)], own_sem)
+
+    @pl.when(step == 0)
+    def _():
+        barrier = pltpu.get_barrier_semaphore()
+        for name in kinds:
+            pl.semaphore_signal(barrier, inc=1, device_id=peers[name], device_id_type=MESH)
+        load().start()
+        pl.semaphore_wait(barrier, 3)
+        for copy in exchange():
+            copy.start()
+
+    @pl.when(step == 1)
+    def _():
+        load().wait()
+        store().start()
+
     lane = lax.broadcasted_iota(jnp.int32, (1, 128), 1)
     first = lane < 64
     keys, values, own = k_ref[...], v_ref[...], own_ref[...]
@@ -412,8 +437,14 @@
         if 1 <= turn <= len(units):
             weigh(turn - 1)
 
-
-def attention_forward(projected, miss, own, block=256):
+    @pl.when(step == pl.num_programs(0) - 1)
+    def _():
+        store().wait()
+        for copy in exchange():
+            copy.wait()
+
+
+def attention_forward(projected, miss, own, cotangent, block=256):
     count, width = projected.shape
     pairs = width // 384
     column = lambda base: pl.BlockSpec((count, 128), lambda i: (0, i + base))
@@ -421,20 +452,22 @@
     return pl.pallas_call(
         functools.partial(attention_forward_kernel, block),
         grid=(pairs,),
-        in_specs=[column(0), column(pairs), column(2 * pairs), full, full],
-        out_specs=[column(0), pl.BlockSpec((1, count, 128), lambda i: (i, 0, 0))],
+        in_specs=[column(0), column(pairs), column(2 * pairs), full, full, ANY],
+        out_specs=[column(0), pl.BlockSpec((1, count, 128), lambda i: (i, 0, 0)), ANY],
         out_shape=[
             jax.ShapeDtypeStruct((count, width // 3), BF),
             jax.ShapeDtypeStruct((pairs, count, 128), F32),
+            jax.ShapeDtypeStruct((count, width // 3), BF),
         ],
         scratch_shapes=[
             pltpu.VMEM((2, block, count), F32), pltpu.VMEM((2, block, count), BF), pltpu.VMEM((2, block, 128), F32),
-            pltpu.VMEM((2, block, 128), F32),
+            pltpu.VMEM((2, block, 128), F32), pltpu.VMEM((count // 4, width // 3), BF), pltpu.SemaphoreType.DMA((3,)),
+            pltpu.SemaphoreType.DMA((3,)), pltpu.SemaphoreType.DMA,
         ],
-        compiler_params=pltpu.CompilerParams(vmem_limit_bytes=VMEM_GRANT),
+        compiler_params=pltpu.CompilerParams(collective_id=3, has_side_effects=True, vmem_limit_bytes=VMEM_GRANT),
         cost_estimate=pl.CostEstimate(flops=24 * 10**9, bytes_accessed=8 * 2**20, transcendentals=12 * 2**20),
         name="attention_forward",
-    )(projected, projected, projected, miss, own)
+    )(projected, projected, projected, miss, own, cotangent)
 
 
 def three_parts(column):
@@ -599,6 +632,8 @@
 
     def tick(self, at, resumed=False):
         if at == 0 or resumed:
+            if at == 4:
+                self.local().start()
             self.start(at)
         elif at <= 3:
             self.arrived(at - 1)
@@ -638,14 +673,15 @@
 FEED_PLAN = {
     (3, 0): [(0, 0)],
     (3, 1): [(0, 1)],
-    (5, 0): [(1, 0)],
-    (5, 1): [(1, 1), (0, 2)],
-    (6, 1): [(1, 2)],
+    (5, 0): [(1, 0), (0, 2)],
+    (5, 1): [(1, 1)],
+    (6, 0): [(0, 3)],
+    (6, 2): [(1, 2)],
 }
 
 
 def feed_kernel(
-    row_ref, att_ref, g0, g1, g2, g3, out_weight_ref, out_bias_ref, gain_ref, shift_ref, fc2_bias_ref,
+    row_ref, att_ref, cot_ref, out_weight_ref, out_bias_ref, gain_ref, shift_ref, fc2_bias_ref,
     w1_ref, bias_ref, w2_ref, *refs
 ):
     outs, refs = refs[:17], refs[17:]
@@ -653,7 +689,7 @@
     last_out, vec_ref = outs[10:16], outs[16]
     (
         n2_s, mid_s, acc_s, back_s, grad_s, hidden_s, hidden_grad_s, result_s, branch_s, att_grad_s,
-        d1_s, d2_s, do_s, pre_s, down_s, bias_s, core1, core2, near1, near2, next1, next2, send_sems, recv_sems, load_sems, out_sems,
+        d1_s, d2_s, do_s, pre_s, down_s, bias_s, core1, core2, near1, near2, next1, next2, last1, last2, send_sems, recv_sems, load_sem, out_sems,
     ) = refs
     step = pl.program_id(0)
     core = lax.axis_index("dp") % 2
@@ -669,7 +705,7 @@
         d, bufs = (d1_s, (core1, near1, next1)) if which == 0 else (d2_s, (core2, near2, next2))
         return Sum(
             (LOW_FIRST, HIGH_FIRST)[which], d.shape[1], d.at[2 * unit], d.at[2 * unit + 1], bufs[0].at[unit],
-            [bufs[1].at[unit], bufs[2].at[unit], None], None, None, send_sems.at[slot], recv_sems.at[slot], None,
+            [bufs[1].at[unit], bufs[2].at[unit], (last1, last2)[which]], None, None, send_sems.at[slot], recv_sems.at[slot], None,
         )
 
     def ticks(at, place):
@@ -677,8 +713,8 @@
             for which in range(2):
                 job(unit, which).tick(tick)
 
-    def load(k):
-        return pltpu.make_async_copy((g0, g1, g2, g3)[k], grad_s.at[blocks[k]], load_sems.at[k])
+    def load():
+        return pltpu.make_async_copy(cot_ref, grad_s, load_sem)
 
     def stores(first, last_store):
         pairs = [(result_s.at[rows], out) for rows, out in zip(blocks, results)]
@@ -689,17 +725,17 @@
         pairs += [(do_s.at[0], last_out[4]), (do_s.at[1], last_out[5])]
         for unit in range(2):
             for which, d in enumerate((d1_s, d2_s)):
-                rows = pl.ds(0, d.shape[1] // 4)
+                rows = pl.ds(0, d.shape[1] // (4 if unit else 16))
                 pairs.append((d.at[2 * unit + 1, rows], sums_out[2 * unit + which]))
         return [pltpu.make_async_copy(src, dst, out_sems.at[n]) for n, (src, dst) in enumerate(pairs) if first <= n < last_store]
 
     @pl.when(step == 0)
     def _():
         barrier = pltpu.get_barrier_semaphore()
-        for name in ("core", "low", "high"):
-            pl.semaphore_signal(barrier, inc=1, device_id=peers[name, 1], device_id_type=MESH)
-        for k in range(4):
-            load(k).start()
+        for name, peer in peers.items():
+            if name != ("both", 1):
+                pl.semaphore_signal(barrier, inc=1, device_id=peer, device_id_type=MESH)
+        load().start()
         vec_ref[...] = jnp.zeros_like(vec_ref)
         for at in range(2 * UNITS):
             bias_s[at : at + 1, :] = bias_ref[at * size : (at + 1) * size].reshape(1, -1)
@@ -715,12 +751,11 @@
 
         lax.fori_loop(0, 4, project, 0)
         back_s[...] = jnp.zeros_like(back_s)
-        for k in range(4):
-            load(k).wait()
+        load().wait()
 
     @pl.when(step == 2)
     def _():
-        pl.semaphore_wait(pltpu.get_barrier_semaphore(), 3)
+        pl.semaphore_wait(pltpu.get_barrier_semaphore(), 6)
 
     for at in range(1, 2 * UNITS + 1):
         unit, keeping = (at - 1) // 2, (at - 1) % 2
@@ -790,6 +825,8 @@
 
     @pl.when(last_step)
     def _():
+        ticks(2 * UNITS, 2)
+
         def body(at, carry):
             slot, part = at // 2, at % 2
             wide = att_ref.shape[1] // 2
@@ -803,17 +840,17 @@
             copy.start()
         for unit in range(2):
             for which in range(2):
-                job(unit, which).settle(2)
+                job(unit, which).settle(2 if unit else 3)
         for copy in stores(12, 16):
             copy.start()
         for copy in stores(0, 16):
             copy.wait()
         for unit in range(2):
             for which in range(2):
-                job(unit, which).left(0, 3)
-
-
-def feed(row, attended, grads, out_weight, out_bias, gain, shift, fc1_weight, fc1_bias, fc2_weight, fc2_bias):
+                job(unit, which).left(0, 3 if unit else 4)
+
+
+def feed(row, attended, cotangent, out_weight, out_bias, gain, shift, fc1_weight, fc1_bias, fc2_weight, fc2_bias):
     count, features = row.shape
     size = fc1_weight.shape[1] // (2 * UNITS)
     half = features // 2
@@ -828,15 +865,15 @@
     return pl.pallas_call(
         feed_kernel,
         grid=(2 * UNITS + 1,),
-        in_specs=[wide, wide] + [ANY] * 4 + [once(out_weight.shape), line, line, line, line]
+        in_specs=[wide, wide, ANY] + [once(out_weight.shape), line, line, line, line]
         + [
             pl.BlockSpec((features, size), lambda i: (0, chunk(i))),
             once(fc1_bias.shape),
             pl.BlockSpec((size, features), lambda i: (chunk(i), 0)),
         ],
         out_specs=[ANY] * 16 + [once((16, features))],
-        out_shape=[shape(grads[0].shape, BF)] * 4 + [shape((count, features), BF)] * 2
-        + [shape((features // 4, size), BF), shape((size // 4, features), BF)] * 2
+        out_shape=[shape((count // 4, features), BF)] * 4 + [shape((count, features), BF)] * 2
+        + [shape((rows // part, columns), BF) for part in (16, 4) for rows, columns in ((features, size), (size, features))]
         + [shape((features, size), BF)] * 2 + [shape((size, features), BF)] * 2
         + [shape((features, half), BF)] * 2 + [shape((16, features), F32)],
         scratch_shapes=[vmem((count, features), BF)] + [vmem((count, features), F32)] * 3
@@ -848,40 +885,42 @@
             vmem((2, features, size), BF), vmem((2, size, features), BF),
             vmem((2, features // 2, size), BF), vmem((2, size // 2, features), BF),
             vmem((2, features // 4, size), BF), vmem((2, size // 4, features), BF),
-            dma((4, SEMS)), dma((4, SEMS)), dma((4,)), dma((16,)),
+            vmem((3 * features // 16, size), BF), vmem((3 * size // 16, features), BF),
+            dma((4, SEMS)), dma((4, SEMS)), dma, dma((16,)),
         ],
         compiler_params=pltpu.CompilerParams(collective_id=2, has_side_effects=True, vmem_limit_bytes=VMEM_GRANT),
         cost_estimate=pl.CostEstimate(flops=35 * 10**9, bytes_accessed=40 * 2**20, transcendentals=0),
         name="feed",
     )(
-        row, attended, *grads, out_weight, out_bias, gain, shift, fc2_bias, fc1_weight, fc1_bias, fc2_weight,
+        row, attended, cotangent, out_weight, out_bias, gain, shift, fc2_bias, fc1_weight, fc1_bias, fc2_weight,
     )
 
 
 ORDERS = (
-    LOW_FIRST, HIGH_FIRST, LOW_FIRST, HIGH_FIRST, LOW_FIRST, HIGH_FIRST, HIGH_FIRST, LOW_FIRST, DEEP_FIRST, HIGH_FIRST,
+    LOW_FIRST, HIGH_FIRST, LOW_FIRST, HIGH_FIRST, LOW_FIRST, HIGH_FIRST, HIGH_FIRST, LOW_FIRST, HIGH_FIRST, LOW_FIRST,
 )
+FIRST_TICK = (4, 4, 3, 3, 0, 0, 0, 0, 0, 0)
 PLAN = {
-    (0, 0): [(0, 3)],
-    (1, 0): [(4, 0), (1, 3), (5, 0), (6, 0)],
-    (1, 1): [(0, 4)],
-    (2, 0): [(2, 3), (4, 1), (5, 1), (1, 4), (6, 1)],
-    (3, 1): [(3, 3)],
-    (4, 0): [(0, 5), (7, 0)],
-    (5, 0): [(7, 1), (2, 4), (1, 5)],
-    (5, 1): [(4, 2), (3, 4)],
-    (7, 0): [(2, 5)],
-    (7, 1): [(3, 5), (6, 2), (7, 2), (1, 6)],
-    (8, 0): [(8, 0), (0, 6)],
-    (9, 0): [(8, 1), (5, 2)],
-    (9, 1): [(6, 3), (4, 3), (3, 6)],
-    (11, 0): [(7, 3), (2, 6)],
-    (11, 1): [(5, 3)],
-    (12, 0): [(9, 0)],
+    (0, 0): [(4, 0), (0, 4)],
+    (1, 0): [(4, 1)],
+    (1, 1): [(5, 0), (3, 3), (0, 5)],
+    (2, 0): [(1, 4), (6, 0)],
+    (3, 0): [(5, 1), (6, 1)],
+    (3, 1): [(1, 5), (2, 3), (3, 4)],
+    (4, 0): [(7, 0)],
+    (5, 0): [(7, 1), (4, 2), (0, 6)],
+    (5, 1): [(2, 4), (3, 5)],
+    (7, 1): [(1, 6), (2, 5)],
+    (8, 0): [(8, 0)],
+    (9, 0): [(6, 2), (8, 1), (4, 3)],
+    (9, 1): [(5, 2), (3, 6)],
+    (11, 0): [(7, 2), (4, 4)],
+    (11, 1): [(6, 3), (2, 6), (0, 7)],
+    (12, 0): [(5, 3), (9, 0)],
     "tail": [
-        (9, 1), (0, 7), (6, 4), (1, 7), (4, 4), (7, 4), (3, 7), (2, 7), (5, 4), (9, 2), (8, 2), (6, 5),
-        (7, 5), (4, 5), (8, 3), (5, 5), (9, 3), (6, 6), (8, 4), (9, 4), (8, 5), (5, 6), (7, 6), (9, 5),
-        (4, 6), (8, 6), (7, 7), (9, 6), (6, 7), (4, 7), (5, 7), (8, 7), (9, 7),
+        (6, 4), (9, 1), (4, 5), (5, 4), (2, 7), (7, 3), (8, 2), (1, 7), (6, 5), (9, 2), (7, 4), (5, 5),
+        (4, 6), (3, 7), (8, 3), (9, 3), (6, 6), (7, 5), (8, 4), (5, 6), (9, 4), (7, 6), (4, 7), (8, 5),
+        (9, 5), (6, 7), (8, 6), (7, 7), (9, 6), (5, 7), (8, 7), (9, 7),
     ],
 }
 BLOCK_OUT_AT = (0, 0)
@@ -956,14 +995,15 @@
         weight_ref, row_ref, branch_ref, gain_ref, vec_in_ref,
     ) = refs[:14]
     results, sums_in, last_in = refs[14:18], refs[18:22], refs[22:28]
-    block_out, tokens_out, vec_out = refs[28:31]
-    owns, others = refs[31:41], refs[41:51]
+    block_out, vec_out = refs[28:30]
+    token_outs = refs[30:34]
+    owns, others = refs[34:44], refs[44:54]
     (
         dq_s, dk_s, dv_s, dk_acc, dv_acc, qkv_s, own_result, grad_s, vec_s, vec_got,
         send_sems, recv_sems, local_sems, load_sems, side_send, side_recv, vec_send, vec_recv,
-    ) = refs[51:69]
-    held = refs[69:76]
-    landing = refs[76:]
+    ) = refs[54:72]
+    held = refs[72:79]
+    landing = refs[79:]
     step = pl.program_id(0)
     me, depth = lax.axis_index("seq"), lax.axis_index("dp")
     core = depth % 2
@@ -974,12 +1014,11 @@
     def job(n):
         sems = send_sems.at[n], recv_sems.at[n], local_sems.at[n]
         if n < 4:
-            return Sum(
-                ORDERS[n], 4 * held[n].shape[0], None, held[n], None, [None, None, landing[n]], owns[n], others[n], *sems
-            )
+            bufs = [None, None, landing[n - 2] if n > 1 else None]
+            return Sum(ORDERS[n], owns[n].shape[0], None, held[n], None, bufs, owns[n], others[n], *sems)
         send = last_in[2 * (n - 4)] if n < 7 else qkv_s.at[2 * (n - 7)]
         keep = held[n] if n < 7 else qkv_s.at[2 * (n - 7) + 1]
-        core_buf, *bufs = landing[4 * (n - 3) : 4 * (n - 2)]
+        core_buf, *bufs = landing[4 * n - 14 : 4 * n - 10]
         return Sum(ORDERS[n], keep.shape[0], send, keep, core_buf, bufs, owns[n], others[n], *sems)
 
     def load(n):
@@ -991,22 +1030,16 @@
     def store():
         return pltpu.make_async_copy(own_result, block_out.at[me, 0], load_sems.at[7])
 
-    def token_store():
-        return pltpu.make_async_copy(grad_s.at[0], tokens_out.at[me, 0], load_sems.at[8])
+    def token_store(k):
+        return pltpu.make_async_copy(grad_s.at[k], token_outs[k], load_sems.at[8 + k])
 
     kinds = [("low", 1), ("high", 1), ("both", 1)]
 
-    def spread_row(number, k, piece, out):
+    def block_copy(k):
         return pltpu.make_async_remote_copy(
-            src_ref=piece, dst_ref=out.at[me, 0], send_sem=side_send.at[number, k - 1],
-            recv_sem=side_recv.at[number, k - 1], device_id=peers[kinds[k - 1]], device_id_type=MESH,
+            src_ref=results[k], dst_ref=block_out.at[me, 0], send_sem=side_send.at[k - 1],
+            recv_sem=side_recv.at[k - 1], device_id=peers[kinds[k - 1]], device_id_type=MESH,
         )
-
-    def block_copy(k):
-        return spread_row(0, k, results[k], block_out)
-
-    def token_copy(k):
-        return spread_row(1, k, grad_s.at[k], tokens_out)
 
     vec_names = [[("core", 1)], kinds, [("deep", 1), ("deep", 2), ("deep", 3)]]
 
@@ -1035,7 +1068,7 @@
 
     def ticks(at, place):
         for n, tick in PLAN.get((at, place), []):
-            resumed = n < 4 and tick == 3
+            resumed = tick == FIRST_TICK[n] > 0
             if resumed or (4 <= n < 7 and tick == 1):
                 load(n).wait()
             job(n).tick(tick, resumed)
@@ -1108,10 +1141,7 @@
 
                 @pl.when(k == piece)
                 def _():
-                    if piece:
-                        token_copy(piece).start()
-                    else:
-                        token_store().start()
+                    token_store(piece).start()
 
             return tuple(old + total_rows(part) for old, part in zip(sums, (back * unit, back)))
 
@@ -1131,12 +1161,12 @@
         for n in range(10):
             job(n).arrived(7)
         for n in range(10):
-            job(n).left(3 if n < 4 else 0, 8)
+            job(n).left(FIRST_TICK[n], 8)
         store().wait()
-        token_store().wait()
+        for k in range(4):
+            token_store(k).wait()
         for k in (1, 2, 3):
             block_copy(k).wait()
-            token_copy(k).wait()
         for stage in range(3):
             for copy in vec_stage(stage):
                 copy.wait_send()
@@ -1166,7 +1196,7 @@
     landing = []
     for n, (rows, columns) in enumerate(sizes):
         lands = landing_rows(ORDERS[n], rows)
-        landing += [vmem((lands[2], columns), BF)] if n < 4 else [vmem((size, columns), BF) for size in [rows] + lands]
+        landing += [vmem((size, columns), BF) for size in ([rows] + lands)[FIRST_TICK[n] :]]
     return pl.pallas_call(
         backward_kernel,
         grid=(14,),
@@ -1176,8 +1206,8 @@
             full, full, wide, once(qkv_weight.shape), wide, wide, once((features,)), once((16, features)),
         ]
         + [ANY] * 14,
-        out_specs=[ANY, ANY, once((16, features))] + [ANY] * 20,
-        out_shape=[shape((4, 1, shard, features), BF)] * 2 + [shape((16, features), F32)]
+        out_specs=[ANY, once((16, features))] + [ANY] * 24,
+        out_shape=[shape((4, 1, shard, features), BF), shape((16, features), F32)] + [shape((shard, features), BF)] * 4
         + [shape(size, BF) for size in sizes] * 2,
         scratch_shapes=[vmem((count, features), BF)] * 3
         + [vmem((128, count), F32)] * 2
@@ -1185,7 +1215,7 @@
         + [
             vmem((shard, features), BF), vmem((4, shard, features), BF),
             vmem((3, 16, features), F32), vmem((3, 3, 16, features), F32),
-            dma((10, SEMS)), dma((10, SEMS)), dma((10,)), dma((9,)), dma((2, 3)), dma((2, 3)), dma((3, 3)), dma((3, 3)),
+            dma((10, SEMS)), dma((10, SEMS)), dma((10,)), dma((12,)), dma((3,)), dma((3,)), dma((3, 3)), dma((3, 3)),
         ]
         + held + landing,
         compiler_params=pltpu.CompilerParams(collective_id=1, has_side_effects=True, vmem_limit_bytes=VMEM_GRANT),
@@ -1281,6 +1311,29 @@
     return d1, d2.reshape(wide, features), out, qkv, vecs
 
 
+def place_row_kernel(p0, p1, p2, p3, out_ref):
+    which = pl.program_id(0) ^ lax.axis_index("seq")
+    for k, piece in enumerate((p0, p1, p2, p3)):
+
+        @pl.when(which == k)
+        def _():
+            out_ref[0, 0] = piece[...]
+
+
+def place_row(pieces):
+    shard, features = pieces[0].shape
+    return pl.pallas_call(
+        place_row_kernel,
+        grid=(4,),
+        in_specs=[once((shard, features))] * 4,
+        out_specs=pl.BlockSpec((1, 1, shard, features), lambda i: (i, 0, 0, 0)),
+        out_shape=jax.ShapeDtypeStruct((4, 1, shard, features), BF),
+        compiler_params=pltpu.CompilerParams(vmem_limit_bytes=VMEM_GRANT),
+        cost_estimate=pl.CostEstimate(flops=0, bytes_accessed=3 * 2**20, transcendentals=0),
+        name="place_row",
+    )(*pieces)
+
+
 def swap(array, axis, bit):
     count = lax.axis_size(axis)
     return lax.ppermute(array, axis, [(i, i ^ bit) for i in range(count)])
@@ -1296,22 +1349,23 @@
     images = image_lengths.shape[2] - 1
     me = lax.axis_index("seq")
 
-    row, normed, projected, *cots = enter(tokens, cotangent, attn_gain, attn_shift, qkv_weight, qv_bias)
+    row, normed, projected = enter(tokens, attn_gain, attn_shift, qkv_weight, qv_bias)
     seg_row = segment_ids(lax.dynamic_index_in_dim(image_lengths, me, 0, keepdims=False), row_len, images)
     seg_row = seg_row.reshape(parties, shard_len)
     segment = jnp.concatenate([seg_row[me ^ k] for k in range(parties)], axis=0)
     miss, own = segment_features(segment)
-    attended, logs = attention_forward(projected, miss, own)
-    grads = [cots[0]] + [swap(cots[k], "seq", k) for k in (1, 2, 3)]
+    attended, logs, grads = attention_forward(projected, miss, own, cotangent)
     fed = feed(
         row, attended, grads, out_weight, out_bias, mlp_gain, mlp_shift, fc1_weight, fc1_bias, fc2_weight, fc2_bias
     )
     results, (branch, attended_grad), sums, last, vec = fed[:4], fed[4:6], fed[6:10], fed[10:16], fed[16]
-    block_out, tokens_grad, vector, *summed = backward(
+    block_out, vector, *rest = backward(
         projected, attended, attended_grad, logs, miss, own, normed, qkv_weight, row, branch, attn_gain, vec,
         results, sums, last,
     )
+    pieces, summed = rest[:4], rest[4:]
     paired = [part for n in range(10) for part in (summed[n], summed[10 + n])]
+    tokens_grad = place_row([pieces[0]] + [swap(pieces[k], "seq", k) for k in (1, 2, 3)])
     fc1_grad, fc2_grad, out_grad, qkv_grad, vecs = assemble(paired, vector)
     gain, shift, out_sum, mlp_gain_sum, mlp_shift_sum, fc2_sum, qv_sum, fc1_sum = vecs
     return (

time: 270 us -> 262 us (0.970)
  Pallas kernels: 259 us -> 253 us
    pallas_call x1, Pallas kernels: 140 us -> 126 us  [backward(): pl.pallas_call(backward_kernel, grid=(14,), in_specs=[column(0), column(p...]
    pallas_call x2 -> x3, Pallas kernels: 83.1 us -> 87 us  [the longest x1 58.7 us: feed(): pl.pallas_call(feed_kernel, grid=(2 * UNITS + 1,), in_specs=[wide, wide,...]
    pallas_call x1, Pallas kernels: 19.4 us -> 22.1 us  [attention_forward(): pl.pallas_call(functools.partial(attention_forward_kernel, block), grid=(...]
  transfers between devices with their start and end apart: 3 -> 3, of which waited for: 0 -> 1; matrix products, arithmetic and copies ran while one was open for 1% -> 0% of each run, Pallas kernels for 7% -> 6%
where the time goes in v4:
time: 262 us; the launch traced here: 261 us
  Pallas kernels  253 us (97%)
  starting transfers between devices  3.55 us (1%)
    pallas_call x1, Pallas kernels, backward(): pl.pallas_call(backward_kernel, grid=(14,), in_specs=[column(0), column(p...  126 us
    pallas_call x1, Pallas kernels, feed(): pl.pallas_call(feed_kernel, grid=(2 * UNITS + 1,), in_specs=[wide, wide,...  58.7 us
    pallas_call x1, Pallas kernels, enter(): pl.pallas_call(enter_kernel, in_specs=[ANY, vmem, vmem, ANY, vmem], out_s...  25.2 us
    pallas_call x1, Pallas kernels, attention_forward(): pl.pallas_call(functools.partial(attention_forward_kernel, block), grid=(...  22.1 us
    pallas_call x1, Pallas kernels, assemble(): pl.pallas_call(assemble_kernel, grid=(STEPS,), in_specs=[spec(n) for n in...  16.9 us
  transfers between devices with their start and end apart: 3, of which 1 were waited for; matrix products, arithmetic and copies ran while one was open for 0% of the time, Pallas kernels for 6%

profile of v4, /device:TPU:0, one launch (start us, length us, event | category | flops | bytes accessed | tf_op | source)
XLA Modules:
  0.0 261.1 jit_solution(15473820883707326506)
XLA Ops:
  0.6 0.0 copy-start
  0.7 0.6 copy-done
  1.3 0.2 reduce-window.7
  1.5 0.1 fusion.1
  1.7 1.0 select_convert_fusion
  2.8 25.2 %enter.1 = (bf16[1024,768]{1,0:T(8,128)(2,1)}, bf16[1024,768]{1,0:T(8,128)(2,1)}, bf16[1024,2304]{1,0:T(8,128)(2,1)}) custom-call(bf16[4,1,256,768]{3,2,1,0:T(8,128)(2,1)} %tokens_ref.1, f32[768]{0:T(1024)} %refs_12_.1, f32[768]{0:T(1024)} %shift_ref.2, bf16[768,2304]{1,0:T(8,128)(2,1)} %refs_9_.1, f32[1536]{0:T(1024)} %bias_ref.2), custom_call_target="tpu_custom_call" | custom-call | flops 4000000000 | bytes 20971520 | tf_op jit(solution)/shard_map/enter/pallas_call | solution.py:344
  27.9 22.1 %attention_forward.1 = (bf16[1024,768]{1,0:T(8,128)(2,1)}, f32[6,1024,128]{2,1,0:T(8,128)}, bf16[1024,768]{1,0:T(8,128)(2,1)}) custom-call(bf16[1024,2304]{1,0:T(8,128)(2,1)} %get-tuple-element.75.q_ref.k_ref.v_ref.refs_0_.refs_1_.refs_2_, bf16[1024,2304]{1,0:T(8,128)(2,1)} %get-tuple-element.75.q_ref.k_ref.v_ref.refs_0_.refs_1_.refs_2_, ...), custom_call_target="tpu_custom_call" | custom-call | flops 24000000000 | bytes 8388608 | tf_op jit(solution)/shard_map/attention_forward/pallas_call | solution.py:452
  50.1 58.7 %feed.1 = (bf16[256,768]{1,0:T(8,128)(2,1)}, bf16[256,768]{1,0:T(8,128)(2,1)}, bf16[256,768]{1,0:T(8,128)(2,1)}, bf16[256,768]{1,0:T(8,128)(2,1)}, bf16[1024,768...) custom-call(bf16[1024,768]{1,0:T(8,128)(2,1)} %get-tuple-element.77., ...), custom_call_target="tpu_custom_call" | custom-call | flops 35000000512 | bytes 41943040 | tf_op jit(solution)/shard_map/feed/pallas_call | solution.py:865
  108.8 126.4 %backward.1 = (bf16[4,1,256,768]{3,2,1,0:T(8,128)(2,1)}, f32[16,768]{1,0:T(8,128)}, bf16[256,768]{1,0:T(8,128)(2,1)}, bf16[256,768]{1,0:T(8,128)(2,1)}, bf16[256...) custom-call(bf16[1024,2304]{1,0:T(8,128)(2,1)} %get-tuple-element.75, ...), custom_call_target="tpu_custom_call" | custom-call | flops 60000002048 | bytes 62914560 | tf_op jit(solution)/shard_map/backward/pallas_call | solution.py:1200
  235.3 0.8 collective-permute-start
  236.1 1.0 collective-permute-start.1
  237.1 1.7 collective-permute-start.2
  238.8 16.9 %assemble.1 = (f32[768,3072]{1,0:T(8,128)}, f32[3,2,512,768]{3,2,1,0:T(8,128)}, f32[768,768]{1,0:T(8,128)}, f32[768,2304]{1,0:T(8,128)}, f32[768]{0:T(1024)}, /*...) custom-call(bf16[768,512]{1,0:T(8,128)(2,1)} %get-tuple-element.103., ...), custom_call_target="tpu_custom_call" | custom-call | bytes 47185920 | tf_op jit(solution)/shard_map/assemble/pallas_call | solution.py:1291
  255.7 0.0 collective-permute-done.p1
  255.8 0.0 copy-start.3
  255.8 0.0 collective-permute-done.1.p2
  255.8 0.0 copy-start.4
  255.8 0.2 collective-permute-done.2.p3
  256.0 0.0 copy-start.5
  256.0 0.5 copy-done.3
  256.5 0.1 copy-done.4
  256.6 0.1 copy-done.5
  256.8 0.0 copy-start.2
  256.8 3.2 %place_row.1 = bf16[4,1,256,768]{3,2,1,0:T(8,128)(2,1)} custom-call(bf16[256,768]{1,0:T(8,128)(2,1)} %get-tuple-element.99.p0, bf16[256,768]{1,0:T(8,128)(2,1)} %copy-done.3, bf16[256,768]{1,0:T(8,128)(2,1)} %copy-done.4, bf16[256,768]{1,0:T(8,128)(2,1)} %copy-done.5), custom_call_target="tpu_custom_call" | custom-call | bytes 3145728 | tf_op jit(solution)/shard_map/place_row/pallas_call | solution.py:1325
  259.9 0.0 copy-start.1
  259.9 0.0 copy-done.2
  259.9 1.1 copy.30
  261.1 0.0 copy-done.1
  (8 shorter events, 0.1 us)
Async XLA Ops:
  0.6 0.7 copy-start
  235.3 20.5 %collective-permute-start = (bf16[256,768]{1,0:T(8,128)(2,1)}, bf16[256,768]{1,0:T(8,128)(2,1)S(1)}, u32[]{:S(2)}, u32[]{:S(2)}) collective-permute-start(bf16[256,768]{1,0:T(8,128)(2,1)} %get-tuple-element.100), channel_id=1, source_target_pairs={{0,1},{1,0},{2,3},{3,2},{4,5},{5,4},{6,7},{7,6},{8,9},{9,8},{10,11... | collective-permute-start | bytes 1179656 | tf_op jit(solution)/shard_map/ppermute | solution.py:1339
  236.1 19.7 %collective-permute-start.1 = (bf16[256,768]{1,0:T(8,128)(2,1)}, bf16[256,768]{1,0:T(8,128)(2,1)S(1)}, u32[]{:S(2)}, u32[]{:S(2)}) collective-permute-start(bf16[256,768]{1,0:T(8,128)(2,1)} %get-tuple-element.101), channel_id=1, source_target_pairs={{0,2},{1,3},{2,0},{3,1},{4,6},{5,7},{6,4},{7,5},{8,10},{9,11},{10,... | collective-permute-start | bytes 1179656 | tf_op jit(solution)/shard_map/ppermute | solution.py:1339
  237.1 18.9 %collective-permute-start.2 = (bf16[256,768]{1,0:T(8,128)(2,1)}, bf16[256,768]{1,0:T(8,128)(2,1)S(1)}, u32[]{:S(2)}, u32[]{:S(2)}) collective-permute-start(bf16[256,768]{1,0:T(8,128)(2,1)} %get-tuple-element.102), channel_id=1, source_target_pairs={{0,3},{1,2},{2,1},{3,0},{4,7},{5,6},{6,5},{7,4},{8,11},{9,10},{10,... | collective-permute-start | bytes 1179656 | tf_op jit(solution)/shard_map/ppermute | solution.py:1339
  255.8 0.7 copy-start.3
  255.8 0.9 copy-start.4
  256.0 0.8 copy-start.5
  256.8 3.2 %copy-start.2 = (bf16[4,1,256,768]{3,2,1,0:T(8,128)(2,1)S(1)}, bf16[4,1,256,768]{3,2,1,0:T(8,128)(2,1)}, u32[]{:S(2)}) copy-start(bf16[4,1,256,768]{3,2,1,0:T(8,128)(2,1)} %get-tuple-element.156) | copy-start | bytes 4718596
  259.9 1.1 copy-start.1

commit v5 on v4

--- a/solution.py
+++ b/solution.py
@@ -512,11 +512,14 @@
     return total
 
 
-def scatter_part(out_ref, values, order, part, base=0):
-    size = values.shape[0] // 8
-    top, *bits = order if isinstance(order, list) else own_bits(order)
-    first = 8 * (part + top - 2 * part * top)
-    for a in range(8):
+def scatter_groups(out_ref, values, order, part=None, base=0):
+    bits = order if isinstance(order, list) else own_bits(order)
+    groups, first = 16, 0
+    if part is not None:
+        top, *bits = bits
+        groups, first = 8, 8 * (part + top - 2 * part * top)
+    size = values.shape[0] // groups
+    for a in range(groups):
         rows = pl.ds(pl.multiple_of((first + flipped(a, bits)) * size, 16), size)
         out_ref[rows, base : base + values.shape[1]] = values[a * size : (a + 1) * size].astype(out_ref.dtype)
 
@@ -814,28 +817,17 @@
 
     @pl.when(step > 0)
     def _():
-        wide, narrow = n2_s.shape[1] // 2, size // 2
         order = blended(ORDERS[1:6:2], (step - 1) // 2)
-        for part in range(2):
-            left = n2_s[:, part * wide : (part + 1) * wide]
-            scatter_part(d1_s.at[step - 1], dot_tokens(left, hidden_grad_s[...]), LOW_FIRST, part)
-        for part in range(2):
-            left = hidden_s[:, part * narrow : (part + 1) * narrow]
-            scatter_part(d2_s.at[step - 1], dot_tokens(left, grad_s[...]), order, part)
+        scatter_groups(d1_s.at[step - 1], dot_tokens(n2_s[...], hidden_grad_s[...]), LOW_FIRST)
+        scatter_groups(d2_s.at[step - 1], dot_tokens(hidden_s[...], grad_s[...]), order)
 
     @pl.when(last_step)
     def _():
         ticks(2 * UNITS, 2)
 
-        def body(at, carry):
-            slot, part = at // 2, at % 2
-            wide = att_ref.shape[1] // 2
+        for slot in range(2):
             columns = pl.ds(pl.multiple_of(((core + 1 + slot) % 2) * half, 128), half)
-            left = att_ref[:, pl.ds(pl.multiple_of(part * wide, 128), wide)]
-            scatter_part(do_s.at[slot], dot_tokens(left, branch_s[:, columns]), ORDERS[6], part)
-            return carry
-
-        lax.fori_loop(0, 4, body, 0)
+            scatter_groups(do_s.at[slot], dot_tokens(att_ref[...], branch_s[:, columns]), ORDERS[6])
         for copy in stores(6, 12):
             copy.start()
         for unit in range(2):
@@ -1122,7 +1114,7 @@
 
         def body(part, carry):
             left = normed_ref[:, pl.ds(pl.multiple_of(part * (features // 2), 128), features // 2)]
-            scatter_part(qkv_s.at[turn], dot_tokens(left, grads), blended(ORDERS[7:10], turn // 2), part)
+            scatter_groups(qkv_s.at[turn], dot_tokens(left, grads), blended(ORDERS[7:10], turn // 2), part)
             return carry
 
         lax.fori_loop(0, 2, body, 0)
@@ -1311,22 +1303,27 @@
     return d1, d2.reshape(wide, features), out, qkv, vecs
 
 
-def place_row_kernel(p0, p1, p2, p3, out_ref):
-    which = pl.program_id(0) ^ lax.axis_index("seq")
-    for k, piece in enumerate((p0, p1, p2, p3)):
-
-        @pl.when(which == k)
-        def _():
-            out_ref[0, 0] = piece[...]
+def place_row_kernel(p0, p1, p2, p3, out_ref, held, sems):
+    me = lax.axis_index("seq")
+    pieces = (p0, p1, p2, p3)
+    loads = [pltpu.make_async_copy(piece, held.at[k], sems.at[k]) for k, piece in enumerate(pieces)]
+    stores = [pltpu.make_async_copy(held.at[k], out_ref.at[me ^ k, 0], sems.at[k + 4]) for k in range(4)]
+    for copy in loads:
+        copy.start()
+    for load, store in zip(loads, stores):
+        load.wait()
+        store.start()
+    for copy in stores:
+        copy.wait()
 
 
 def place_row(pieces):
     shard, features = pieces[0].shape
     return pl.pallas_call(
         place_row_kernel,
-        grid=(4,),
-        in_specs=[once((shard, features))] * 4,
-        out_specs=pl.BlockSpec((1, 1, shard, features), lambda i: (i, 0, 0, 0)),
+        in_specs=[ANY] * 4,
+        out_specs=ANY,
+        scratch_shapes=[pltpu.VMEM((4, shard, features), BF), pltpu.SemaphoreType.DMA((8,))],
         out_shape=jax.ShapeDtypeStruct((4, 1, shard, features), BF),
         compiler_params=pltpu.CompilerParams(vmem_limit_bytes=VMEM_GRANT),
         cost_estimate=pl.CostEstimate(flops=0, bytes_accessed=3 * 2**20, transcendentals=0),

time: 262 us -> 261 us (level)
  no operation moved by 1% of the time
where the time goes in v5:
time: 261 us
  Pallas kernels  252 us (97%)
  starting transfers between devices  3.55 us (1%)
  local copies, waits for them, and re-layouts  2.7 us (1%)
    pallas_call x1, Pallas kernels, backward(): pl.pallas_call(backward_kernel, grid=(14,), in_specs=[column(0), column(p...  127 us
    pallas_call x1, Pallas kernels, feed(): pl.pallas_call(feed_kernel, grid=(2 * UNITS + 1,), in_specs=[wide, wide,...  58.8 us
    pallas_call x1, Pallas kernels, enter(): pl.pallas_call(enter_kernel, in_specs=[ANY, vmem, vmem, ANY, vmem], out_s...  25.2 us
    pallas_call x1, Pallas kernels, attention_forward(): pl.pallas_call(functools.partial(attention_forward_kernel, block), grid=(...  22.1 us
    pallas_call x1, Pallas kernels, assemble(): pl.pallas_call(assemble_kernel, grid=(STEPS,), in_specs=[spec(n) for n in...  16.9 us
  transfers between devices with their start and end apart: 3, of which 1 were waited for; matrix products, arithmetic and copies ran while one was open for 0% of the time, Pallas kernels for 6%

profile of v5, /device:TPU:0, one launch (start us, length us, event | category | flops | bytes accessed | tf_op | source)
XLA Modules:
  0.0 260.5 jit_solution(12538077838040549854)
XLA Ops:
  0.6 0.0 copy-start
  0.7 0.6 copy-done
  1.3 0.2 reduce-window.7
  1.5 0.1 fusion.1
  1.7 1.0 select_convert_fusion
  2.8 25.2 %enter.1 = (bf16[1024,768]{1,0:T(8,128)(2,1)}, bf16[1024,768]{1,0:T(8,128)(2,1)}, bf16[1024,2304]{1,0:T(8,128)(2,1)}) custom-call(bf16[4,1,256,768]{3,2,1,0:T(8,128)(2,1)} %tokens_ref.1, f32[768]{0:T(1024)} %refs_12_.1, f32[768]{0:T(1024)} %shift_ref.2, bf16[768,2304]{1,0:T(8,128)(2,1)} %refs_9_.1, f32[1536]{0:T(1024)} %bias_ref.2), custom_call_target="tpu_custom_call" | custom-call | flops 4000000000 | bytes 20971520 | tf_op jit(solution)/shard_map/enter/pallas_call | solution.py:344
  27.9 22.1 %attention_forward.1 = (bf16[1024,768]{1,0:T(8,128)(2,1)}, f32[6,1024,128]{2,1,0:T(8,128)}, bf16[1024,768]{1,0:T(8,128)(2,1)}) custom-call(bf16[1024,2304]{1,0:T(8,128)(2,1)} %get-tuple-element.75.q_ref.k_ref.v_ref.refs_0_.refs_1_.refs_2_, bf16[1024,2304]{1,0:T(8,128)(2,1)} %get-tuple-element.75.q_ref.k_ref.v_ref.refs_0_.refs_1_.refs_2_, ...), custom_call_target="tpu_custom_call" | custom-call | flops 24000000000 | bytes 8388608 | tf_op jit(solution)/shard_map/attention_forward/pallas_call | solution.py:452
  50.1 58.8 %feed.1 = (bf16[256,768]{1,0:T(8,128)(2,1)}, bf16[256,768]{1,0:T(8,128)(2,1)}, bf16[256,768]{1,0:T(8,128)(2,1)}, bf16[256,768]{1,0:T(8,128)(2,1)}, bf16[1024,768...) custom-call(bf16[1024,768]{1,0:T(8,128)(2,1)} %get-tuple-element.77., ...), custom_call_target="tpu_custom_call" | custom-call | flops 35000000512 | bytes 41943040 | tf_op jit(solution)/shard_map/feed/pallas_call | solution.py:857
  108.9 126.6 %backward.1 = (bf16[4,1,256,768]{3,2,1,0:T(8,128)(2,1)}, f32[16,768]{1,0:T(8,128)}, bf16[256,768]{1,0:T(8,128)(2,1)}, bf16[256,768]{1,0:T(8,128)(2,1)}, bf16[256...) custom-call(bf16[1024,2304]{1,0:T(8,128)(2,1)} %get-tuple-element.75, ...), custom_call_target="tpu_custom_call" | custom-call | flops 60000002048 | bytes 62914560 | tf_op jit(solution)/shard_map/backward/pallas_call | solution.py:1192
  235.5 0.8 collective-permute-start
  236.2 0.9 collective-permute-start.1
  237.2 1.9 collective-permute-start.2
  239.0 16.9 %assemble.1 = (f32[768,3072]{1,0:T(8,128)}, f32[3,2,512,768]{3,2,1,0:T(8,128)}, f32[768,768]{1,0:T(8,128)}, f32[768,2304]{1,0:T(8,128)}, f32[768]{0:T(1024)}, /*...) custom-call(bf16[768,512]{1,0:T(8,128)(2,1)} %get-tuple-element.103., ...), custom_call_target="tpu_custom_call" | custom-call | bytes 47185920 | tf_op jit(solution)/shard_map/assemble/pallas_call | solution.py:1283
  256.0 0.0 collective-permute-done.p1
  256.0 0.0 copy-start.3
  256.0 0.2 collective-permute-done.1.p2
  256.2 0.0 copy-start.4
  256.2 0.0 collective-permute-done.2.p3
  256.2 0.0 copy-start.5
  256.2 0.6 copy-done.3
  256.7 0.2 copy-done.4
  256.9 0.1 copy-done.5
  257.0 0.0 copy-start.2
  257.0 2.3 place_row.1
  259.4 0.0 copy-start.1
  259.4 0.0 copy-done.2
  259.4 1.1 copy.30
  260.5 0.0 copy-done.1
  (8 shorter events, 0.1 us)
Async XLA Ops:
  0.6 0.7 copy-start
  235.5 20.5 %collective-permute-start = (bf16[256,768]{1,0:T(8,128)(2,1)}, bf16[256,768]{1,0:T(8,128)(2,1)S(1)}, u32[]{:S(2)}, u32[]{:S(2)}) collective-permute-start(bf16[256,768]{1,0:T(8,128)(2,1)} %get-tuple-element.100), channel_id=1, source_target_pairs={{0,1},{1,0},{2,3},{3,2},{4,5},{5,4},{6,7},{7,6},{8,9},{9,8},{10,11... | collective-permute-start | bytes 1179656 | tf_op jit(solution)/shard_map/ppermute | solution.py:1336
  236.2 19.9 %collective-permute-start.1 = (bf16[256,768]{1,0:T(8,128)(2,1)}, bf16[256,768]{1,0:T(8,128)(2,1)S(1)}, u32[]{:S(2)}, u32[]{:S(2)}) collective-permute-start(bf16[256,768]{1,0:T(8,128)(2,1)} %get-tuple-element.101), channel_id=1, source_target_pairs={{0,2},{1,3},{2,0},{3,1},{4,6},{5,7},{6,4},{7,5},{8,10},{9,11},{10,... | collective-permute-start | bytes 1179656 | tf_op jit(solution)/shard_map/ppermute | solution.py:1336
  237.2 19.0 %collective-permute-start.2 = (bf16[256,768]{1,0:T(8,128)(2,1)}, bf16[256,768]{1,0:T(8,128)(2,1)S(1)}, u32[]{:S(2)}, u32[]{:S(2)}) collective-permute-start(bf16[256,768]{1,0:T(8,128)(2,1)} %get-tuple-element.102), channel_id=1, source_target_pairs={{0,3},{1,2},{2,1},{3,0},{4,7},{5,6},{6,5},{7,4},{8,11},{9,10},{10,... | collective-permute-start | bytes 1179656 | tf_op jit(solution)/shard_map/ppermute | solution.py:1336
  256.0 0.7 copy-start.3
  256.2 0.7 copy-start.4
  256.2 0.9 copy-start.5
  257.0 2.3 copy-start.2
  259.4 1.2 copy-start.1
